TPU v7x, 512 devices: a whole 4x4x16 slice. The times are simulated.
512 devices in a mesh: depth: 64 (over z, y_lo, core), row: 8 (over y_hi, x).
Axes of the slice: x: 4, y: 4 (y_hi: 2, y_lo: 2; y = y_hi * 2 + y_lo), z: 16, core: 2. Of those that a mesh axis runs over, the one named last changes fastest.
Arguments:
- data: float32 [2, 192, 512, 512], P(None, 'depth', 'row'), may hold values from -0.25 to 0.25
- wavenumbers: float32 [512], replicated, may hold values from 0.3 to 3
- eps_rows: int32 [512], P('row'), may hold values from 1 to 2, as said below
- eps_cols: int32 [512], replicated, may hold values from 1 to 2, as said below
Outputs:
- prediction: float32 [2, 512, 512], P(None, 'row', 'depth')
Inputs may be any that keep to these rules, and one draw needn't show every extreme that they name: `eps_rows`: each entry is a separation between 1 and 2; the value 2 occurs. `eps_cols`: each entry is a separation between 1 and 2; the value 2 occurs.
All inputs are finite; a program needn't handle non-finite values.
Results may differ from a plain program's by a relative error of at most 0.0003.
Values sent between devices are 32-bit elements; how exact they have to be, the bound alone decides.
No kernel may reach another device: no remote copies, remote signals or barrier semaphores. Data moves between devices by JAX's collectives and lax.ppermute only.
A program may use at most 64 MiB of HBM per device.

v0:
```python
import jax
import jax.numpy as jnp
from jax import lax
from jax.sharding import PartitionSpec as P

EPS_MOST = 2


def carried_in(part, axis, combine, identity):
    count = lax.axis_size(axis)
    place = lax.axis_index(axis)
    ahead = count - 1 - place
    gathered = lax.all_gather(part, axis)
    state = jnp.zeros_like(part) + jnp.asarray(identity, part.dtype)

    def one(lap, state):
        source = count - 1 - lap
        return combine(state, lax.dynamic_index_in_dim(gathered, source, 0, False))

    return lax.fori_loop(0, ahead, one, state)


def shifted_2(value, axis, by):
    peers = lax.axis_size(axis)
    pairs = [(i, i + by) for i in range(peers) if 0 <= i + by < peers]
    return lax.ppermute(value, axis, pairs)


def rotated(stacked, cosine, sine):
    real_part = stacked[0] * cosine - stacked[1] * sine
    imag_part = stacked[0] * sine + stacked[1] * cosine
    return jnp.stack([real_part, imag_part])


def complex_product(first, second, form):
    high = lax.Precision.HIGHEST
    real_part = jnp.einsum(form, first[0], second[0], precision=high) - jnp.einsum(
        form, first[1], second[1], precision=high
    )
    imag_part = jnp.einsum(form, first[0], second[1], precision=high) + jnp.einsum(
        form, first[1], second[0], precision=high
    )
    return jnp.stack([real_part, imag_part])


def add_arrays(earlier, later):
    return earlier + later


def body(data, wavenumbers, eps_rows, eps_cols):
    slab_count = data.shape[1]
    row_count = data.shape[2]
    total_depth = slab_count * lax.axis_size("depth")
    first_slab = lax.axis_index("depth") * slab_count
    row_start = lax.axis_index("row") * row_count
    row_waves = lax.dynamic_slice_in_dim(wavenumbers, row_start, row_count)
    local_sum = row_waves[:, None] + wavenumbers[None, :]
    levels = (first_slab + jnp.arange(slab_count)).astype(jnp.float32) + 0.5
    phase = local_sum[None, :, :] * levels[:, None, None]
    cosine = jnp.cos(phase)
    sine = jnp.sin(phase)
    downward = rotated(data, cosine, sine)
    totals = jnp.sum(downward, axis=1)
    tail_carry = carried_in(totals, "depth", add_arrays, jnp.zeros_like(totals))
    suffix = jnp.flip(jnp.cumsum(jnp.flip(downward, 1), 1), 1) + tail_carry[:, None]
    rim_slabs = shifted_2(suffix, "depth", -1)
    extended = jnp.concatenate([suffix, rim_slabs], 1)
    left_factor = jnp.zeros_like(suffix)
    right_factor = jnp.zeros_like(suffix)
    for offset in range(1, EPS_MOST + 1):
        shifted = extended[:, offset + 1 : offset + 1 + slab_count]
        row_mask = (eps_rows == offset)[None, None, :, None]
        col_mask = (eps_cols == offset)[None, None, None, :]
        left_factor = jnp.where(row_mask, shifted, left_factor)
        right_factor = jnp.where(col_mask, shifted, right_factor)
    right_whole = lax.all_gather(right_factor, "row", axis=2, tiled=True)
    upward = rotated(data, cosine, -sine)
    middle = complex_product(upward, right_whole, "zrk,zkc->zrc")
    middle_whole = lax.all_gather(middle, "row", axis=2, tiled=True)
    depth_term = complex_product(left_factor, middle_whole, "zrk,zkc->rc")
    depth_term = depth_term * (4.0 / total_depth)
    return lax.psum_scatter(depth_term, "depth", scatter_dimension=2, tiled=True)


def solution(mesh):
    in_specs = (P(None, "depth", "row", None), P(), P("row"), P())
    out_specs = P(None, "row", "depth")
    return jax.shard_map(body, mesh=mesh, in_specs=in_specs, out_specs=out_specs, check_vma=False)
```

profile of v0, /device:TPU:1, one launch (start us, length us, event | category | flops | bytes accessed | tf_op | source)
XLA Modules:
  0.0 908.4 jit_solution(5063147253867985097)
XLA Ops:
  8.1 2.7 fusion.28
  12.8 144.9 %all-gather.9.cloned.1.call-done = f32[128,64,512]{2,1,0:T(8,128)} async-done(((f32[2,64,512]{2,1,0:T(8,128)}), f32[128,64,512]{2,1,0:T(8,128)}) %all-gather.9.cloned.1.call-update) | async-done | bytes 16777232 | tf_op jit(solution)/shard_map/all_gather | solution.py:13
  157.7 65.0 %while.12 = (s32[]{:T(128)}, f32[2,64,512]{2,1,0:T(8,128)S(1)}, s32[]{:T(128)}, f32[64,2,64,512]{3,2,1,0:T(8,128)}, s32[]{:T(128)}, /*index=5*/s32[]{:T(128)}, s32[]{:T(128)}, s32[]{:T(128)}) while((s32[]{:T(128)}, f32[2,64,512]{2,1,0:T(8,128)S(1)}, s32[]{:T(128)}, f32[64,2,64,512]{3,2,1,0:T(8,128)}, s32[]{:T(128)}, /*index=5*/s32[]{:T(128)}, ...), condition=%wide.region_3.4_spmd, body=%wide.region_2.3_spmd.sunk | while | flops 65542 | bytes 786575 | solution.py:20
  157.8 1.0 bitcast_add_fusion.2
  158.8 1.0 bitcast_add_fusion.2
  159.8 1.0 bitcast_add_fusion.2
  160.9 1.0 bitcast_add_fusion.2
  161.9 1.0 bitcast_add_fusion.2
  163.0 1.0 bitcast_add_fusion.2
  164.0 1.0 bitcast_add_fusion.2
  165.1 1.0 bitcast_add_fusion.2
  166.1 1.0 bitcast_add_fusion.2
  167.2 1.0 bitcast_add_fusion.2
  168.2 1.0 bitcast_add_fusion.2
  169.3 1.0 bitcast_add_fusion.2
  170.3 1.0 bitcast_add_fusion.2
  171.4 1.0 bitcast_add_fusion.2
  172.4 1.0 bitcast_add_fusion.2
  173.5 1.0 bitcast_add_fusion.2
  174.5 1.0 bitcast_add_fusion.2
  175.6 1.0 bitcast_add_fusion.2
  176.6 1.0 bitcast_add_fusion.2
  177.7 1.0 bitcast_add_fusion.2
  178.7 1.0 bitcast_add_fusion.2
  179.8 1.0 bitcast_add_fusion.2
  180.8 1.0 bitcast_add_fusion.2
  181.9 1.0 bitcast_add_fusion.2
  182.9 1.0 bitcast_add_fusion.2
  183.9 1.0 bitcast_add_fusion.2
  185.0 1.0 bitcast_add_fusion.2
  186.0 1.0 bitcast_add_fusion.2
  187.1 1.0 bitcast_add_fusion.2
  188.1 1.0 bitcast_add_fusion.2
  189.2 1.0 bitcast_add_fusion.2
  190.2 1.0 bitcast_add_fusion.2
  191.3 1.0 bitcast_add_fusion.2
  192.3 1.0 bitcast_add_fusion.2
  193.4 1.0 bitcast_add_fusion.2
  194.4 1.0 bitcast_add_fusion.2
  195.5 1.0 bitcast_add_fusion.2
  196.5 1.0 bitcast_add_fusion.2
  197.6 1.0 bitcast_add_fusion.2
  198.6 1.0 bitcast_add_fusion.2
  199.7 1.0 bitcast_add_fusion.2
  200.7 1.0 bitcast_add_fusion.2
  201.8 1.0 bitcast_add_fusion.2
  202.8 1.0 bitcast_add_fusion.2
  213.3 1.0 bitcast_add_fusion.2
  217.5 1.0 bitcast_add_fusion.2
  221.7 1.0 bitcast_add_fusion.2
  222.8 3.2 collective-permute-start
  226.1 10.0 %collective-permute-done = f32[2,3,64,512]{3,2,1,0:T(8,128)S(1)} collective-permute-done((f32[2,3,64,512]{3,2,1,0:T(8,128)S(1)}, f32[2,3,64,512]{3,2,1,0:T(8,128)S(1)}, u32[]{:S(2)}, u32[]{:S(2)}) %collective-permute-start) | collective-permute-done | bytes 786464 | tf_op jit(solution)/shard_map/ppermute | solution.py:26
  237.2 94.8 %all-gather.5.cloned.1.call-done = f32[2,3,512,512]{3,2,1,0:T(8,128)} async-done(((f32[2,3,64,512]{3,2,1,0:T(8,128)}), f32[2,3,512,512]{3,2,1,0:T(8,128)}) %all-gather.5.cloned.1.call-update) | async-done | bytes 6291472 | tf_op jit(solution)/shard_map/all_gather | solution.py:76
  332.0 5.1 fusion
  337.2 5.0 fusion.3
  342.2 3.4 fusion.9
  345.6 3.4 fusion.11
  350.2 102.9 %all-gather.7.cloned.1.call-done = f32[2,3,512,512]{3,2,1,0:T(8,128)} async-done(((f32[2,3,64,512]{3,2,1,0:T(8,128)}), f32[2,3,512,512]{3,2,1,0:T(8,128)}) %all-gather.7.cloned.1.call-update) | async-done | bytes 6291472 | tf_op jit(solution)/shard_map/all_gather | solution.py:79
  453.2 4.1 fusion.15
  457.2 3.9 fusion.12
  461.2 2.0 fusion.19
  463.2 2.0 fusion.17
  466.3 1.3 dynamic-slice
  468.2 432.4 %all-reduce.3.cloned.1.call-done = f32[2,64,512]{1,0,2:T(2,128)} async-done(((f32[2,64,512]{1,0,2:T(2,128)}), f32[2,64,512]{1,0,2:T(2,128)}) %all-reduce.3.cloned.1.call-update) | async-done | bytes 262160
  (49 shorter events, 23.6 us)
Async XLA Ops:
  6.5 151.2 %all-gather.9.cloned.1.call-start = ((), (), s32[]{:S(2)}) async-start(), calls=%async_computation.2 | async-start | bytes 17039360 | tf_op jit(solution)/shard_map/all_gather | solution.py:13
  8.1 218.0 %copy-start.4 = (s32[64]{0:T(128)S(1)}, s32[64]{0:T(128)}, u32[]{:S(2)}) copy-start(s32[64]{0:T(128)} %param.8) | copy-start | bytes 772
  8.1 218.0 %copy-start.3 = (s32[512]{0:T(512)S(1)}, s32[512]{0:T(512)}, u32[]{:S(2)}) copy-start(s32[512]{0:T(512)} %param.9) | copy-start | bytes 6148
  11.6 320.4 %all-gather.5.cloned.1.call-start = ((), (), s32[]{:S(2)}) async-start(), calls=%async_computation | async-start | bytes 7077888 | tf_op jit(solution)/shard_map/all_gather | solution.py:76
  11.6 320.4 %copy-start.2 = (f32[2,3,64,512]{3,2,1,0:T(8,128)S(1)}, f32[2,3,64,512]{3,2,1,0:T(8,128)}, u32[]{:S(2)}) copy-start(f32[2,3,64,512]{3,2,1,0:T(8,128)} %param.6) | copy-start | bytes 2359300
  222.8 13.3 %collective-permute-start = (f32[2,3,64,512]{3,2,1,0:T(8,128)S(1)}, f32[2,3,64,512]{3,2,1,0:T(8,128)S(1)}, u32[]{:S(2)}, u32[]{:S(2)}) collective-permute-start(f32[2,3,64,512]{3,2,1,0:T(8,128)S(1)} %reverse_add_fusion), channel_id=1, source_target_pairs={{8,0},{16,8},{24,16},{32,24},{40,32},{48,40},{56,48},{64,56},{72,6... | collective-permute-start | bytes 2359304 | tf_op jit(solution)/shard_map/ppermute | solution.py:26
  237.2 216.0 %all-gather.7.cloned.1.call-start = ((), (), s32[]{:S(2)}) async-start(), calls=%async_computation.1 | async-start | bytes 7077888 | tf_op jit(solution)/shard_map/all_gather | solution.py:79
  332.0 10.1 %copy-start = (f32[2,3,512,512]{3,2,1,0:T(8,128)S(1)}, f32[2,3,512,512]{3,2,1,0:T(8,128)}, u32[]{:S(2)}) copy-start(f32[2,3,512,512]{3,2,1,0:T(8,128)} %all-gather.5.cloned.1.call-done) | copy-start | bytes 18874372
  350.0 550.6 %all-reduce.3.cloned.1.call-start = ((), (), s32[]{:S(2)}) async-start(), calls=%async_computation.3 | async-start | bytes 1048576
  453.2 8.0 copy-start.1
Sparse Core Ops, SparseCore 0:
  11.7 145.9 all-gather.8
  237.3 94.7 all-gather.4
  350.1 102.9 all-gather.6
  466.4 434.1 all-reduce.2
where the time goes:
time: 911 us; the launch traced here: 908 us
  waiting for transfers between devices  785 us (86%)
  other arithmetic  70.9 us (8%)
  matrix products  29 us (3%)
  between operations  13.9 us (2%)
    unnamed x5, waiting for transfers between devices  432 us
    all_gather x1, waiting for transfers between devices, carried_in(): gathered = lax.all_gather(part, axis)  145 us
    all_gather x1, waiting for transfers between devices, body(): middle_whole = lax.all_gather(middle, 'row', axis=2, tiled=True)  103 us
    all_gather x1, waiting for transfers between devices, body(): right_whole = lax.all_gather(right_factor, 'row', axis=2, tiled=True)  94.8 us
    add x62, other arithmetic, add_arrays(): return earlier + later  63.6 us
  transfers between devices with their start and end apart: 5, of which 5 were waited for; matrix products, arithmetic and copies ran while one was open for 0% of the time, Pallas kernels for 0%

commit v1 on v0

v1 whole, which is shorter than its diff:
```python
import jax
import jax.numpy as jnp
from jax import lax
from jax.experimental import pallas as pl
from jax.experimental.pallas import tpu as pltpu
from jax.sharding import PartitionSpec as P

EPS_MOST = 2
CHUNK = 8
VMEM = pl.BlockSpec(memory_space=pltpu.VMEM)
SMEM = pl.BlockSpec(memory_space=pltpu.SMEM)
BIG = 40 * 1024 * 1024


def call(kernel, out_shape, *args, scratch=(), smem=(), flops=0):
    moved = sum(a.size * 4 for a in args) + 4 * out_shape.size
    return pl.pallas_call(
        kernel,
        out_shape=out_shape,
        in_specs=[SMEM if i in smem else VMEM for i in range(len(args))],
        out_specs=VMEM,
        scratch_shapes=list(scratch),
        compiler_params=pltpu.CompilerParams(vmem_limit_bytes=BIG),
        cost_estimate=pl.CostEstimate(flops=flops, bytes_accessed=moved, transcendentals=0),
    )(*args)


def suffix_kernel(parts, out):
    count = parts.shape[0]
    state = jnp.zeros(parts.shape[1:], jnp.float32)
    for place in range(count - 1, -1, -1):
        out[place] = state
        state = state + parts[place]


def factor_kernel(carry, down, up, rim, eps_r, eps_c, out):
    slabs = down.shape[1]
    near_row = eps_r[...] == 1
    near_col = eps_c[...] == 1
    for part in range(2):
        below = carry[part]
        for slab in range(slabs - 1, -1, -1):
            here = below + down[part, slab]
            out[slab, part] = jnp.where(near_row, here, below)
            out[slab, 2 + part] = rim[part, slab] if slab < EPS_MOST else up[part, slab - EPS_MOST]
            out[slab, 4 + part] = jnp.where(near_col, here, below)
            below = here
    for idle in range(slabs, out.shape[0]):
        out[idle] = jnp.zeros(out.shape[1:], jnp.float32)


def split(value):
    high = value.astype(jnp.bfloat16)
    return high, (value - high.astype(jnp.float32)).astype(jnp.bfloat16)


def real_dot(first, second):
    dot = lambda a, b: jnp.dot(a, b, preferred_element_type=jnp.float32)
    return dot(first[0], second[0]) + (dot(first[0], second[1]) + dot(first[1], second[0]))


def complex_dot(first, second):
    p = real_dot(first[0], second[0])
    q = real_dot(first[1], second[1])
    r = real_dot(first[2], second[2])
    return p - q, r - p - q


def triple(re, im):
    return split(re), split(im), split(re + im)


def product_kernel(core, own, other, out, mid, last):
    me = core[0]
    half = own.shape[-1]
    chips, rows = own.shape[0], own.shape[2] * CHUNK * 2

    def rows_of(ref, array, parity):
        return ref[:, array, :, parity].reshape(half, half)

    for column, ref in enumerate((own, other)):
        for block in range(2):
            parity = me if block == 0 else 1 - me
            both = triple(rows_of(ref, 2, parity), rows_of(ref, 3, parity))
            for kind in range(3):
                for level in range(2):
                    mid[kind, level, block * half : (block + 1) * half, column * half : (column + 1) * half] = both[kind][level]
    for block in range(2):
        parity = me if block == 0 else 1 - me
        both = triple(rows_of(own, 4, parity), rows_of(own, 5, parity))
        for kind in range(3):
            for level in range(2):
                last[kind, level, block * half : (block + 1) * half, :] = both[kind][level]
    second = [(mid[kind, 0], mid[kind, 1]) for kind in range(3)]
    third = [(last[kind, 0], last[kind, 1]) for kind in range(3)]
    step = 2
    for start in range(0, chips, step):
        pieces = slice(start, start + step)

        def left(array):
            near = own[pieces, array].reshape(step * rows, half)
            far = other[pieces, array].reshape(step * rows, half)
            return jnp.concatenate([near, far], axis=1)

        middle = complex_dot(triple(left(0), left(1)), second)
        result = complex_dot(triple(*middle), third)
        for part in range(2):
            out[pieces, part] = result[part].reshape(step, rows, half)


def turn_kernel(scale, parts, out):
    total = parts[0]
    for chip in range(1, 6):
        total = total + parts[chip]
    rows = jnp.concatenate([total[0], total[1]], axis=0) * scale
    out[...] = rows.T.reshape(out.shape)


def last_kernel(parts, out):
    total = jnp.sum(parts[...], axis=0)
    turned = total.T
    rows = out.shape[1]
    out[0] = turned[:rows]
    out[1] = turned[rows:]


def body(data, wavenumbers, eps_rows, eps_cols):
    slab_count, row_count, width = data.shape[1:]
    deep = lax.axis_size("depth")
    chips = lax.axis_size("row")
    pairs = deep // 2
    half = width // 2
    six = 2 * slab_count
    place = lax.axis_index("depth")
    core = place % 2
    pair = place // 2
    total_depth = slab_count * deep
    f32 = jnp.float32

    spot = jnp.arange(width)
    parity = jnp.where(spot < half, core, 1 - core)
    column = (spot % half) // CHUNK * (2 * CHUNK) + parity * CHUNK + spot % CHUNK
    chosen = (jnp.arange(width)[:, None] == column[None, :]).astype(f32)
    sorted_data = jnp.dot(data.reshape(-1, width), chosen, precision=lax.Precision.HIGHEST)
    kept = sorted_data[:, :half].reshape(2, slab_count, row_count, half)
    given = sorted_data[:, half:].reshape(2, slab_count, row_count, half)
    swap = [(i, i ^ 1) for i in range(deep)]
    taken = lax.ppermute(given, "depth", swap)
    first = jnp.where(core == 0, kept, taken)
    second = jnp.where(core == 0, taken, kept)
    slabs = jnp.concatenate([first, second], axis=1)

    row_waves = lax.dynamic_slice_in_dim(wavenumbers, lax.axis_index("row") * row_count, row_count)
    mine = lambda v: lax.dynamic_index_in_dim(v.reshape(pairs, 2, CHUNK), core, 1, False).reshape(half)
    col_waves = mine(wavenumbers)
    near_cols = mine(eps_cols)
    levels = (pair * six + jnp.arange(six)).astype(f32) + 0.5
    phase = (row_waves[:, None] + col_waves[None, :])[None] * levels[:, None, None]
    cosine, sine = jnp.cos(phase), jnp.sin(phase)
    down = jnp.stack([slabs[0] * cosine - slabs[1] * sine, slabs[0] * sine + slabs[1] * cosine])
    up = jnp.stack([slabs[0] * cosine + slabs[1] * sine, slabs[1] * cosine - slabs[0] * sine])
    rim = lax.ppermute(up[:, six - EPS_MOST :], "depth", [(i, i + 2) for i in range(deep - 2)])

    groups = [[2 * e + c for e in range(pairs)] for c in range(2)]
    spread = lambda v: lax.all_to_all(v, "depth", 0, 0, axis_index_groups=groups, tiled=True)
    totals = jnp.sum(down, axis=1)
    tiles = totals.reshape(2, row_count // 8, 8, half // 128, 128).transpose(0, 1, 3, 2, 4).reshape(pairs, 8, 128)
    seen = spread(tiles)
    sums = call(suffix_kernel, jax.ShapeDtypeStruct(seen.shape, f32), seen)
    back = spread(sums)
    carry = back.reshape(2, row_count // 8, half // 128, 8, 128).transpose(0, 1, 3, 2, 4).reshape(2, row_count, half)

    pieces = call(
        factor_kernel,
        jax.ShapeDtypeStruct((chips, 6, row_count, half), f32),
        carry, down, up, rim, eps_rows.reshape(row_count, 1), near_cols.reshape(1, half),
    )
    whole = lax.all_to_all(pieces, "row", 0, 0, tiled=True)
    other = lax.ppermute(whole[:, :4], "depth", swap)
    shape = lambda v: v.reshape(chips, v.shape[1], row_count // 16, 2, 8, half)
    partial = call(
        product_kernel,
        jax.ShapeDtypeStruct((chips, 2, row_count, half), f32),
        core.reshape(1).astype(jnp.int32), shape(whole), shape(other),
        smem=(0,),
        scratch=[pltpu.VMEM((3, 2, width, width), jnp.bfloat16), pltpu.VMEM((3, 2, width, half), jnp.bfloat16)],
        flops=18 * width * width * (width + half),
    )
    gathered = lax.all_to_all(partial, "row", 0, 0, tiled=True)
    turned = call(
        lambda parts, out: turn_kernel(4.0 / total_depth, parts, out),
        jax.ShapeDtypeStruct((pairs, CHUNK, 2 * row_count), f32),
        gathered,
    )
    ends = spread(turned)
    return call(last_kernel, jax.ShapeDtypeStruct((2, row_count, CHUNK), f32), ends)


def solution(mesh):
    in_specs = (P(None, "depth", "row", None), P(), P("row"), P())
    out_specs = P(None, "row", "depth")
    return jax.shard_map(body, mesh=mesh, in_specs=in_specs, out_specs=out_specs, check_vma=False)
```

time: 911 us -> 165 us (0.18)
  waiting for transfers between devices: 785 us -> 13.3 us
  blocking collectives: 0 us -> 112 us
  other arithmetic: 70.9 us -> 4.55 us
  matrix products: 29 us -> 0.85 us
  starting transfers between devices: 3.54 us -> 24 us
  between operations: 13.9 us -> 0.23 us
    unnamed x5 -> x0, waiting for transfers between devices: 432 us -> none
    all_gather x3 -> x0, waiting for transfers between devices: 343 us -> none  [the longest x1 145 us: carried_in(): gathered = lax.all_gather(part, axis)]
    all_to_all x0 -> x4, blocking collectives: none -> 112 us  [the longest x2 51.2 us: body(): lax.all_to_all(v, 'depth', 0, 0, axis_index_groups=groups, tiled=True)]
    add x65 -> x4, other arithmetic: 64.4 us -> 1.68 us  [the longest x1 1.59 us: body(): slabs[0] * cosine + slabs[1] * sine]
    dot_general x8 -> x1, matrix products: 29 us -> 0.85 us  [body(): jnp.dot(data.reshape(-1, width), chosen, precision=lax.Precision.HIGHEST)]
    ppermute x1 -> x3, starting transfers between devices: 3.23 us -> 19.8 us  [the longest x1 8.79 us: body(): taken = lax.ppermute(given, 'depth', swap)]
  transfers between devices with their start and end apart: 5 -> 4, of which waited for: 5 -> 4; matrix products, arithmetic and copies ran while one was open for 0% -> 1% of each run, Pallas kernels for 0% -> 0%
where the time goes in v1:
time: 165 us; the launch traced here: 163 us
  blocking collectives  112 us (68%)
  starting transfers between devices  24 us (15%)
  waiting for transfers between devices  13.3 us (8%)
  Pallas kernels  5.76 us (3%)
  other arithmetic  4.55 us (3%)
  local copies, waits for them, and re-layouts  2.67 us (2%)
    all_to_all x2, blocking collectives, body(): lax.all_to_all(v, 'depth', 0, 0, axis_index_groups=groups, tiled=True)  51.2 us
    all_to_all x1, blocking collectives, body(): whole = lax.all_to_all(pieces, 'row', 0, 0, tiled=True)  40.9 us
    all_to_all x1, blocking collectives, body(): gathered = lax.all_to_all(partial, 'row', 0, 0, tiled=True)  19.8 us
    ppermute x1, starting transfers between devices, body(): taken = lax.ppermute(given, 'depth', swap)  8.79 us
    ppermute x1, starting transfers between devices, body(): other = lax.ppermute(whole[:, :4], 'depth', swap)  7.84 us
    all_to_all x1, waiting for transfers between devices, body(): lax.all_to_all(v, 'depth', 0, 0, axis_index_groups=groups, tiled=True)  5.82 us
    pallas_call x5, Pallas kernels, call(): pl.pallas_call(kernel, out_shape=out_shape, in_specs=[SMEM if i in smem e...  5.76 us
    all_to_all x1, starting transfers between devices, body(): lax.all_to_all(v, 'depth', 0, 0, axis_index_groups=groups, tiled=True)  4.2 us
  transfers between devices with their start and end apart: 4, of which 4 were waited for; matrix products, arithmetic and copies ran while one was open for 1% of the time, Pallas kernels for 0%

profile of v1, /device:TPU:1, one launch (start us, length us, event | category | flops | bytes accessed | tf_op | source)
XLA Modules:
  0.0 163.1 jit_solution(1186309367280926641)
XLA Ops:
  0.0 0.0 copy-start
  0.0 0.0 copy-start.2
  0.0 1.1 copy-done
  1.1 0.9 convolution_bitcast_fusion
  2.0 0.1 fusion.25
  2.1 8.8 %collective-permute-start = (f32[2,3,64,256]{3,2,1,0:T(8,128)S(1)}, f32[2,3,64,256]{3,2,1,0:T(8,128)S(1)}, u32[]{:S(2)}, u32[]{:S(2)}) collective-permute-start(f32[2,3,64,256]{3,2,1,0:T(8,128)S(1)} %bitcast.26), channel_id=1, source_target_pairs={{0,8},{8,0},{16,24},{24,16},{32,40},{40,32},{48,56},{56,48},{64,72... | collective-permute-start | bytes 1179656 | tf_op jit(solution)/shard_map/ppermute | solution.py:148
  10.9 0.0 copy-done.2
  10.9 0.1 reshape.128
  11.0 0.1 dynamic_slice.11
  11.1 0.1 dynamic-slice_reduce_fusion.1
  11.1 0.1 add.103
  11.2 0.1 broadcast_add_fusion
  11.3 0.9 collective-permute-done
  12.2 0.1 broadcast_select_fusion.1
  12.2 1.6 fusion.6
  13.8 0.0 copy-start.4
  13.9 0.0 copy-start.3
  13.9 1.6 %fusion.8 = (f32[1,6,64,256]{3,2,1,0:T(8,128)S(1)}, f32[1,6,64,256]{3,2,1,0:T(8,128)S(1)}, f32[1,6,64,256]{3,2,1,0:T(8,128)S(1)}) fusion(f32[1,6,64,256]{3,2,1,0:T(8,128)S(1)} %get-tuple-element.7, f32[1,6,64,256]{3,2,1,0:T(8,128)S(1)} %get-tuple-element.6, f32[6]{0:T(128)S(1)} %convert_add_fusion, f32[64,256]{1,0:T(8,128)S(1)} %broadcast_add_fusion), kind=kLoop, calls=%fused_computation.19 | loop fusion | flops 786432 | bytes 2031640 | tf_op jit(solution)/shard_map/sub | solution.py:161
  15.5 0.0 copy-start.1
  15.5 0.1 pad_maximum_fusion.1
  15.6 25.8 %all_to_all.25.parts = f32[32,8,128]{2,1,0:T(8,128)S(1)} all-to-all(f32[32,8,128]{2,1,0:T(8,128)S(1)} %bitcast.25), channel_id=1, replica_groups={{0,16,32,48,64,80,96,112,128,144,160,176,192,208,224,240,256,272,288,30..., dimensions={0} | all-to-all | bytes 262144 | tf_op jit(solution)/shard_map/all_to_all | solution.py:165
  41.5 0.7 shard_map.46
  42.2 4.2 %all-to-all-start.1 = ((f32[32,8,128]{2,1,0:T(8,128)}), f32[32,8,128]{2,1,0:T(8,128)S(1)}, u32[]{:S(2)}, u32[]{:S(2)}) async-start(f32[32,8,128]{2,1,0:T(8,128)} %shard_map.46), calls=%async_computation.1 | async-start | bytes 262144 | tf_op jit(solution)/shard_map/all_to_all | solution.py:165
  46.4 0.0 copy-done.1
  46.4 3.1 %collective-permute-start.1 = (f32[2,2,64,256]{3,2,1,0:T(8,128)S(1)}, f32[2,2,64,256]{3,2,1,0:T(8,128)S(1)}, u32[]{:S(2)}, u32[]{:S(2)}) collective-permute-start(f32[2,2,64,256]{3,2,1,0:T(8,128)S(1)} %fusion.10), channel_id=1, source_target_pairs={{0,16},{8,24},{16,32},{24,40},{32,48},{40,56},{48,64},{56,72},{64,... | collective-permute-start | bytes 786440 | tf_op jit(solution)/shard_map/ppermute | solution.py:162
  49.6 0.0 copy-done.4
  49.6 0.1 copy.7.eps_r
  49.7 0.0 copy-done.3
  49.7 0.1 reshape.134
  49.8 0.1 dynamic-slice_reduce_fusion
  49.8 0.1 reshape_reshape.3.eps_c
  49.9 1.1 pad_maximum_fusion.up
  51.0 2.8 %collective-permute-done.1.rim = f32[2,2,64,256]{3,2,1,0:T(8,128)S(1)} collective-permute-done((f32[2,2,64,256]{3,2,1,0:T(8,128)S(1)}, f32[2,2,64,256]{3,2,1,0:T(8,128)S(1)}, u32[]{:S(2)}, u32[]{:S(2)}) %collective-permute-start.1) | collective-permute-done | bytes 262176 | tf_op jit(solution)/shard_map/ppermute | solution.py:162
  53.8 5.8 %all-to-all-done.1 = f32[32,8,128]{2,1,0:T(8,128)S(1)} async-done(((f32[32,8,128]{2,1,0:T(8,128)}), f32[32,8,128]{2,1,0:T(8,128)S(1)}, u32[]{:S(2)}, u32[]{:S(2)}) %all-to-all-start.1) | async-done | bytes 131104 | tf_op jit(solution)/shard_map/all_to_all | solution.py:165
  59.6 0.2 shard_map.47
  59.9 40.9 %all_to_all.26 = f32[8,6,64,256]{3,2,1,0:T(8,128)S(1)} all-to-all(f32[8,6,64,256]{3,2,1,0:T(8,128)S(1)} %shard_map.47), channel_id=1, replica_groups=mesh['depth'=64,'row'=8] {'row'}, dimensions={0} | all-to-all | bytes 6291456 | tf_op jit(solution)/shard_map/all_to_all | solution.py:178
  100.7 0.1 slice.36
  100.9 7.8 %collective-permute-start.2 = (f32[8,4,64,256]{3,2,1,0:T(8,128)S(1)}, f32[8,4,64,256]{3,2,1,0:T(8,128)S(1)}, u32[]{:S(2)}, u32[]{:S(2)}) collective-permute-start(f32[8,4,64,256]{3,2,1,0:T(8,128)S(1)} %slice.36), channel_id=1, source_target_pairs={{0,8},{8,0},{16,24},{24,16},{32,40},{40,32},{48,56},{56,48},{64,72... | collective-permute-start | bytes 6291464 | tf_op jit(solution)/shard_map/ppermute | solution.py:179
  108.7 3.8 %collective-permute-done.2 = f32[8,4,64,256]{3,2,1,0:T(8,128)S(1)} collective-permute-done((f32[8,4,64,256]{3,2,1,0:T(8,128)S(1)}, f32[8,4,64,256]{3,2,1,0:T(8,128)S(1)}, u32[]{:S(2)}, u32[]{:S(2)}) %collective-permute-start.2) | collective-permute-done | bytes 2097184 | tf_op jit(solution)/shard_map/ppermute | solution.py:179
  112.5 4.6 %shard_map.48 = f32[8,2,64,256]{3,2,1,0:T(8,128)S(1)} custom-call(s32[1]{0:T(128)} %bitcast.core, f32[8,6,4,2,8,256]{5,4,3,2,1,0:T(8,128)S(1)} %bitcast.21, f32[8,4,4,2,8,256]{5,4,3,2,1,0:T(8,128)S(1)} %bitcast.23), custom_call_target="tpu_custom_call" | custom-call | flops 3623878656 | bytes 6291460 | tf_op jit(solution)/shard_map/pallas_call | solution.py:17
  117.1 19.8 %all_to_all.27.parts = f32[8,2,64,256]{3,2,1,0:T(8,128)S(1)} all-to-all(f32[8,2,64,256]{3,2,1,0:T(8,128)S(1)} %shard_map.48), channel_id=1, replica_groups=mesh['depth'=64,'row'=8] {'row'}, dimensions={0} | all-to-all | bytes 2097152 | tf_op jit(solution)/shard_map/all_to_all | solution.py:189
  136.9 0.1 shard_map.49
  137.0 25.3 %all_to_all.28.parts = f32[32,8,128]{2,1,0:T(8,128)S(1)} all-to-all(f32[32,8,128]{2,1,0:T(8,128)S(1)} %shard_map.49), channel_id=1, replica_groups={{0,16,32,48,64,80,96,112,128,144,160,176,192,208,224,240,256,272,288,30..., dimensions={0} | all-to-all | bytes 262144 | tf_op jit(solution)/shard_map/all_to_all | solution.py:165
  162.3 0.1 shard_map.50
  162.5 0.7 copy.8
  (3 shorter events, 0.0 us)
Async XLA Ops:
  0.0 1.1 copy-start
  0.0 10.9 %copy-start.2 = (f32[512]{0:T(512)S(1)}, f32[512]{0:T(512)}, u32[]{:S(2)}) copy-start(f32[512]{0:T(512)} %param.5) | copy-start | bytes 6148
  2.1 10.1 %collective-permute-start = (f32[2,3,64,256]{3,2,1,0:T(8,128)S(1)}, f32[2,3,64,256]{3,2,1,0:T(8,128)S(1)}, u32[]{:S(2)}, u32[]{:S(2)}) collective-permute-start(f32[2,3,64,256]{3,2,1,0:T(8,128)S(1)} %bitcast.26), channel_id=1, source_target_pairs={{0,8},{8,0},{16,24},{24,16},{32,40},{40,32},{48,56},{56,48},{64,72... | collective-permute-start | bytes 1179656 | tf_op jit(solution)/shard_map/ppermute | solution.py:148
  13.8 35.7 %copy-start.4 = (s32[64]{0:T(128)S(1)}, s32[64]{0:T(128)}, u32[]{:S(2)}) copy-start(s32[64]{0:T(128)} %param.6) | copy-start | bytes 772
  13.9 35.8 %copy-start.3 = (s32[512]{0:T(512)S(1)}, s32[512]{0:T(512)}, u32[]{:S(2)}) copy-start(s32[512]{0:T(512)} %param.7) | copy-start | bytes 6148
  15.5 30.8 %copy-start.1 = (f32[1,6,64,256]{3,2,1,0:T(8,128)}, f32[1,6,64,256]{3,2,1,0:T(8,128)S(1)}, u32[]{:S(2)}) copy-start(f32[1,6,64,256]{3,2,1,0:T(8,128)S(1)} %get-tuple-element.8) | copy-start | bytes 1179652
  42.2 17.5 %all-to-all-start.1 = ((f32[32,8,128]{2,1,0:T(8,128)}), f32[32,8,128]{2,1,0:T(8,128)S(1)}, u32[]{:S(2)}, u32[]{:S(2)}) async-start(f32[32,8,128]{2,1,0:T(8,128)} %shard_map.46), calls=%async_computation.1 | async-start | bytes 262144 | tf_op jit(solution)/shard_map/all_to_all | solution.py:165
  46.4 7.4 %collective-permute-start.1 = (f32[2,2,64,256]{3,2,1,0:T(8,128)S(1)}, f32[2,2,64,256]{3,2,1,0:T(8,128)S(1)}, u32[]{:S(2)}, u32[]{:S(2)}) collective-permute-start(f32[2,2,64,256]{3,2,1,0:T(8,128)S(1)} %fusion.10), channel_id=1, source_target_pairs={{0,16},{8,24},{16,32},{24,40},{32,48},{40,56},{48,64},{56,72},{64,... | collective-permute-start | bytes 786440 | tf_op jit(solution)/shard_map/ppermute | solution.py:162
  100.9 11.6 %collective-permute-start.2 = (f32[8,4,64,256]{3,2,1,0:T(8,128)S(1)}, f32[8,4,64,256]{3,2,1,0:T(8,128)S(1)}, u32[]{:S(2)}, u32[]{:S(2)}) collective-permute-start(f32[8,4,64,256]{3,2,1,0:T(8,128)S(1)} %slice.36), channel_id=1, source_target_pairs={{0,8},{8,0},{16,24},{24,16},{32,40},{40,32},{48,56},{56,48},{64,72... | collective-permute-start | bytes 6291464 | tf_op jit(solution)/shard_map/ppermute | solution.py:179

commit v2 on v1

v2 whole, which is shorter than its diff:
```python
import jax
import jax.numpy as jnp
from jax import lax
from jax.experimental import pallas as pl
from jax.experimental.pallas import tpu as pltpu
from jax.sharding import PartitionSpec as P

EPS_MOST = 2
CHUNK = 8
SLABS = 6
NEAR = 8
VMEM = pl.BlockSpec(memory_space=pltpu.VMEM)
SMEM = pl.BlockSpec(memory_space=pltpu.SMEM)
MIB = 1024 * 1024
f32 = jnp.float32


def call(kernel, out_shape, *args, scratch=(), smem=(), flops=0, room=6):
    single = not isinstance(out_shape, list)
    shapes = [out_shape] if single else out_shape
    shapes = [s if hasattr(s, "dtype") else jax.ShapeDtypeStruct(s, f32) for s in shapes]
    moved = sum(a.size * 4 for a in args) + sum(4 * s.size for s in shapes)
    return pl.pallas_call(
        kernel,
        out_shape=shapes[0] if single else shapes,
        in_specs=[SMEM if i in smem else VMEM for i in range(len(args))],
        out_specs=VMEM if single else [VMEM] * len(shapes),
        scratch_shapes=list(scratch),
        compiler_params=pltpu.CompilerParams(vmem_limit_bytes=room * MIB),
        cost_estimate=pl.CostEstimate(flops=flops, bytes_accessed=moved, transcendentals=0),
    )(*args)


def phase_kernel(core, kept, taken, row_trig, col_trig, down, up, rim, total):
    first_core = core[0] == 0
    held = kept.shape[1]
    totals = [None, None]
    for slab in range(2 * held):
        local = slab % held
        pick = lambda part: (
            jnp.where(first_core, kept[part, local], taken[part, local])
            if slab < held
            else jnp.where(first_core, taken[part, local], kept[part, local])
        )
        re, im = pick(0), pick(1)
        row_cos, row_sin = row_trig[:, slab : slab + 1], row_trig[:, 8 + slab : 9 + slab]
        col_cos, col_sin = col_trig[slab : slab + 1, :], col_trig[8 + slab : 9 + slab, :]
        cosine = row_cos * col_cos - row_sin * col_sin
        sine = row_sin * col_cos + row_cos * col_sin
        a, b, c, d = re * cosine, im * sine, re * sine, im * cosine
        sums = (a - b, c + d)
        rises = (a + b, d - c)
        for part in range(2):
            down[part, slab] = sums[part]
            totals[part] = sums[part] if slab == 0 else totals[part] + sums[part]
            if slab < 2 * held - EPS_MOST:
                up[part, slab] = rises[part]
            else:
                rim[part, slab - 2 * held + EPS_MOST] = rises[part]
    for part in range(2):
        for block in range(8):
            for lane in range(2):
                tile = totals[part][8 * block : 8 * block + 8, 128 * lane : 128 * lane + 128]
                total[(8 * part + block) // 2, 2 * (block % 2) + lane] = tile


def early_kernel(down, up, rim, eps_r, eps_c, out):
    gap = (eps_c[...] == 1).astype(f32) - (eps_r[...] == 1).astype(f32)
    for slab in range(SLABS):
        for part in range(2):
            out[slab, part] = rim[part, slab] if slab < EPS_MOST else up[part, slab - EPS_MOST]
            out[slab, 2 + part] = down[part, slab] * gap
    for idle in range(SLABS, out.shape[0]):
        out[idle] = jnp.zeros(out.shape[1:], f32)


def group_kernel(parts, out, total):
    state = parts[parts.shape[0] - 1]
    out[parts.shape[0] - 1] = jnp.zeros(parts.shape[1:], f32)
    for place in range(parts.shape[0] - 2, -1, -1):
        out[place] = state
        state = state + parts[place]
    total[...] = state


def deep_kernel(sums, *refs):
    deeper, out = refs[:-1], refs[-1]
    extra = deeper[0][...]
    for other in deeper[1:]:
        extra = extra + other[...]
    for place in range(sums.shape[0]):
        out[place] = sums[place] + extra


def late_kernel(carry, down, eps_r, out):
    near_row = eps_r[...] == 1
    for part in range(2):
        for block in range(8):
            rows = slice(8 * block, 8 * block + 8)
            for lane in range(2):
                cols = slice(128 * lane, 128 * lane + 128)
                below = carry[(8 * part + block) // 2, 2 * (block % 2) + lane]
                for slab in range(SLABS - 1, -1, -1):
                    here = below + down[part, slab, rows, cols]
                    out[slab, part, rows, cols] = jnp.where(near_row[rows], here, below)
                    below = here
    for idle in range(SLABS, out.shape[0]):
        out[idle] = jnp.zeros(out.shape[1:], f32)


def split(value):
    high = value.astype(jnp.bfloat16)
    return high, (value - high.astype(f32)).astype(jnp.bfloat16)


def real_dot(first, second):
    dot = lambda a, b: jnp.dot(a, b, preferred_element_type=f32)
    return dot(first[0], second[0]) + (dot(first[0], second[1]) + dot(first[1], second[0]))


def complex_dot(first, second):
    p = real_dot(first[0], second[0])
    q = real_dot(first[1], second[1])
    r = real_dot(first[2], second[2])
    return p - q, r - p - q


def triple(re, im):
    return split(re), split(im), split(re + im)


def ready_kernel(core, own, far, mid):
    half = own.shape[-1]
    for block in range(2):
        parity = core[0] if block == 0 else 1 - core[0]
        stretch = slice(block * half, block * half + half)
        for column, ref in enumerate((own, far)):
            both = triple(*(ref[:, part, :, parity].reshape(half, half) for part in range(2)))
            for kind in range(3):
                for level in range(2):
                    mid[kind, level, stretch, column * half : (column + 1) * half] = both[kind][level]


def product_kernel(core, own, far, early, mid, out, last):
    half = out.shape[-1]
    chips, rows = out.shape[0], out.shape[2]
    for block in range(2):
        parity = core[0] if block == 0 else 1 - core[0]
        stretch = slice(block * half, block * half + half)
        both = triple(*((own[:, part, :, parity] + early[:, 2 + part, :, parity]).reshape(half, half) for part in range(2)))
        for kind in range(3):
            for level in range(2):
                last[kind, level, stretch, :] = both[kind][level]
    second = [(mid[kind, 0], mid[kind, 1]) for kind in range(3)]
    third = [(last[kind, 0], last[kind, 1]) for kind in range(3)]
    step = 2
    for start in range(0, chips, step):
        pieces = slice(start, start + step)
        left = [jnp.concatenate([ref[pieces, part].reshape(step * rows, half) for ref in (own, far)], axis=1) for part in range(2)]
        middle = complex_dot(triple(*left), second)
        result = complex_dot(triple(*middle), third)
        for part in range(2):
            out[pieces, part] = result[part].reshape(step, rows, half)


def turn_kernel(scale, parts, out):
    total = parts[0]
    for chip in range(1, SLABS):
        total = total + parts[chip]
    turned = (jnp.concatenate([total[0], total[1]], axis=0) * scale).T
    out[...] = turned.reshape(out.shape)


def last_kernel(parts, out):
    total = parts[0]
    for place in range(1, parts.shape[0]):
        total = total + parts[place]
    turned = total.T
    rows = out.shape[1]
    out[0] = turned[:rows]
    out[1] = turned[rows:]


def body(data, wavenumbers, eps_rows, eps_cols):
    slab_count, row_count, width = data.shape[1:]
    deep = lax.axis_size("depth")
    chips = lax.axis_size("row")
    pairs = deep // 2
    half = width // 2
    place = lax.axis_index("depth")
    core = place % 2
    pair = place // 2
    total_depth = slab_count * deep
    me = core.reshape(1).astype(jnp.int32)

    spot = jnp.arange(width)
    parity = jnp.where(spot < half, core, 1 - core)
    column = (spot % half) // CHUNK * (2 * CHUNK) + parity * CHUNK + spot % CHUNK
    chosen = (jnp.arange(width)[:, None] == column[None, :]).astype(f32)
    sorted_data = jnp.dot(data.reshape(-1, width), chosen, precision=lax.Precision.HIGHEST)
    kept = sorted_data[:, :half].reshape(2, slab_count, row_count, half)
    given = sorted_data[:, half:].reshape(2, slab_count, row_count, half)
    swap = [(i, i ^ 1) for i in range(deep)]
    taken = lax.ppermute(given, "depth", swap)

    row_waves = lax.dynamic_slice_in_dim(wavenumbers, lax.axis_index("row") * row_count, row_count)
    mine = lambda v: lax.dynamic_index_in_dim(v.reshape(pairs, 2, CHUNK), core, 1, False).reshape(half)
    col_waves = mine(wavenumbers)
    near_cols = mine(eps_cols).reshape(1, half)
    levels = (pair * SLABS + jnp.arange(8)).astype(f32) + 0.5
    row_phase = row_waves[:, None] * levels[None, :]
    col_phase = levels[:, None] * col_waves[None, :]
    row_trig = jnp.concatenate([jnp.cos(row_phase), jnp.sin(row_phase)], axis=1)
    col_trig = jnp.concatenate([jnp.cos(col_phase), jnp.sin(col_phase)], axis=0)
    down, up, rim, total = call(
        phase_kernel,
        [
            (2, SLABS, row_count, half),
            (2, SLABS - EPS_MOST, row_count, half),
            (2, EPS_MOST, row_count, half),
            (NEAR, 32 // NEAR, 8, 128),
        ],
        me, kept, taken, row_trig, col_trig,
        smem=(0,),
        room=10,
    )

    near = [[2 * (g * NEAR + i) + c for i in range(NEAR)] for g in range(pairs // NEAR) for c in range(2)]
    spread = lambda v, groups: lax.all_to_all(v, "depth", 0, 0, axis_index_groups=groups, tiled=True)
    seen = spread(total, near)
    sums, group = call(group_kernel, [seen.shape, seen.shape[1:]], seen)
    deeper = [
        lax.ppermute(group, "depth", [(i, i - shift) for i in range(shift, deep)])
        for shift in range(2 * NEAR, deep, 2 * NEAR)
    ]

    rim = lax.ppermute(rim, "depth", [(i, i + 2) for i in range(deep - 2)])
    row_marks = eps_rows.reshape(row_count, 1)
    early = call(early_kernel, (chips, 4, row_count, half), down, up, rim, row_marks, near_cols)
    early = lax.all_to_all(early, "row", 0, 0, tiled=True)
    early, *deeper = lax.optimization_barrier((early, *deeper))
    carry = spread(call(deep_kernel, sums.shape, sums, *deeper), near)
    early_far = lax.ppermute(early, "depth", swap)
    shape = lambda v: v.reshape(chips, v.shape[1], row_count // 16, 2, 8, half)
    mid = call(
        ready_kernel,
        jax.ShapeDtypeStruct((3, 2, width, width), jnp.bfloat16),
        me, shape(early), shape(early_far),
        smem=(0,),
        room=12,
    )

    whole = (chips, 2, row_count, half)
    late = call(late_kernel, whole, carry, down, row_marks)
    left = lax.all_to_all(late, "row", 0, 0, tiled=True)
    left_far = lax.ppermute(left, "depth", swap)
    partial = call(
        product_kernel,
        whole,
        me, shape(left), shape(left_far), shape(early), mid,
        smem=(0,),
        scratch=[pltpu.VMEM((3, 2, width, half), jnp.bfloat16)],
        flops=18 * width * width * (width + half),
        room=20,
    )
    gathered = lax.all_to_all(partial, "row", 0, 0, tiled=True)
    turned = call(
        lambda parts, out: turn_kernel(4.0 / total_depth, parts, out),
        (pairs, CHUNK, 2 * row_count),
        gathered,
    )
    ends = spread(turned, [[2 * e + c for e in range(pairs)] for c in range(2)])
    return call(last_kernel, (2, row_count, CHUNK), ends)


def solution(mesh):
    in_specs = (P(None, "depth", "row", None), P(), P("row"), P())
    out_specs = P(None, "row", "depth")
    return jax.shard_map(body, mesh=mesh, in_specs=in_specs, out_specs=out_specs, check_vma=False)
```

time: 165 us -> 152 us (0.921)
  blocking collectives: 112 us -> 62 us
  waiting for transfers between devices: 13.3 us -> 34.1 us
  starting transfers between devices: 24 us -> 38.6 us
  Pallas kernels: 5.76 us -> 10.2 us
  other arithmetic: 4.55 us -> 0.26 us
    all_to_all x2 -> x1, blocking collectives: 51.2 us -> 24.7 us  [body(): lax.all_to_all(v, 'depth', 0, 0, axis_index_groups=groups, tiled=True)]
    all_to_all x1, blocking collectives: 40.9 us -> 17.5 us  [body(): left = lax.all_to_all(late, 'row', 0, 0, tiled=True)]
    ppermute x2 -> x6, waiting for transfers between devices: 6.58 us -> 22.7 us  [the longest x3 17 us: body(): lax.ppermute(group, 'depth', [(i, i - shift) for i in range(shift, deep)])]
    all_to_all x0 -> x1, waiting for transfers between devices: none -> 7.63 us  [body(): early = lax.all_to_all(early, 'row', 0, 0, tiled=True)]
    all_to_all x1 -> x2, starting transfers between devices: 4.2 us -> 10.2 us  [body(): lax.all_to_all(v, 'depth', 0, 0, axis_index_groups=groups, tiled=True)]
    ppermute x2 -> x6, starting transfers between devices: 11 us -> 15.6 us  [the longest x1 5.45 us: body(): left_far = lax.ppermute(left, 'depth', swap)]
    pallas_call x5 -> x9, Pallas kernels: 5.76 us -> 10.2 us  [call(): pl.pallas_call(kernel, out_shape=shapes[0] if single else shapes, in_spec...]
    all_to_all x0 -> x1, starting transfers between devices: none -> 4.03 us  [body(): early = lax.all_to_all(early, 'row', 0, 0, tiled=True)]
  transfers between devices with their start and end apart: 4 -> 10, of which waited for: 4 -> 8; matrix products, arithmetic and copies ran while one was open for 1% -> 1% of each run, Pallas kernels for 0% -> 2%
where the time goes in v2:
time: 152 us; the launch traced here: 150 us
  blocking collectives  62 us (41%)
  starting transfers between devices  38.6 us (25%)
  waiting for transfers between devices  34.1 us (22%)
  Pallas kernels  10.2 us (7%)
  local copies, waits for them, and re-layouts  3.74 us (2%)
    all_to_all x1, blocking collectives, body(): lax.all_to_all(v, 'depth', 0, 0, axis_index_groups=groups, tiled=True)  24.7 us
    all_to_all x1, blocking collectives, body(): gathered = lax.all_to_all(partial, 'row', 0, 0, tiled=True)  19.8 us
    all_to_all x1, blocking collectives, body(): left = lax.all_to_all(late, 'row', 0, 0, tiled=True)  17.5 us
    ppermute x3, waiting for transfers between devices, body(): lax.ppermute(group, 'depth', [(i, i - shift) for i in range(shift, deep)])  17 us
    all_to_all x2, starting transfers between devices, body(): lax.all_to_all(v, 'depth', 0, 0, axis_index_groups=groups, tiled=True)  10.2 us
    pallas_call x9, Pallas kernels, call(): pl.pallas_call(kernel, out_shape=shapes[0] if single else shapes, in_spec...  10.2 us
    ppermute x1, starting transfers between devices, body(): taken = lax.ppermute(given, 'depth', swap)  8.78 us
    all_to_all x1, waiting for transfers between devices, body(): early = lax.all_to_all(early, 'row', 0, 0, tiled=True)  7.63 us
  transfers between devices with their start and end apart: 10, of which 8 were waited for; matrix products, arithmetic and copies ran while one was open for 1% of the time, Pallas kernels for 2%

profile of v2, /device:TPU:1, one launch (start us, length us, event | category | flops | bytes accessed | tf_op | source)
XLA Modules:
  0.0 150.0 jit_solution(7166099871135541797)
XLA Ops:
  0.0 0.0 copy-start
  0.0 0.0 copy-start.3
  0.0 1.1 copy-done
  1.1 0.0 copy-start.4
  1.1 0.0 copy-start.5
  1.1 0.9 convolution_bitcast_fusion
  2.0 0.1 fusion.13
  2.1 8.8 %collective-permute-start = (f32[2,3,64,256]{3,2,1,0:T(8,128)S(1)}, f32[2,3,64,256]{3,2,1,0:T(8,128)S(1)}, u32[]{:S(2)}, u32[]{:S(2)}) collective-permute-start(f32[2,3,64,256]{3,2,1,0:T(8,128)S(1)} %bitcast.18), channel_id=1, source_target_pairs={{0,8},{8,0},{16,24},{24,16},{32,40},{40,32},{48,56},{56,48},{64,72... | collective-permute-start | bytes 1179656 | tf_op jit(solution)/shard_map/ppermute | solution.py:204
  10.9 0.0 copy-done.3
  10.9 0.1 dynamic_slice.11
  11.0 0.1 multiply_cosine_fusion.1
  11.1 0.1 reshape.92
  11.2 0.1 dynamic-slice_reduce_fusion.1
  11.3 0.1 mul.61
  11.4 0.1 copy.11.row_trig
  11.5 0.1 multiply_cosine_fusion
  11.6 0.6 collective-permute-done.taken
  12.2 1.0 shard_map.46
  13.2 0.0 copy-start.1
  13.2 3.4 %all-to-all-start = ((f32[8,4,8,128]{3,2,1,0:T(8,128)}), f32[8,4,8,128]{3,2,1,0:T(8,128)S(1)}, u32[]{:S(2)}, u32[]{:S(2)}) async-start(f32[8,4,8,128]{3,2,1,0:T(8,128)} %get-tuple-element.15), calls=%async_computation | async-start | bytes 262144 | tf_op jit(solution)/shard_map/all_to_all | solution.py:229
  16.5 3.3 %collective-permute-start.1 = (f32[2,2,64,256]{3,2,1,0:T(8,128)S(1)}, f32[2,2,64,256]{3,2,1,0:T(8,128)S(1)}, u32[]{:S(2)}, u32[]{:S(2)}) collective-permute-start(f32[2,2,64,256]{3,2,1,0:T(8,128)S(1)} %get-tuple-element.19), channel_id=1, source_target_pairs={{0,16},{8,24},{16,32},{24,40},{32,48},{40,56},{48,64},{56,72},{64,... | collective-permute-start | bytes 786440 | tf_op jit(solution)/shard_map/ppermute | solution.py:237
  19.8 0.0 copy-done.4
  19.8 0.1 reshape.94
  19.9 0.1 dynamic-slice_reduce_fusion
  20.0 0.1 reshape_reshape.3.eps_c
  20.1 0.0 copy-done.5
  20.1 0.1 copy.12.eps_r
  20.2 5.5 %collective-permute-done.1.rim = f32[2,2,64,256]{3,2,1,0:T(8,128)S(1)} collective-permute-done((f32[2,2,64,256]{3,2,1,0:T(8,128)S(1)}, f32[2,2,64,256]{3,2,1,0:T(8,128)S(1)}, u32[]{:S(2)}, u32[]{:S(2)}) %collective-permute-start.1) | collective-permute-done | bytes 262176 | tf_op jit(solution)/shard_map/ppermute | solution.py:237
  25.7 1.5 shard_map.48
  27.2 0.0 all-to-all-done.parts
  27.2 0.0 copy-done.1
  27.2 4.0 %all-to-all-start.1 = ((f32[8,4,64,256]{3,2,1,0:T(8,128)}), f32[8,4,64,256]{3,2,1,0:T(8,128)S(1)}, u32[]{:S(2)}, u32[]{:S(2)}) async-start(f32[8,4,64,256]{3,2,1,0:T(8,128)} %shard_map.48), calls=%async_computation.1 | async-start | bytes 4194304 | tf_op jit(solution)/shard_map/all_to_all | solution.py:240
  31.2 1.3 collective-permute-start.2
  32.5 1.3 collective-permute-start.3
  33.8 1.3 collective-permute-start.4
  35.1 8.6 %collective-permute-done.2.refs_0_ = f32[4,8,128]{2,1,0:T(8,128)S(1)} collective-permute-done((f32[4,8,128]{2,1,0:T(8,128)S(1)}, f32[4,8,128]{2,1,0:T(8,128)S(1)}, u32[]{:S(2)}, u32[]{:S(2)}) %collective-permute-start.2) | collective-permute-done | bytes 16416 | tf_op jit(solution)/shard_map/ppermute | solution.py:233
  43.7 6.2 %collective-permute-done.3.refs_1_ = f32[4,8,128]{2,1,0:T(8,128)S(1)} collective-permute-done((f32[4,8,128]{2,1,0:T(8,128)S(1)}, f32[4,8,128]{2,1,0:T(8,128)S(1)}, u32[]{:S(2)}, u32[]{:S(2)}) %collective-permute-start.3) | collective-permute-done | bytes 16416 | tf_op jit(solution)/shard_map/ppermute | solution.py:233
  49.9 2.2 %collective-permute-done.4.refs_2_ = f32[4,8,128]{2,1,0:T(8,128)S(1)} collective-permute-done((f32[4,8,128]{2,1,0:T(8,128)S(1)}, f32[4,8,128]{2,1,0:T(8,128)S(1)}, u32[]{:S(2)}, u32[]{:S(2)}) %collective-permute-start.4) | collective-permute-done | bytes 16416 | tf_op jit(solution)/shard_map/ppermute | solution.py:233
  52.1 7.6 %all-to-all-done.1 = f32[8,4,64,256]{3,2,1,0:T(8,128)S(1)} async-done(((f32[8,4,64,256]{3,2,1,0:T(8,128)}), f32[8,4,64,256]{3,2,1,0:T(8,128)S(1)}, u32[]{:S(2)}, u32[]{:S(2)}) %all-to-all-start.1) | async-done | bytes 2097184 | tf_op jit(solution)/shard_map/all_to_all | solution.py:240
  59.8 0.7 shard_map.49
  60.4 6.8 %all-to-all-start.2 = ((f32[8,4,8,128]{3,2,1,0:T(8,128)}), f32[8,4,8,128]{3,2,1,0:T(8,128)S(1)}, u32[]{:S(2)}, u32[]{:S(2)}) async-start(f32[8,4,8,128]{3,2,1,0:T(8,128)} %shard_map.49), calls=%async_computation.2 | async-start | bytes 262144 | tf_op jit(solution)/shard_map/all_to_all | solution.py:229
  67.2 3.0 %collective-permute-start.6 = (f32[8,4,64,256]{3,2,1,0:T(8,128)S(1)}, f32[8,4,64,256]{3,2,1,0:T(8,128)}, u32[]{:S(2)}, u32[]{:S(2)}) collective-permute-start(f32[8,4,64,256]{3,2,1,0:T(8,128)S(1)} %all-to-all-done.1), channel_id=1, source_target_pairs={{0,8},{8,0},{16,24},{24,16},{32,40},{40,32},{48,56},{56,48},{64,72... | collective-permute-start | bytes 6291464 | tf_op jit(solution)/shard_map/ppermute | solution.py:243
  70.3 3.3 %all-to-all-done.2.carry = f32[8,4,8,128]{3,2,1,0:T(8,128)S(1)} async-done(((f32[8,4,8,128]{3,2,1,0:T(8,128)}), f32[8,4,8,128]{3,2,1,0:T(8,128)S(1)}, u32[]{:S(2)}, u32[]{:S(2)}) %all-to-all-start.2) | async-done | bytes 131104 | tf_op jit(solution)/shard_map/all_to_all | solution.py:229
  73.5 0.0 copy-start.2
  73.5 1.1 copy-done.2
  74.7 0.1 shard_map.50
  74.8 17.5 %all_to_all.30 = f32[8,2,64,256]{3,2,1,0:T(8,128)S(1)} all-to-all(f32[8,2,64,256]{3,2,1,0:T(8,128)S(1)} %shard_map.50), channel_id=1, replica_groups=mesh['depth'=64,'row'=8] {'row'}, dimensions={0} | all-to-all | bytes 2097152 | tf_op jit(solution)/shard_map/all_to_all | solution.py:255
  92.3 5.4 %collective-permute-start.5 = (f32[8,2,64,256]{3,2,1,0:T(8,128)S(1)}, f32[8,2,64,256]{3,2,1,0:T(8,128)S(1)}, u32[]{:S(2)}, u32[]{:S(2)}) collective-permute-start(f32[8,2,64,256]{3,2,1,0:T(8,128)S(1)} %all_to_all.30), channel_id=1, source_target_pairs={{0,8},{8,0},{16,24},{24,16},{32,40},{40,32},{48,56},{56,48},{64,72... | collective-permute-start | bytes 3145736 | tf_op jit(solution)/shard_map/ppermute | solution.py:256
  97.7 0.0 collective-permute-done.6
  97.7 2.1 %shard_map.51.mid = bf16[3,2,512,512]{3,2,1,0:T(8,128)(2,1)S(1)} custom-call(s32[1]{0:T(128)} %bitcast.core, f32[8,4,4,2,8,256]{5,4,3,2,1,0:T(8,128)S(1)} %bitcast.13, f32[8,4,4,2,8,256]{5,4,3,2,1,0:T(8,128)} %bitcast.9.far), custom_call_target="tpu_custom_call" | custom-call | bytes 10485764 | tf_op jit(solution)/shard_map/pallas_call | solution.py:23
  99.8 0.2 collective-permute-done.5
  100.0 4.6 %shard_map.52 = f32[8,2,64,256]{3,2,1,0:T(8,128)S(1)} custom-call(s32[1]{0:T(128)} %bitcast.core, f32[8,2,4,2,8,256]{5,4,3,2,1,0:T(8,128)S(1)} %bitcast.16, f32[8,2,4,2,8,256]{5,4,3,2,1,0:T(8,128)S(1)} %bitcast.17, f32[8,4,4,2,8,256]{5,4,3,2,1,0:T(8,128)S(1)} %bitcast.14, bf16[3,2,512,512]{3,2,1,0:T(8,128)(2,1)S(1)} %shard_map.51.mid), custom_call_target="tpu_custom_call" | custom-call | flops 3623878656 | bytes 11534340 | tf_op jit(solution)/shard_map/pallas_call | solution.py:23
  104.6 19.8 %all_to_all.31.parts = f32[8,2,64,256]{3,2,1,0:T(8,128)S(1)} all-to-all(f32[8,2,64,256]{3,2,1,0:T(8,128)S(1)} %shard_map.52), channel_id=1, replica_groups=mesh['depth'=64,'row'=8] {'row'}, dimensions={0} | all-to-all | bytes 2097152 | tf_op jit(solution)/shard_map/all_to_all | solution.py:266
  124.4 0.1 shard_map.53
  124.5 24.7 %all_to_all.32.parts = f32[32,8,128]{2,1,0:T(8,128)S(1)} all-to-all(f32[32,8,128]{2,1,0:T(8,128)S(1)} %shard_map.53), channel_id=1, replica_groups={{0,16,32,48,64,80,96,112,128,144,160,176,192,208,224,240,256,272,288,30..., dimensions={0} | all-to-all | bytes 262144 | tf_op jit(solution)/shard_map/all_to_all | solution.py:229
  149.2 0.1 shard_map.54
  149.3 0.7 copy.14
  (5 shorter events, 0.0 us)
Async XLA Ops:
  0.0 1.1 copy-start
  0.0 10.9 %copy-start.3 = (f32[512]{0:T(512)S(1)}, f32[512]{0:T(512)}, u32[]{:S(2)}) copy-start(f32[512]{0:T(512)} %param.5) | copy-start | bytes 6148
  1.1 18.7 %copy-start.4 = (s32[512]{0:T(512)S(1)}, s32[512]{0:T(512)}, u32[]{:S(2)}) copy-start(s32[512]{0:T(512)} %param.7) | copy-start | bytes 6148
  1.1 19.0 %copy-start.5 = (s32[64]{0:T(128)S(1)}, s32[64]{0:T(128)}, u32[]{:S(2)}) copy-start(s32[64]{0:T(128)} %param.6) | copy-start | bytes 772
  2.1 10.1 %collective-permute-start = (f32[2,3,64,256]{3,2,1,0:T(8,128)S(1)}, f32[2,3,64,256]{3,2,1,0:T(8,128)S(1)}, u32[]{:S(2)}, u32[]{:S(2)}) collective-permute-start(f32[2,3,64,256]{3,2,1,0:T(8,128)S(1)} %bitcast.18), channel_id=1, source_target_pairs={{0,8},{8,0},{16,24},{24,16},{32,40},{40,32},{48,56},{56,48},{64,72... | collective-permute-start | bytes 1179656 | tf_op jit(solution)/shard_map/ppermute | solution.py:204
  13.2 14.0 %copy-start.1 = (f32[2,6,64,256]{3,2,1,0:T(8,128)}, f32[2,6,64,256]{3,2,1,0:T(8,128)S(1)}, u32[]{:S(2)}) copy-start(f32[2,6,64,256]{3,2,1,0:T(8,128)S(1)} %get-tuple-element.17.down) | copy-start | bytes 2359300
  13.2 14.0 %all-to-all-start = ((f32[8,4,8,128]{3,2,1,0:T(8,128)}), f32[8,4,8,128]{3,2,1,0:T(8,128)S(1)}, u32[]{:S(2)}, u32[]{:S(2)}) async-start(f32[8,4,8,128]{3,2,1,0:T(8,128)} %get-tuple-element.15), calls=%async_computation | async-start | bytes 262144 | tf_op jit(solution)/shard_map/all_to_all | solution.py:229
  16.5 9.2 %collective-permute-start.1 = (f32[2,2,64,256]{3,2,1,0:T(8,128)S(1)}, f32[2,2,64,256]{3,2,1,0:T(8,128)S(1)}, u32[]{:S(2)}, u32[]{:S(2)}) collective-permute-start(f32[2,2,64,256]{3,2,1,0:T(8,128)S(1)} %get-tuple-element.19), channel_id=1, source_target_pairs={{0,16},{8,24},{16,32},{24,40},{32,48},{40,56},{48,64},{56,72},{64,... | collective-permute-start | bytes 786440 | tf_op jit(solution)/shard_map/ppermute | solution.py:237
  27.2 32.6 %all-to-all-start.1 = ((f32[8,4,64,256]{3,2,1,0:T(8,128)}), f32[8,4,64,256]{3,2,1,0:T(8,128)S(1)}, u32[]{:S(2)}, u32[]{:S(2)}) async-start(f32[8,4,64,256]{3,2,1,0:T(8,128)} %shard_map.48), calls=%async_computation.1 | async-start | bytes 4194304 | tf_op jit(solution)/shard_map/all_to_all | solution.py:240
  31.2 12.5 %collective-permute-start.2 = (f32[4,8,128]{2,1,0:T(8,128)S(1)}, f32[4,8,128]{2,1,0:T(8,128)S(1)}, u32[]{:S(2)}, u32[]{:S(2)}) collective-permute-start(f32[4,8,128]{2,1,0:T(8,128)S(1)} %get-tuple-element.20), channel_id=1, source_target_pairs={{128,0},{136,8},{144,16},{152,24},{160,32},{168,40},{176,48},{184,... | collective-permute-start | bytes 49160 | tf_op jit(solution)/shard_map/ppermute | solution.py:233
  32.5 17.4 %collective-permute-start.3 = (f32[4,8,128]{2,1,0:T(8,128)S(1)}, f32[4,8,128]{2,1,0:T(8,128)S(1)}, u32[]{:S(2)}, u32[]{:S(2)}) collective-permute-start(f32[4,8,128]{2,1,0:T(8,128)S(1)} %get-tuple-element.20), channel_id=1, source_target_pairs={{256,0},{264,8},{272,16},{280,24},{288,32},{296,40},{304,48},{312,... | collective-permute-start | bytes 49160 | tf_op jit(solution)/shard_map/ppermute | solution.py:233
  33.8 18.3 %collective-permute-start.4 = (f32[4,8,128]{2,1,0:T(8,128)S(1)}, f32[4,8,128]{2,1,0:T(8,128)S(1)}, u32[]{:S(2)}, u32[]{:S(2)}) collective-permute-start(f32[4,8,128]{2,1,0:T(8,128)S(1)} %get-tuple-element.20), channel_id=1, source_target_pairs={{384,0},{392,8},{400,16},{408,24},{416,32},{424,40},{432,48},{440,... | collective-permute-start | bytes 49160 | tf_op jit(solution)/shard_map/ppermute | solution.py:233
  60.4 13.1 %all-to-all-start.2 = ((f32[8,4,8,128]{3,2,1,0:T(8,128)}), f32[8,4,8,128]{3,2,1,0:T(8,128)S(1)}, u32[]{:S(2)}, u32[]{:S(2)}) async-start(f32[8,4,8,128]{3,2,1,0:T(8,128)} %shard_map.49), calls=%async_computation.2 | async-start | bytes 262144 | tf_op jit(solution)/shard_map/all_to_all | solution.py:229
  67.2 30.5 %collective-permute-start.6 = (f32[8,4,64,256]{3,2,1,0:T(8,128)S(1)}, f32[8,4,64,256]{3,2,1,0:T(8,128)}, u32[]{:S(2)}, u32[]{:S(2)}) collective-permute-start(f32[8,4,64,256]{3,2,1,0:T(8,128)S(1)} %all-to-all-done.1), channel_id=1, source_target_pairs={{0,8},{8,0},{16,24},{24,16},{32,40},{40,32},{48,56},{56,48},{64,72... | collective-permute-start | bytes 6291464 | tf_op jit(solution)/shard_map/ppermute | solution.py:243
  73.5 1.1 copy-start.2
  92.3 7.7 %collective-permute-start.5 = (f32[8,2,64,256]{3,2,1,0:T(8,128)S(1)}, f32[8,2,64,256]{3,2,1,0:T(8,128)S(1)}, u32[]{:S(2)}, u32[]{:S(2)}) collective-permute-start(f32[8,2,64,256]{3,2,1,0:T(8,128)S(1)} %all_to_all.30), channel_id=1, source_target_pairs={{0,8},{8,0},{16,24},{24,16},{32,40},{40,32},{48,56},{56,48},{64,72... | collective-permute-start | bytes 3145736 | tf_op jit(solution)/shard_map/ppermute | solution.py:256

commit v3 on v2

--- a/solution.py
+++ b/solution.py
@@ -11,11 +11,12 @@
 NEAR = 8
 VMEM = pl.BlockSpec(memory_space=pltpu.VMEM)
 SMEM = pl.BlockSpec(memory_space=pltpu.SMEM)
+HBM = pl.BlockSpec(memory_space=pltpu.HBM)
 MIB = 1024 * 1024
 f32 = jnp.float32
 
 
-def call(kernel, out_shape, *args, scratch=(), smem=(), flops=0, room=6):
+def call(kernel, out_shape, *args, scratch=(), smem=(), hbm=(), flops=0, room=6):
     single = not isinstance(out_shape, list)
     shapes = [out_shape] if single else out_shape
     shapes = [s if hasattr(s, "dtype") else jax.ShapeDtypeStruct(s, f32) for s in shapes]
@@ -23,12 +24,18 @@
     return pl.pallas_call(
         kernel,
         out_shape=shapes[0] if single else shapes,
-        in_specs=[SMEM if i in smem else VMEM for i in range(len(args))],
+        in_specs=[SMEM if i in smem else HBM if i in hbm else VMEM for i in range(len(args))],
         out_specs=VMEM if single else [VMEM] * len(shapes),
         scratch_shapes=list(scratch),
         compiler_params=pltpu.CompilerParams(vmem_limit_bytes=room * MIB),
         cost_estimate=pl.CostEstimate(flops=flops, bytes_accessed=moved, transcendentals=0),
     )(*args)
+
+
+def turned(row_trig, col_trig, level):
+    row_cos, row_sin = row_trig[:, level : level + 1], row_trig[:, 8 + level : 9 + level]
+    col_cos, col_sin = col_trig[level : level + 1, :], col_trig[8 + level : 9 + level, :]
+    return row_cos * col_cos - row_sin * col_sin, row_sin * col_cos + row_cos * col_sin
 
 
 def phase_kernel(core, kept, taken, row_trig, col_trig, down, up, rim, total):
@@ -43,10 +50,7 @@
             else jnp.where(first_core, taken[part, local], kept[part, local])
         )
         re, im = pick(0), pick(1)
-        row_cos, row_sin = row_trig[:, slab : slab + 1], row_trig[:, 8 + slab : 9 + slab]
-        col_cos, col_sin = col_trig[slab : slab + 1, :], col_trig[8 + slab : 9 + slab, :]
-        cosine = row_cos * col_cos - row_sin * col_sin
-        sine = row_sin * col_cos + row_cos * col_sin
+        cosine, sine = turned(row_trig, col_trig, slab)
         a, b, c, d = re * cosine, im * sine, re * sine, im * cosine
         sums = (a - b, c + d)
         rises = (a + b, d - c)
@@ -64,16 +68,6 @@
                 total[(8 * part + block) // 2, 2 * (block % 2) + lane] = tile
 
 
-def early_kernel(down, up, rim, eps_r, eps_c, out):
-    gap = (eps_c[...] == 1).astype(f32) - (eps_r[...] == 1).astype(f32)
-    for slab in range(SLABS):
-        for part in range(2):
-            out[slab, part] = rim[part, slab] if slab < EPS_MOST else up[part, slab - EPS_MOST]
-            out[slab, 2 + part] = down[part, slab] * gap
-    for idle in range(SLABS, out.shape[0]):
-        out[idle] = jnp.zeros(out.shape[1:], f32)
-
-
 def group_kernel(parts, out, total):
     state = parts[parts.shape[0] - 1]
     out[parts.shape[0] - 1] = jnp.zeros(parts.shape[1:], f32)
@@ -92,17 +86,21 @@
         out[place] = sums[place] + extra
 
 
-def late_kernel(carry, down, eps_r, out):
+def late_kernel(carry, down, up, rim, eps_r, eps_c, out):
     near_row = eps_r[...] == 1
     for part in range(2):
+        for slab in range(SLABS):
+            out[slab, 2 + part] = rim[part, slab] if slab < EPS_MOST else up[part, slab - EPS_MOST]
         for block in range(8):
             rows = slice(8 * block, 8 * block + 8)
             for lane in range(2):
                 cols = slice(128 * lane, 128 * lane + 128)
+                near_col = eps_c[:, cols] == 1
                 below = carry[(8 * part + block) // 2, 2 * (block % 2) + lane]
                 for slab in range(SLABS - 1, -1, -1):
                     here = below + down[part, slab, rows, cols]
                     out[slab, part, rows, cols] = jnp.where(near_row[rows], here, below)
+                    out[slab, 4 + part, rows, cols] = jnp.where(near_col, here, below)
                     below = here
     for idle in range(SLABS, out.shape[0]):
         out[idle] = jnp.zeros(out.shape[1:], f32)
@@ -129,36 +127,43 @@
     return split(re), split(im), split(re + im)
 
 
-def ready_kernel(core, own, far, mid):
-    half = own.shape[-1]
-    for block in range(2):
-        parity = core[0] if block == 0 else 1 - core[0]
+def right_kernel(core, whole, right):
+    half = right.shape[-1]
+    for block, parity in enumerate((core[0], 1 - core[0])):
         stretch = slice(block * half, block * half + half)
-        for column, ref in enumerate((own, far)):
-            both = triple(*(ref[:, part, :, parity].reshape(half, half) for part in range(2)))
+        both = triple(*(whole[:, 4 + part, :, parity].reshape(half, half) for part in range(2)))
+        for kind in range(3):
+            for level in range(2):
+                right[kind, level, stretch, :] = both[kind][level]
+
+
+def first_kernel(core, own, far, right, out):
+    half = out.shape[-1]
+    second = [(right[kind, 0], right[kind, 1]) for kind in range(3)]
+    step = half // 2
+    for block, parity in enumerate((core[0], 1 - core[0])):
+        for start in range(0, 2):
+            pieces = slice(4 * start, 4 * start + 4)
+            rises = [
+                jnp.concatenate([ref[pieces, 2 + part, :, parity].reshape(step, half) for ref in (own, far)], axis=1)
+                for part in range(2)
+            ]
+            both = triple(*complex_dot(triple(*rises), second))
+            rows = slice(block * half + start * step, block * half + start * step + step)
             for kind in range(3):
                 for level in range(2):
-                    mid[kind, level, stretch, column * half : (column + 1) * half] = both[kind][level]
-
-
-def product_kernel(core, own, far, early, mid, out, last):
+                    out[kind, level, rows] = both[kind][level]
+
+
+def second_kernel(own, far, middle, out):
     half = out.shape[-1]
     chips, rows = out.shape[0], out.shape[2]
-    for block in range(2):
-        parity = core[0] if block == 0 else 1 - core[0]
-        stretch = slice(block * half, block * half + half)
-        both = triple(*((own[:, part, :, parity] + early[:, 2 + part, :, parity]).reshape(half, half) for part in range(2)))
-        for kind in range(3):
-            for level in range(2):
-                last[kind, level, stretch, :] = both[kind][level]
-    second = [(mid[kind, 0], mid[kind, 1]) for kind in range(3)]
-    third = [(last[kind, 0], last[kind, 1]) for kind in range(3)]
+    second = [(middle[kind, 0], middle[kind, 1]) for kind in range(3)]
     step = 2
     for start in range(0, chips, step):
         pieces = slice(start, start + step)
         left = [jnp.concatenate([ref[pieces, part].reshape(step * rows, half) for ref in (own, far)], axis=1) for part in range(2)]
-        middle = complex_dot(triple(*left), second)
-        result = complex_dot(triple(*middle), third)
+        result = complex_dot(triple(*left), second)
         for part in range(2):
             out[pieces, part] = result[part].reshape(step, rows, half)
 
@@ -233,35 +238,34 @@
         lax.ppermute(group, "depth", [(i, i - shift) for i in range(shift, deep)])
         for shift in range(2 * NEAR, deep, 2 * NEAR)
     ]
-
     rim = lax.ppermute(rim, "depth", [(i, i + 2) for i in range(deep - 2)])
-    row_marks = eps_rows.reshape(row_count, 1)
-    early = call(early_kernel, (chips, 4, row_count, half), down, up, rim, row_marks, near_cols)
-    early = lax.all_to_all(early, "row", 0, 0, tiled=True)
-    early, *deeper = lax.optimization_barrier((early, *deeper))
+    rim, *deeper = lax.optimization_barrier((rim, *deeper))
     carry = spread(call(deep_kernel, sums.shape, sums, *deeper), near)
-    early_far = lax.ppermute(early, "depth", swap)
+
+    late = call(
+        late_kernel,
+        (chips, 6, row_count, half),
+        carry, down, up, rim, eps_rows.reshape(row_count, 1), near_cols,
+    )
+    whole = lax.all_to_all(late, "row", 0, 0, tiled=True)
+    other = lax.ppermute(whole[:, :4], "depth", swap)
     shape = lambda v: v.reshape(chips, v.shape[1], row_count // 16, 2, 8, half)
-    mid = call(
-        ready_kernel,
-        jax.ShapeDtypeStruct((3, 2, width, width), jnp.bfloat16),
-        me, shape(early), shape(early_far),
+    parts = lambda n: jax.ShapeDtypeStruct((3, 2, width, n), jnp.bfloat16)
+    right = call(right_kernel, parts(half), me, shape(whole), smem=(0,), room=8)
+    middle = call(
+        first_kernel,
+        parts(half),
+        me, shape(whole), shape(other), right,
         smem=(0,),
+        flops=18 * width * width * half,
         room=12,
     )
-
-    whole = (chips, 2, row_count, half)
-    late = call(late_kernel, whole, carry, down, row_marks)
-    left = lax.all_to_all(late, "row", 0, 0, tiled=True)
-    left_far = lax.ppermute(left, "depth", swap)
     partial = call(
-        product_kernel,
-        whole,
-        me, shape(left), shape(left_far), shape(early), mid,
-        smem=(0,),
-        scratch=[pltpu.VMEM((3, 2, width, half), jnp.bfloat16)],
-        flops=18 * width * width * (width + half),
-        room=20,
+        second_kernel,
+        (chips, 2, row_count, half),
+        whole, other, middle,
+        flops=18 * width * width * half,
+        room=12,
     )
     gathered = lax.all_to_all(partial, "row", 0, 0, tiled=True)
     turned = call(

time: 152 us -> 148 us (0.974)
  blocking collectives: 62 us -> 80.2 us
  starting transfers between devices: 38.6 us -> 29.7 us
  waiting for transfers between devices: 34.1 us -> 25.9 us
  Pallas kernels: 10.2 us -> 5.4 us
    all_to_all x1, blocking collectives: 17.5 us -> 41.2 us  [body(): whole = lax.all_to_all(late, 'row', 0, 0, tiled=True)]
    all_to_all x1 -> x0, waiting for transfers between devices: 7.63 us -> none  [body(): early = lax.all_to_all(early, 'row', 0, 0, tiled=True)]
    ppermute x1, waiting for transfers between devices: 5.5 us -> 0.01 us  [body(): rim = lax.ppermute(rim, 'depth', [(i, i + 2) for i in range(deep - 2)])]
    all_to_all x2, waiting for transfers between devices: 3.26 us -> 8.75 us  [body(): lax.all_to_all(v, 'depth', 0, 0, axis_index_groups=groups, tiled=True)]
    all_to_all x1, blocking collectives: 24.7 us -> 19.3 us  [body(): lax.all_to_all(v, 'depth', 0, 0, axis_index_groups=groups, tiled=True)]
    pallas_call x9, Pallas kernels: 10.2 us -> 5.4 us  [call(): pl.pallas_call(kernel, out_shape=shapes[0] if single else shapes, in_spec...]
    all_to_all x1 -> x0, starting transfers between devices: 4.03 us -> none  [body(): early = lax.all_to_all(early, 'row', 0, 0, tiled=True)]
    ppermute x3, waiting for transfers between devices: 17 us -> 13 us  [body(): lax.ppermute(group, 'depth', [(i, i - shift) for i in range(shift, deep)])]
  transfers between devices with their start and end apart: 10 -> 8, of which waited for: 8 -> 7; matrix products, arithmetic and copies ran while one was open for 1% -> 1% of each run, Pallas kernels for 2% -> 0%
where the time goes in v3:
time: 148 us; the launch traced here: 145 us
  blocking collectives  80.2 us (54%)
  starting transfers between devices  29.7 us (20%)
  waiting for transfers between devices  25.9 us (18%)
  Pallas kernels  5.4 us (4%)
  local copies, waits for them, and re-layouts  2.82 us (2%)
    all_to_all x1, blocking collectives, body(): whole = lax.all_to_all(late, 'row', 0, 0, tiled=True)  41.2 us
    all_to_all x1, blocking collectives, body(): gathered = lax.all_to_all(partial, 'row', 0, 0, tiled=True)  19.8 us
    all_to_all x1, blocking collectives, body(): lax.all_to_all(v, 'depth', 0, 0, axis_index_groups=groups, tiled=True)  19.3 us
    ppermute x3, waiting for transfers between devices, body(): lax.ppermute(group, 'depth', [(i, i - shift) for i in range(shift, deep)])  13 us
    ppermute x1, starting transfers between devices, body(): taken = lax.ppermute(given, 'depth', swap)  8.79 us
    all_to_all x2, waiting for transfers between devices, body(): lax.all_to_all(v, 'depth', 0, 0, axis_index_groups=groups, tiled=True)  8.75 us
    ppermute x1, starting transfers between devices, body(): other = lax.ppermute(whole[:, :4], 'depth', swap)  7.02 us
    all_to_all x2, starting transfers between devices, body(): lax.all_to_all(v, 'depth', 0, 0, axis_index_groups=groups, tiled=True)  6.74 us
  transfers between devices with their start and end apart: 8, of which 7 were waited for; matrix products, arithmetic and copies ran while one was open for 1% of the time, Pallas kernels for 0%

profile of v3, /device:TPU:1, one launch (start us, length us, event | category | flops | bytes accessed | tf_op | source)
XLA Modules:
  0.0 145.4 jit_solution(9527359087627246233)
XLA Ops:
  0.0 0.0 copy-start
  0.0 0.0 copy-start.1
  0.0 1.1 copy-done
  1.1 0.9 convolution_bitcast_fusion
  2.0 0.0 copy-start.2
  2.0 0.0 copy-start.3
  2.0 0.1 fusion.13
  2.1 8.8 %collective-permute-start = (f32[2,3,64,256]{3,2,1,0:T(8,128)S(1)}, f32[2,3,64,256]{3,2,1,0:T(8,128)S(1)}, u32[]{:S(2)}, u32[]{:S(2)}) collective-permute-start(f32[2,3,64,256]{3,2,1,0:T(8,128)S(1)} %bitcast.15), channel_id=1, source_target_pairs={{0,8},{8,0},{16,24},{24,16},{32,40},{40,32},{48,56},{56,48},{64,72... | collective-permute-start | bytes 1179656 | tf_op jit(solution)/shard_map/ppermute | solution.py:209
  10.9 0.0 copy-done.1
  10.9 0.1 dynamic_slice.11
  11.0 0.1 multiply_cosine_fusion.1
  11.1 0.1 reshape.86
  11.2 0.1 dynamic-slice_reduce_fusion.1
  11.3 0.1 mul.61
  11.4 0.1 copy.9.row_trig
  11.5 0.1 multiply_cosine_fusion
  11.6 0.6 collective-permute-done.taken
  12.2 1.0 shard_map.46
  13.2 3.4 %all-to-all-start = ((f32[8,4,8,128]{3,2,1,0:T(8,128)}), f32[8,4,8,128]{3,2,1,0:T(8,128)S(1)}, u32[]{:S(2)}, u32[]{:S(2)}) async-start(f32[8,4,8,128]{3,2,1,0:T(8,128)} %get-tuple-element.15), calls=%async_computation | async-start | bytes 262144 | tf_op jit(solution)/shard_map/all_to_all | solution.py:234
  16.6 3.3 %collective-permute-start.1 = (f32[2,2,64,256]{3,2,1,0:T(8,128)S(1)}, f32[2,2,64,256]{3,2,1,0:T(8,128)S(1)}, u32[]{:S(2)}, u32[]{:S(2)}) collective-permute-start(f32[2,2,64,256]{3,2,1,0:T(8,128)S(1)} %get-tuple-element.17), channel_id=1, source_target_pairs={{0,16},{8,24},{16,32},{24,40},{32,48},{40,56},{48,64},{56,72},{64,... | collective-permute-start | bytes 786440 | tf_op jit(solution)/shard_map/ppermute | solution.py:241
  19.8 2.9 %all-to-all-done.parts = f32[8,4,8,128]{3,2,1,0:T(8,128)S(1)} async-done(((f32[8,4,8,128]{3,2,1,0:T(8,128)}), f32[8,4,8,128]{3,2,1,0:T(8,128)S(1)}, u32[]{:S(2)}, u32[]{:S(2)}) %all-to-all-start) | async-done | bytes 131104 | tf_op jit(solution)/shard_map/all_to_all | solution.py:234
  22.8 1.3 collective-permute-start.2
  24.1 1.3 collective-permute-start.3
  25.4 1.3 collective-permute-start.4
  26.7 0.0 collective-permute-done.1.rim
  26.7 4.5 %collective-permute-done.2.refs_0_ = f32[4,8,128]{2,1,0:T(8,128)S(1)} collective-permute-done((f32[4,8,128]{2,1,0:T(8,128)S(1)}, f32[4,8,128]{2,1,0:T(8,128)S(1)}, u32[]{:S(2)}, u32[]{:S(2)}) %collective-permute-start.2) | collective-permute-done | bytes 16416 | tf_op jit(solution)/shard_map/ppermute | solution.py:238
  31.2 6.1 %collective-permute-done.3.refs_1_ = f32[4,8,128]{2,1,0:T(8,128)S(1)} collective-permute-done((f32[4,8,128]{2,1,0:T(8,128)S(1)}, f32[4,8,128]{2,1,0:T(8,128)S(1)}, u32[]{:S(2)}, u32[]{:S(2)}) %collective-permute-start.3) | collective-permute-done | bytes 16416 | tf_op jit(solution)/shard_map/ppermute | solution.py:238
  37.3 2.4 %collective-permute-done.4.refs_2_ = f32[4,8,128]{2,1,0:T(8,128)S(1)} collective-permute-done((f32[4,8,128]{2,1,0:T(8,128)S(1)}, f32[4,8,128]{2,1,0:T(8,128)S(1)}, u32[]{:S(2)}, u32[]{:S(2)}) %collective-permute-start.4) | collective-permute-done | bytes 16416 | tf_op jit(solution)/shard_map/ppermute | solution.py:238
  39.7 0.7 shard_map.48
  40.4 3.4 %all-to-all-start.1 = ((f32[8,4,8,128]{3,2,1,0:T(8,128)}), f32[8,4,8,128]{3,2,1,0:T(8,128)S(1)}, u32[]{:S(2)}, u32[]{:S(2)}) async-start(f32[8,4,8,128]{3,2,1,0:T(8,128)} %shard_map.48), calls=%async_computation.1 | async-start | bytes 262144 | tf_op jit(solution)/shard_map/all_to_all | solution.py:234
  43.7 0.0 copy-done.2
  43.8 0.1 reshape.88
  43.9 0.1 dynamic-slice_reduce_fusion
  43.9 0.1 reshape_reshape.3.eps_c
  44.0 0.0 copy-done.3
  44.0 0.1 copy.10.eps_r
  44.1 5.8 %all-to-all-done.1.carry = f32[8,4,8,128]{3,2,1,0:T(8,128)S(1)} async-done(((f32[8,4,8,128]{3,2,1,0:T(8,128)}), f32[8,4,8,128]{3,2,1,0:T(8,128)S(1)}, u32[]{:S(2)}, u32[]{:S(2)}) %all-to-all-start.1) | async-done | bytes 131104 | tf_op jit(solution)/shard_map/all_to_all | solution.py:234
  49.9 0.2 shard_map.49
  50.2 41.2 %all_to_all.25.own = f32[8,6,64,256]{3,2,1,0:T(8,128)S(1)} all-to-all(f32[8,6,64,256]{3,2,1,0:T(8,128)S(1)} %shard_map.49), channel_id=1, replica_groups=mesh['depth'=64,'row'=8] {'row'}, dimensions={0} | all-to-all | bytes 6291456 | tf_op jit(solution)/shard_map/all_to_all | solution.py:250
  91.4 0.2 slice.14
  91.6 7.0 %collective-permute-start.5 = (f32[8,4,64,256]{3,2,1,0:T(8,128)S(1)}, f32[8,4,64,256]{3,2,1,0:T(8,128)S(1)}, u32[]{:S(2)}, u32[]{:S(2)}) collective-permute-start(f32[8,4,64,256]{3,2,1,0:T(8,128)S(1)} %slice.14), channel_id=1, source_target_pairs={{0,8},{8,0},{16,24},{24,16},{32,40},{40,32},{48,56},{56,48},{64,72... | collective-permute-start | bytes 6291464 | tf_op jit(solution)/shard_map/ppermute | solution.py:251
  98.6 0.3 shard_map.50.right
  98.9 3.5 %collective-permute-done.5.far = f32[8,4,64,256]{3,2,1,0:T(8,128)S(1)} collective-permute-done((f32[8,4,64,256]{3,2,1,0:T(8,128)S(1)}, f32[8,4,64,256]{3,2,1,0:T(8,128)S(1)}, u32[]{:S(2)}, u32[]{:S(2)}) %collective-permute-start.5) | collective-permute-done | bytes 2097184 | tf_op jit(solution)/shard_map/ppermute | solution.py:251
  102.4 1.6 %shard_map.51.middle = bf16[3,2,512,256]{3,2,1,0:T(8,128)(2,1)S(1)} custom-call(s32[1]{0:T(128)} %bitcast.core, f32[8,6,4,2,8,256]{5,4,3,2,1,0:T(8,128)S(1)} %bitcast.12, f32[8,4,4,2,8,256]{5,4,3,2,1,0:T(8,128)S(1)} %bitcast.13, bf16[3,2,512,256]{3,2,1,0:T(8,128)(2,1)S(1)} %shard_map.50.right), custom_call_target="tpu_custom_call" | custom-call | flops 1207959552 | bytes 11534340 | tf_op jit(solution)/shard_map/pallas_call | solution.py:24
  104.0 1.4 shard_map.52
  105.4 19.8 %all_to_all.26.parts = f32[8,2,64,256]{3,2,1,0:T(8,128)S(1)} all-to-all(f32[8,2,64,256]{3,2,1,0:T(8,128)S(1)} %shard_map.52), channel_id=1, replica_groups=mesh['depth'=64,'row'=8] {'row'}, dimensions={0} | all-to-all | bytes 2097152 | tf_op jit(solution)/shard_map/all_to_all | solution.py:270
  125.2 0.1 shard_map.53
  125.3 19.3 %all_to_all.27.parts = f32[32,8,128]{2,1,0:T(8,128)S(1)} all-to-all(f32[32,8,128]{2,1,0:T(8,128)S(1)} %shard_map.53), channel_id=1, replica_groups={{0,16,32,48,64,80,96,112,128,144,160,176,192,208,224,240,256,272,288,30..., dimensions={0} | all-to-all | bytes 262144 | tf_op jit(solution)/shard_map/all_to_all | solution.py:234
  144.6 0.1 shard_map.54
  144.7 0.7 copy.11
  (5 shorter events, 0.0 us)
Async XLA Ops:
  0.0 1.1 copy-start
  0.0 10.9 %copy-start.1 = (f32[512]{0:T(512)S(1)}, f32[512]{0:T(512)}, u32[]{:S(2)}) copy-start(f32[512]{0:T(512)} %param.5) | copy-start | bytes 6148
  2.0 41.8 %copy-start.2 = (s32[512]{0:T(512)S(1)}, s32[512]{0:T(512)}, u32[]{:S(2)}) copy-start(s32[512]{0:T(512)} %param.7) | copy-start | bytes 6148
  2.0 42.0 %copy-start.3 = (s32[64]{0:T(128)S(1)}, s32[64]{0:T(128)}, u32[]{:S(2)}) copy-start(s32[64]{0:T(128)} %param.6) | copy-start | bytes 772
  2.1 10.1 %collective-permute-start = (f32[2,3,64,256]{3,2,1,0:T(8,128)S(1)}, f32[2,3,64,256]{3,2,1,0:T(8,128)S(1)}, u32[]{:S(2)}, u32[]{:S(2)}) collective-permute-start(f32[2,3,64,256]{3,2,1,0:T(8,128)S(1)} %bitcast.15), channel_id=1, source_target_pairs={{0,8},{8,0},{16,24},{24,16},{32,40},{40,32},{48,56},{56,48},{64,72... | collective-permute-start | bytes 1179656 | tf_op jit(solution)/shard_map/ppermute | solution.py:209
  13.2 9.6 %all-to-all-start = ((f32[8,4,8,128]{3,2,1,0:T(8,128)}), f32[8,4,8,128]{3,2,1,0:T(8,128)S(1)}, u32[]{:S(2)}, u32[]{:S(2)}) async-start(f32[8,4,8,128]{3,2,1,0:T(8,128)} %get-tuple-element.15), calls=%async_computation | async-start | bytes 262144 | tf_op jit(solution)/shard_map/all_to_all | solution.py:234
  16.6 10.1 %collective-permute-start.1 = (f32[2,2,64,256]{3,2,1,0:T(8,128)S(1)}, f32[2,2,64,256]{3,2,1,0:T(8,128)S(1)}, u32[]{:S(2)}, u32[]{:S(2)}) collective-permute-start(f32[2,2,64,256]{3,2,1,0:T(8,128)S(1)} %get-tuple-element.17), channel_id=1, source_target_pairs={{0,16},{8,24},{16,32},{24,40},{32,48},{40,56},{48,64},{56,72},{64,... | collective-permute-start | bytes 786440 | tf_op jit(solution)/shard_map/ppermute | solution.py:241
  22.8 8.4 %collective-permute-start.2 = (f32[4,8,128]{2,1,0:T(8,128)S(1)}, f32[4,8,128]{2,1,0:T(8,128)S(1)}, u32[]{:S(2)}, u32[]{:S(2)}) collective-permute-start(f32[4,8,128]{2,1,0:T(8,128)S(1)} %get-tuple-element.18), channel_id=1, source_target_pairs={{128,0},{136,8},{144,16},{152,24},{160,32},{168,40},{176,48},{184,... | collective-permute-start | bytes 49160 | tf_op jit(solution)/shard_map/ppermute | solution.py:238
  24.1 13.2 %collective-permute-start.3 = (f32[4,8,128]{2,1,0:T(8,128)S(1)}, f32[4,8,128]{2,1,0:T(8,128)S(1)}, u32[]{:S(2)}, u32[]{:S(2)}) collective-permute-start(f32[4,8,128]{2,1,0:T(8,128)S(1)} %get-tuple-element.18), channel_id=1, source_target_pairs={{256,0},{264,8},{272,16},{280,24},{288,32},{296,40},{304,48},{312,... | collective-permute-start | bytes 49160 | tf_op jit(solution)/shard_map/ppermute | solution.py:238
  25.4 14.3 %collective-permute-start.4 = (f32[4,8,128]{2,1,0:T(8,128)S(1)}, f32[4,8,128]{2,1,0:T(8,128)S(1)}, u32[]{:S(2)}, u32[]{:S(2)}) collective-permute-start(f32[4,8,128]{2,1,0:T(8,128)S(1)} %get-tuple-element.18), channel_id=1, source_target_pairs={{384,0},{392,8},{400,16},{408,24},{416,32},{424,40},{432,48},{440,... | collective-permute-start | bytes 49160 | tf_op jit(solution)/shard_map/ppermute | solution.py:238
  40.4 9.6 %all-to-all-start.1 = ((f32[8,4,8,128]{3,2,1,0:T(8,128)}), f32[8,4,8,128]{3,2,1,0:T(8,128)S(1)}, u32[]{:S(2)}, u32[]{:S(2)}) async-start(f32[8,4,8,128]{3,2,1,0:T(8,128)} %shard_map.48), calls=%async_computation.1 | async-start | bytes 262144 | tf_op jit(solution)/shard_map/all_to_all | solution.py:234
  91.6 10.8 %collective-permute-start.5 = (f32[8,4,64,256]{3,2,1,0:T(8,128)S(1)}, f32[8,4,64,256]{3,2,1,0:T(8,128)S(1)}, u32[]{:S(2)}, u32[]{:S(2)}) collective-permute-start(f32[8,4,64,256]{3,2,1,0:T(8,128)S(1)} %slice.14), channel_id=1, source_target_pairs={{0,8},{8,0},{16,24},{24,16},{32,40},{40,32},{48,56},{56,48},{64,72... | collective-permute-start | bytes 6291464 | tf_op jit(solution)/shard_map/ppermute | solution.py:251

commit v4 on v3

--- a/solution.py
+++ b/solution.py
@@ -129,12 +129,14 @@
 
 def right_kernel(core, whole, right):
     half = right.shape[-1]
+    step = half // 2
     for block, parity in enumerate((core[0], 1 - core[0])):
-        stretch = slice(block * half, block * half + half)
-        both = triple(*(whole[:, 4 + part, :, parity].reshape(half, half) for part in range(2)))
-        for kind in range(3):
-            for level in range(2):
-                right[kind, level, stretch, :] = both[kind][level]
+        for line in range(2):
+            rows = slice(block * half + line * step, block * half + line * step + step)
+            both = triple(*(whole[:, 4 + part, :, line, parity].reshape(step, half) for part in range(2)))
+            for kind in range(3):
+                for level in range(2):
+                    right[kind, level, rows, :] = both[kind][level]
 
 
 def first_kernel(core, own, far, right, out):
@@ -142,22 +144,22 @@
     second = [(right[kind, 0], right[kind, 1]) for kind in range(3)]
     step = half // 2
     for block, parity in enumerate((core[0], 1 - core[0])):
-        for start in range(0, 2):
-            pieces = slice(4 * start, 4 * start + 4)
+        for line in range(2):
             rises = [
-                jnp.concatenate([ref[pieces, 2 + part, :, parity].reshape(step, half) for ref in (own, far)], axis=1)
+                jnp.concatenate([ref[:, 2 + part, :, line, parity].reshape(step, half) for ref in (own, far)], axis=1)
                 for part in range(2)
             ]
             both = triple(*complex_dot(triple(*rises), second))
-            rows = slice(block * half + start * step, block * half + start * step + step)
+            rows = slice(block * half + line * step, block * half + line * step + step)
             for kind in range(3):
                 for level in range(2):
                     out[kind, level, rows] = both[kind][level]
 
 
 def second_kernel(own, far, middle, out):
-    half = out.shape[-1]
-    chips, rows = out.shape[0], out.shape[2]
+    quarter = out.shape[-1]
+    half = 2 * quarter
+    chips, rows = own.shape[0], own.shape[2]
     second = [(middle[kind, 0], middle[kind, 1]) for kind in range(3)]
     step = 2
     for start in range(0, chips, step):
@@ -165,13 +167,16 @@
         left = [jnp.concatenate([ref[pieces, part].reshape(step * rows, half) for ref in (own, far)], axis=1) for part in range(2)]
         result = complex_dot(triple(*left), second)
         for part in range(2):
-            out[pieces, part] = result[part].reshape(step, rows, half)
-
-
-def turn_kernel(scale, parts, out):
-    total = parts[0]
-    for chip in range(1, SLABS):
-        total = total + parts[chip]
+            value = result[part].reshape(step, rows, half)
+            for line in range(2):
+                out[line, pieces, part] = value[:, :, line * quarter : line * quarter + quarter]
+
+
+def turn_kernel(scale, chips, parts, out):
+    total = None
+    for place in range(parts.shape[0]):
+        if place % chips < SLABS:
+            total = parts[place] if total is None else total + parts[place]
     turned = (jnp.concatenate([total[0], total[1]], axis=0) * scale).T
     out[...] = turned.reshape(out.shape)
 
@@ -198,9 +203,11 @@
     total_depth = slab_count * deep
     me = core.reshape(1).astype(jnp.int32)
 
+    planes = pairs // 2
     spot = jnp.arange(width)
     parity = jnp.where(spot < half, core, 1 - core)
-    column = (spot % half) // CHUNK * (2 * CHUNK) + parity * CHUNK + spot % CHUNK
+    line, plane = spot % half // (half // 2), spot % (half // 2) // CHUNK
+    column = ((plane * 2 + line) * 2 + parity) * CHUNK + spot % CHUNK
     chosen = (jnp.arange(width)[:, None] == column[None, :]).astype(f32)
     sorted_data = jnp.dot(data.reshape(-1, width), chosen, precision=lax.Precision.HIGHEST)
     kept = sorted_data[:, :half].reshape(2, slab_count, row_count, half)
@@ -209,9 +216,9 @@
     taken = lax.ppermute(given, "depth", swap)
 
     row_waves = lax.dynamic_slice_in_dim(wavenumbers, lax.axis_index("row") * row_count, row_count)
-    mine = lambda v: lax.dynamic_index_in_dim(v.reshape(pairs, 2, CHUNK), core, 1, False).reshape(half)
+    mine = lambda v: jnp.sum(chosen[:, :half] * v[:, None], axis=0)
     col_waves = mine(wavenumbers)
-    near_cols = mine(eps_cols).reshape(1, half)
+    near_cols = mine(eps_cols.astype(f32)).astype(jnp.int32).reshape(1, half)
     levels = (pair * SLABS + jnp.arange(8)).astype(f32) + 0.5
     row_phase = row_waves[:, None] * levels[None, :]
     col_phase = levels[:, None] * col_waves[None, :]
@@ -249,7 +256,7 @@
     )
     whole = lax.all_to_all(late, "row", 0, 0, tiled=True)
     other = lax.ppermute(whole[:, :4], "depth", swap)
-    shape = lambda v: v.reshape(chips, v.shape[1], row_count // 16, 2, 8, half)
+    shape = lambda v: v.reshape(chips, v.shape[1], row_count // 32, 2, 2, CHUNK, half)
     parts = lambda n: jax.ShapeDtypeStruct((3, 2, width, n), jnp.bfloat16)
     right = call(right_kernel, parts(half), me, shape(whole), smem=(0,), room=8)
     middle = call(
@@ -262,18 +269,22 @@
     )
     partial = call(
         second_kernel,
-        (chips, 2, row_count, half),
+        (2, chips, 2, row_count, half // 2),
         whole, other, middle,
         flops=18 * width * width * half,
         room=12,
     )
-    gathered = lax.all_to_all(partial, "row", 0, 0, tiled=True)
+    in_plane = [
+        [(4 * z + 2 * line + c) * chips + chip for line in range(2) for chip in range(chips)] for z in range(planes) for c in range(2)
+    ]
+    partial = partial.reshape(2 * chips, 2, row_count, half // 2)
+    gathered = lax.all_to_all(partial, ("depth", "row"), 0, 0, axis_index_groups=in_plane, tiled=True)
     turned = call(
-        lambda parts, out: turn_kernel(4.0 / total_depth, parts, out),
-        (pairs, CHUNK, 2 * row_count),
+        lambda parts, out: turn_kernel(4.0 / total_depth, chips, parts, out),
+        (planes, CHUNK, 2 * row_count),
         gathered,
     )
-    ends = spread(turned, [[2 * e + c for e in range(pairs)] for c in range(2)])
+    ends = spread(turned, [[4 * z + k for z in range(planes)] for k in range(4)])
     return call(last_kernel, (2, row_count, CHUNK), ends)
 
 

time: 148 us -> 143 us (0.966); the launches traced: 145 us -> 142 us
  blocking collectives: 80.2 us -> 77.1 us
    all_to_all x1, blocking collectives: 19.3 us -> 16.5 us  [body(): lax.all_to_all(v, 'depth', 0, 0, axis_index_groups=groups, tiled=True)]
where the time goes in v4:
time: 143 us; the launch traced here: 142 us
  blocking collectives  77.1 us (54%)
  starting transfers between devices  29.7 us (21%)
  waiting for transfers between devices  26 us (18%)
  Pallas kernels  5.34 us (4%)
  local copies, waits for them, and re-layouts  2.29 us (2%)
    all_to_all x1, blocking collectives, body(): whole = lax.all_to_all(late, 'row', 0, 0, tiled=True)  41.2 us
    all_to_all x1, blocking collectives, body(): lax.all_to_all(partial, ('depth', 'row'), 0, 0, axis_index_groups=in_plan...  19.4 us
    all_to_all x1, blocking collectives, body(): lax.all_to_all(v, 'depth', 0, 0, axis_index_groups=groups, tiled=True)  16.5 us
    ppermute x3, waiting for transfers between devices, body(): lax.ppermute(group, 'depth', [(i, i - shift) for i in range(shift, deep)])  13 us
    all_to_all x2, waiting for transfers between devices, body(): lax.all_to_all(v, 'depth', 0, 0, axis_index_groups=groups, tiled=True)  9.01 us
    ppermute x1, starting transfers between devices, body(): taken = lax.ppermute(given, 'depth', swap)  8.79 us
    ppermute x1, starting transfers between devices, body(): other = lax.ppermute(whole[:, :4], 'depth', swap)  7.02 us
    all_to_all x2, starting transfers between devices, body(): lax.all_to_all(v, 'depth', 0, 0, axis_index_groups=groups, tiled=True)  6.74 us
  transfers between devices with their start and end apart: 8, of which 7 were waited for; matrix products, arithmetic and copies ran while one was open for 1% of the time, Pallas kernels for 0%

profile of v4, /device:TPU:1, one launch (start us, length us, event | category | flops | bytes accessed | tf_op | source)
XLA Modules:
  0.0 142.2 jit_solution(7192244028804605965)
XLA Ops:
  0.0 0.0 copy-start
  0.0 0.0 copy-start.2
  0.0 0.0 copy-start.1
  0.0 1.1 copy-done
  1.1 0.9 convolution_bitcast_fusion
  2.0 0.0 copy-start.3
  2.0 0.1 fusion.25
  2.1 8.8 %collective-permute-start = (f32[2,3,64,256]{3,2,1,0:T(8,128)S(1)}, f32[2,3,64,256]{3,2,1,0:T(8,128)S(1)}, u32[]{:S(2)}, u32[]{:S(2)}) collective-permute-start(f32[2,3,64,256]{3,2,1,0:T(8,128)S(1)} %bitcast.19), channel_id=1, source_target_pairs={{0,8},{8,0},{16,24},{24,16},{32,40},{40,32},{48,56},{56,48},{64,72... | collective-permute-start | bytes 1179656 | tf_op jit(solution)/shard_map/ppermute | solution.py:216
  10.9 0.2 iota_compare_fusion
  11.0 0.0 copy-done.2
  11.1 0.0 copy-done.1
  11.1 0.1 dynamic_slice.3
  11.2 0.2 select_reduce_fusion
  11.4 0.1 multiply_cosine_fusion.1
  11.5 0.1 copy.10.row_trig
  11.6 0.1 multiply_cosine_fusion
  11.7 0.5 collective-permute-done.taken
  12.2 1.0 shard_map.46
  13.2 3.4 %all-to-all-start = ((f32[8,4,8,128]{3,2,1,0:T(8,128)}), f32[8,4,8,128]{3,2,1,0:T(8,128)S(1)}, u32[]{:S(2)}, u32[]{:S(2)}) async-start(f32[8,4,8,128]{3,2,1,0:T(8,128)} %get-tuple-element.15), calls=%async_computation | async-start | bytes 262144 | tf_op jit(solution)/shard_map/all_to_all | solution.py:241
  16.5 3.3 %collective-permute-start.1 = (f32[2,2,64,256]{3,2,1,0:T(8,128)S(1)}, f32[2,2,64,256]{3,2,1,0:T(8,128)S(1)}, u32[]{:S(2)}, u32[]{:S(2)}) collective-permute-start(f32[2,2,64,256]{3,2,1,0:T(8,128)S(1)} %get-tuple-element.17), channel_id=1, source_target_pairs={{0,16},{8,24},{16,32},{24,40},{32,48},{40,56},{48,64},{56,72},{64,... | collective-permute-start | bytes 786440 | tf_op jit(solution)/shard_map/ppermute | solution.py:248
  19.8 2.9 %all-to-all-done.parts = f32[8,4,8,128]{3,2,1,0:T(8,128)S(1)} async-done(((f32[8,4,8,128]{3,2,1,0:T(8,128)}), f32[8,4,8,128]{3,2,1,0:T(8,128)S(1)}, u32[]{:S(2)}, u32[]{:S(2)}) %all-to-all-start) | async-done | bytes 131104 | tf_op jit(solution)/shard_map/all_to_all | solution.py:241
  22.8 1.3 collective-permute-start.2
  24.1 1.3 collective-permute-start.3
  25.4 1.3 collective-permute-start.4
  26.7 0.0 collective-permute-done.1.rim
  26.7 4.5 %collective-permute-done.2.refs_0_ = f32[4,8,128]{2,1,0:T(8,128)S(1)} collective-permute-done((f32[4,8,128]{2,1,0:T(8,128)S(1)}, f32[4,8,128]{2,1,0:T(8,128)S(1)}, u32[]{:S(2)}, u32[]{:S(2)}) %collective-permute-start.2) | collective-permute-done | bytes 16416 | tf_op jit(solution)/shard_map/ppermute | solution.py:245
  31.2 6.1 %collective-permute-done.3.refs_1_ = f32[4,8,128]{2,1,0:T(8,128)S(1)} collective-permute-done((f32[4,8,128]{2,1,0:T(8,128)S(1)}, f32[4,8,128]{2,1,0:T(8,128)S(1)}, u32[]{:S(2)}, u32[]{:S(2)}) %collective-permute-start.3) | collective-permute-done | bytes 16416 | tf_op jit(solution)/shard_map/ppermute | solution.py:245
  37.3 2.4 %collective-permute-done.4.refs_2_ = f32[4,8,128]{2,1,0:T(8,128)S(1)} collective-permute-done((f32[4,8,128]{2,1,0:T(8,128)S(1)}, f32[4,8,128]{2,1,0:T(8,128)S(1)}, u32[]{:S(2)}, u32[]{:S(2)}) %collective-permute-start.4) | collective-permute-done | bytes 16416 | tf_op jit(solution)/shard_map/ppermute | solution.py:245
  39.7 0.7 shard_map.48
  40.4 3.4 %all-to-all-start.1 = ((f32[8,4,8,128]{3,2,1,0:T(8,128)}), f32[8,4,8,128]{3,2,1,0:T(8,128)S(1)}, u32[]{:S(2)}, u32[]{:S(2)}) async-start(f32[8,4,8,128]{3,2,1,0:T(8,128)} %shard_map.48), calls=%async_computation.1 | async-start | bytes 262144 | tf_op jit(solution)/shard_map/all_to_all | solution.py:241
  43.7 0.0 copy-done.3
  43.8 0.1 copy.11.eps_r
  43.9 6.1 %all-to-all-done.1.carry = f32[8,4,8,128]{3,2,1,0:T(8,128)S(1)} async-done(((f32[8,4,8,128]{3,2,1,0:T(8,128)}), f32[8,4,8,128]{3,2,1,0:T(8,128)S(1)}, u32[]{:S(2)}, u32[]{:S(2)}) %all-to-all-start.1) | async-done | bytes 131104 | tf_op jit(solution)/shard_map/all_to_all | solution.py:241
  49.9 0.2 shard_map.49
  50.2 41.2 %all_to_all.25.own = f32[8,6,64,256]{3,2,1,0:T(8,128)S(1)} all-to-all(f32[8,6,64,256]{3,2,1,0:T(8,128)S(1)} %shard_map.49), channel_id=1, replica_groups=mesh['depth'=64,'row'=8] {'row'}, dimensions={0} | all-to-all | bytes 6291456 | tf_op jit(solution)/shard_map/all_to_all | solution.py:257
  91.4 0.2 slice.21
  91.6 7.0 %collective-permute-start.5 = (f32[8,4,64,256]{3,2,1,0:T(8,128)S(1)}, f32[8,4,64,256]{3,2,1,0:T(8,128)S(1)}, u32[]{:S(2)}, u32[]{:S(2)}) collective-permute-start(f32[8,4,64,256]{3,2,1,0:T(8,128)S(1)} %slice.21), channel_id=1, source_target_pairs={{0,8},{8,0},{16,24},{24,16},{32,40},{40,32},{48,56},{56,48},{64,72... | collective-permute-start | bytes 6291464 | tf_op jit(solution)/shard_map/ppermute | solution.py:258
  98.6 0.2 shard_map.50.right
  98.8 3.5 %collective-permute-done.5.far = f32[8,4,64,256]{3,2,1,0:T(8,128)S(1)} collective-permute-done((f32[8,4,64,256]{3,2,1,0:T(8,128)S(1)}, f32[8,4,64,256]{3,2,1,0:T(8,128)S(1)}, u32[]{:S(2)}, u32[]{:S(2)}) %collective-permute-start.5) | collective-permute-done | bytes 2097184 | tf_op jit(solution)/shard_map/ppermute | solution.py:258
  102.4 1.6 %shard_map.51.middle = bf16[3,2,512,256]{3,2,1,0:T(8,128)(2,1)S(1)} custom-call(s32[1]{0:T(128)} %bitcast.core, f32[8,6,2,2,2,8,256]{6,5,4,3,2,1,0:T(8,128)S(1)} %bitcast.14, f32[8,4,2,2,2,8,256]{6,5,4,3,2,1,0:T(8,128)S(1)} %bitcast.15, bf16[3,2,512,256]{3,2,1,0:T(8,128)(2,1)S(1)} %shard_map.50.right), custom_call_target="tpu_custom_call" | custom-call | flops 1207959552 | bytes 11534340 | tf_op jit(solution)/shard_map/pallas_call | solution.py:24
  104.0 1.4 %shard_map.52 = f32[2,8,2,64,128]{4,3,2,1,0:T(8,128)S(1)} custom-call(f32[8,6,64,256]{3,2,1,0:T(8,128)S(1)} %all_to_all.25.own, f32[8,4,64,256]{3,2,1,0:T(8,128)S(1)} %collective-permute-done.5.far, bf16[3,2,512,256]{3,2,1,0:T(8,128)(2,1)S(1)} %shard_map.51.middle), custom_call_target="tpu_custom_call" | custom-call | flops 1207959552 | bytes 9437184 | tf_op jit(solution)/shard_map/pallas_call | solution.py:24
  105.4 19.4 %all_to_all.26.parts = f32[16,2,64,128]{3,2,1,0:T(8,128)S(1)} all-to-all(f32[16,2,64,128]{3,2,1,0:T(8,128)S(1)} %bitcast.16), channel_id=1, replica_groups={{0,1,2,3,4,5,6,7,16,17,18,19,20,21,22,23},{8,9,10,11,12,13,14,15,24,25,..., dimensions={0} | all-to-all | bytes 2097152 | tf_op jit(solution)/shard_map/all_to_all | solution.py:281
  124.8 0.1 shard_map.53
  124.9 16.5 %all_to_all.27.parts = f32[16,8,128]{2,1,0:T(8,128)S(1)} all-to-all(f32[16,8,128]{2,1,0:T(8,128)S(1)} %shard_map.53), channel_id=1, replica_groups={{0,32,64,96,128,160,192,224,256,288,320,352,384,416,448,480},{8,40,72,1..., dimensions={0} | all-to-all | bytes 131072 | tf_op jit(solution)/shard_map/all_to_all | solution.py:241
  141.4 0.1 shard_map.54
  141.5 0.7 copy.12
  (7 shorter events, 0.0 us)
Async XLA Ops:
  0.0 1.1 copy-start
  0.0 11.0 %copy-start.2 = (s32[512]{0:T(512)S(1)}, s32[512]{0:T(512)}, u32[]{:S(2)}) copy-start(s32[512]{0:T(512)} %param.7) | copy-start | bytes 6148
  0.0 11.1 %copy-start.1 = (f32[512]{0:T(512)S(1)}, f32[512]{0:T(512)}, u32[]{:S(2)}) copy-start(f32[512]{0:T(512)} %param.5) | copy-start | bytes 6148
  2.0 41.8 %copy-start.3 = (s32[64]{0:T(128)S(1)}, s32[64]{0:T(128)}, u32[]{:S(2)}) copy-start(s32[64]{0:T(128)} %param.6) | copy-start | bytes 772
  2.1 10.1 %collective-permute-start = (f32[2,3,64,256]{3,2,1,0:T(8,128)S(1)}, f32[2,3,64,256]{3,2,1,0:T(8,128)S(1)}, u32[]{:S(2)}, u32[]{:S(2)}) collective-permute-start(f32[2,3,64,256]{3,2,1,0:T(8,128)S(1)} %bitcast.19), channel_id=1, source_target_pairs={{0,8},{8,0},{16,24},{24,16},{32,40},{40,32},{48,56},{56,48},{64,72... | collective-permute-start | bytes 1179656 | tf_op jit(solution)/shard_map/ppermute | solution.py:216
  13.2 9.6 %all-to-all-start = ((f32[8,4,8,128]{3,2,1,0:T(8,128)}), f32[8,4,8,128]{3,2,1,0:T(8,128)S(1)}, u32[]{:S(2)}, u32[]{:S(2)}) async-start(f32[8,4,8,128]{3,2,1,0:T(8,128)} %get-tuple-element.15), calls=%async_computation | async-start | bytes 262144 | tf_op jit(solution)/shard_map/all_to_all | solution.py:241
  16.5 10.1 %collective-permute-start.1 = (f32[2,2,64,256]{3,2,1,0:T(8,128)S(1)}, f32[2,2,64,256]{3,2,1,0:T(8,128)S(1)}, u32[]{:S(2)}, u32[]{:S(2)}) collective-permute-start(f32[2,2,64,256]{3,2,1,0:T(8,128)S(1)} %get-tuple-element.17), channel_id=1, source_target_pairs={{0,16},{8,24},{16,32},{24,40},{32,48},{40,56},{48,64},{56,72},{64,... | collective-permute-start | bytes 786440 | tf_op jit(solution)/shard_map/ppermute | solution.py:248
  22.8 8.4 %collective-permute-start.2 = (f32[4,8,128]{2,1,0:T(8,128)S(1)}, f32[4,8,128]{2,1,0:T(8,128)S(1)}, u32[]{:S(2)}, u32[]{:S(2)}) collective-permute-start(f32[4,8,128]{2,1,0:T(8,128)S(1)} %get-tuple-element.18), channel_id=1, source_target_pairs={{128,0},{136,8},{144,16},{152,24},{160,32},{168,40},{176,48},{184,... | collective-permute-start | bytes 49160 | tf_op jit(solution)/shard_map/ppermute | solution.py:245
  24.1 13.2 %collective-permute-start.3 = (f32[4,8,128]{2,1,0:T(8,128)S(1)}, f32[4,8,128]{2,1,0:T(8,128)S(1)}, u32[]{:S(2)}, u32[]{:S(2)}) collective-permute-start(f32[4,8,128]{2,1,0:T(8,128)S(1)} %get-tuple-element.18), channel_id=1, source_target_pairs={{256,0},{264,8},{272,16},{280,24},{288,32},{296,40},{304,48},{312,... | collective-permute-start | bytes 49160 | tf_op jit(solution)/shard_map/ppermute | solution.py:245
  25.4 14.3 %collective-permute-start.4 = (f32[4,8,128]{2,1,0:T(8,128)S(1)}, f32[4,8,128]{2,1,0:T(8,128)S(1)}, u32[]{:S(2)}, u32[]{:S(2)}) collective-permute-start(f32[4,8,128]{2,1,0:T(8,128)S(1)} %get-tuple-element.18), channel_id=1, source_target_pairs={{384,0},{392,8},{400,16},{408,24},{416,32},{424,40},{432,48},{440,... | collective-permute-start | bytes 49160 | tf_op jit(solution)/shard_map/ppermute | solution.py:245
  40.4 9.6 %all-to-all-start.1 = ((f32[8,4,8,128]{3,2,1,0:T(8,128)}), f32[8,4,8,128]{3,2,1,0:T(8,128)S(1)}, u32[]{:S(2)}, u32[]{:S(2)}) async-start(f32[8,4,8,128]{3,2,1,0:T(8,128)} %shard_map.48), calls=%async_computation.1 | async-start | bytes 262144 | tf_op jit(solution)/shard_map/all_to_all | solution.py:241
  91.6 10.8 %collective-permute-start.5 = (f32[8,4,64,256]{3,2,1,0:T(8,128)S(1)}, f32[8,4,64,256]{3,2,1,0:T(8,128)S(1)}, u32[]{:S(2)}, u32[]{:S(2)}) collective-permute-start(f32[8,4,64,256]{3,2,1,0:T(8,128)S(1)} %slice.21), channel_id=1, source_target_pairs={{0,8},{8,0},{16,24},{24,16},{32,40},{40,32},{48,56},{56,48},{64,72... | collective-permute-start | bytes 6291464 | tf_op jit(solution)/shard_map/ppermute | solution.py:258

commit v5 on v4

--- a/solution.py
+++ b/solution.py
@@ -127,30 +127,38 @@
     return split(re), split(im), split(re + im)
 
 
-def right_kernel(core, whole, right):
-    half = right.shape[-1]
+def right_kernel(core, whole, far_right, part):
+    half = part.shape[-1]
+    step = half // 2
+
+    def rows_of(array, line, parity):
+        return [whole[:, array + part, :, line, parity].reshape(step, half) for part in range(2)]
+
+    own = [jnp.concatenate(pair, axis=0) for pair in zip(rows_of(4, 0, core[0]), rows_of(4, 1, core[0]))]
+    own = triple(*own)
+    for line in range(2):
+        both = triple(*rows_of(4, line, 1 - core[0]))
+        for kind in range(3):
+            for level in range(2):
+                far_right[kind, level, line * step : line * step + step] = both[kind][level]
+    for block, parity in enumerate((core[0], 1 - core[0])):
+        for line in range(2):
+            rows = slice(block * half + line * step, block * half + line * step + step)
+            product = complex_dot(triple(*rows_of(2, line, parity)), own)
+            for level in range(2):
+                part[level, rows] = product[level]
+
+
+def first_kernel(core, far, far_right, part, out):
+    half = out.shape[-1]
+    second = [(far_right[kind, 0], far_right[kind, 1]) for kind in range(3)]
     step = half // 2
     for block, parity in enumerate((core[0], 1 - core[0])):
         for line in range(2):
             rows = slice(block * half + line * step, block * half + line * step + step)
-            both = triple(*(whole[:, 4 + part, :, line, parity].reshape(step, half) for part in range(2)))
-            for kind in range(3):
-                for level in range(2):
-                    right[kind, level, rows, :] = both[kind][level]
-
-
-def first_kernel(core, own, far, right, out):
-    half = out.shape[-1]
-    second = [(right[kind, 0], right[kind, 1]) for kind in range(3)]
-    step = half // 2
-    for block, parity in enumerate((core[0], 1 - core[0])):
-        for line in range(2):
-            rises = [
-                jnp.concatenate([ref[:, 2 + part, :, line, parity].reshape(step, half) for ref in (own, far)], axis=1)
-                for part in range(2)
-            ]
-            both = triple(*complex_dot(triple(*rises), second))
-            rows = slice(block * half + line * step, block * half + line * step + step)
+            rises = [far[:, level, :, line, parity].reshape(step, half) for level in range(2)]
+            product = complex_dot(triple(*rises), second)
+            both = triple(*(product[level] + part[level, rows] for level in range(2)))
             for kind in range(3):
                 for level in range(2):
                     out[kind, level, rows] = both[kind][level]
@@ -241,10 +249,8 @@
     spread = lambda v, groups: lax.all_to_all(v, "depth", 0, 0, axis_index_groups=groups, tiled=True)
     seen = spread(total, near)
     sums, group = call(group_kernel, [seen.shape, seen.shape[1:]], seen)
-    deeper = [
-        lax.ppermute(group, "depth", [(i, i - shift) for i in range(shift, deep)])
-        for shift in range(2 * NEAR, deep, 2 * NEAR)
-    ]
+    onward = lambda v, by: lax.ppermute(v, "depth", [(i, i - by) for i in range(by, deep)])
+    deeper = [onward(group, 2 * NEAR * by) for by in (3, 1, 2)]
     rim = lax.ppermute(rim, "depth", [(i, i + 2) for i in range(deep - 2)])
     rim, *deeper = lax.optimization_barrier((rim, *deeper))
     carry = spread(call(deep_kernel, sums.shape, sums, *deeper), near)
@@ -255,22 +261,30 @@
         carry, down, up, rim, eps_rows.reshape(row_count, 1), near_cols,
     )
     whole = lax.all_to_all(late, "row", 0, 0, tiled=True)
-    other = lax.ppermute(whole[:, :4], "depth", swap)
+    up_far = lax.ppermute(whole[:, 2:4], "depth", swap)
+    left_far = lax.ppermute(whole[:, :2], "depth", swap)
     shape = lambda v: v.reshape(chips, v.shape[1], row_count // 32, 2, 2, CHUNK, half)
-    parts = lambda n: jax.ShapeDtypeStruct((3, 2, width, n), jnp.bfloat16)
-    right = call(right_kernel, parts(half), me, shape(whole), smem=(0,), room=8)
+    parts = lambda n: jax.ShapeDtypeStruct((3, 2, n, half), jnp.bfloat16)
+    far_right, part = call(
+        right_kernel,
+        [parts(half), (2, width, half)],
+        me, shape(whole),
+        smem=(0,),
+        flops=9 * width * width * half,
+        room=12,
+    )
     middle = call(
         first_kernel,
-        parts(half),
-        me, shape(whole), shape(other), right,
+        parts(width),
+        me, shape(up_far), far_right, part,
         smem=(0,),
-        flops=18 * width * width * half,
+        flops=9 * width * width * half,
         room=12,
     )
     partial = call(
         second_kernel,
         (2, chips, 2, row_count, half // 2),
-        whole, other, middle,
+        whole, left_far, middle,
         flops=18 * width * width * half,
         room=12,
     )

time: 143 us -> 142 us (level)
  waiting for transfers between devices: 26 us -> 22.8 us
  starting transfers between devices: 29.7 us -> 31.4 us
    ppermute x4 -> x5, waiting for transfers between devices: 16.6 us -> 13.3 us  [the longest x3 12.8 us: body(): lax.ppermute(v, 'depth', [(i, i - by) for i in range(by, deep)])]
    ppermute x4 -> x5, starting transfers between devices: 10.9 us -> 12.6 us  [the longest x1 6.83 us: body(): up_far = lax.ppermute(whole[:, 2:4], 'depth', swap)]
  transfers between devices with their start and end apart: 8 -> 9, of which waited for: 7 -> 6; matrix products, arithmetic and copies ran while one was open for 1% -> 1% of each run, Pallas kernels for 0% -> 1%
where the time goes in v5:
time: 142 us
  blocking collectives  77.7 us (55%)
  starting transfers between devices  31.4 us (22%)
  waiting for transfers between devices  22.8 us (16%)
  Pallas kernels  5.61 us (4%)
  local copies, waits for them, and re-layouts  2.28 us (2%)
    all_to_all x1, blocking collectives, body(): whole = lax.all_to_all(late, 'row', 0, 0, tiled=True)  41.7 us
    all_to_all x1, blocking collectives, body(): lax.all_to_all(partial, ('depth', 'row'), 0, 0, axis_index_groups=in_plan...  19.5 us
    all_to_all x1, blocking collectives, body(): lax.all_to_all(v, 'depth', 0, 0, axis_index_groups=groups, tiled=True)  16.5 us
    ppermute x3, waiting for transfers between devices, body(): lax.ppermute(v, 'depth', [(i, i - by) for i in range(by, deep)])  12.8 us
    all_to_all x2, waiting for transfers between devices, body(): lax.all_to_all(v, 'depth', 0, 0, axis_index_groups=groups, tiled=True)  8.97 us
    ppermute x1, starting transfers between devices, body(): taken = lax.ppermute(given, 'depth', swap)  8.79 us
    ppermute x1, starting transfers between devices, body(): up_far = lax.ppermute(whole[:, 2:4], 'depth', swap)  6.83 us
    all_to_all x2, starting transfers between devices, body(): lax.all_to_all(v, 'depth', 0, 0, axis_index_groups=groups, tiled=True)  6.74 us
  transfers between devices with their start and end apart: 9, of which 6 were waited for; matrix products, arithmetic and copies ran while one was open for 1% of the time, Pallas kernels for 1%

profile of v5, /device:TPU:1, one launch (start us, length us, event | category | flops | bytes accessed | tf_op | source)
XLA Modules:
  0.0 141.5 jit_solution(4129031065153387946)
XLA Ops:
  0.0 0.0 copy-start
  0.0 0.0 copy-start.2
  0.0 0.0 copy-start.1
  0.0 0.0 copy-start.3
  0.1 1.1 copy-done
  1.1 0.9 convolution_bitcast_fusion
  2.0 0.1 fusion.26
  2.1 8.8 %collective-permute-start = (f32[2,3,64,256]{3,2,1,0:T(8,128)S(1)}, f32[2,3,64,256]{3,2,1,0:T(8,128)S(1)}, u32[]{:S(2)}, u32[]{:S(2)}) collective-permute-start(f32[2,3,64,256]{3,2,1,0:T(8,128)S(1)} %bitcast.18), channel_id=1, source_target_pairs={{0,8},{8,0},{16,24},{24,16},{32,40},{40,32},{48,56},{56,48},{64,72... | collective-permute-start | bytes 1179656 | tf_op jit(solution)/shard_map/ppermute | solution.py:224
  10.9 0.2 iota_compare_fusion
  11.1 0.0 copy-done.2
  11.1 0.0 copy-done.1
  11.1 0.1 dynamic_slice.3
  11.2 0.1 multiply_cosine_fusion.1
  11.3 0.2 select_reduce_fusion
  11.5 0.1 copy.10.row_trig
  11.6 0.1 multiply_cosine_fusion
  11.7 0.5 collective-permute-done.taken
  12.2 1.0 shard_map.46
  13.2 3.4 %all-to-all-start = ((f32[8,4,8,128]{3,2,1,0:T(8,128)}), f32[8,4,8,128]{3,2,1,0:T(8,128)S(1)}, u32[]{:S(2)}, u32[]{:S(2)}) async-start(f32[8,4,8,128]{3,2,1,0:T(8,128)} %get-tuple-element.17), calls=%async_computation | async-start | bytes 262144 | tf_op jit(solution)/shard_map/all_to_all | solution.py:249
  16.5 3.3 %collective-permute-start.1 = (f32[2,2,64,256]{3,2,1,0:T(8,128)S(1)}, f32[2,2,64,256]{3,2,1,0:T(8,128)S(1)}, u32[]{:S(2)}, u32[]{:S(2)}) collective-permute-start(f32[2,2,64,256]{3,2,1,0:T(8,128)S(1)} %get-tuple-element.19), channel_id=1, source_target_pairs={{0,16},{8,24},{16,32},{24,40},{32,48},{40,56},{48,64},{56,72},{64,... | collective-permute-start | bytes 786440 | tf_op jit(solution)/shard_map/ppermute | solution.py:254
  19.8 2.9 %all-to-all-done.parts = f32[8,4,8,128]{3,2,1,0:T(8,128)S(1)} async-done(((f32[8,4,8,128]{3,2,1,0:T(8,128)}), f32[8,4,8,128]{3,2,1,0:T(8,128)S(1)}, u32[]{:S(2)}, u32[]{:S(2)}) %all-to-all-start) | async-done | bytes 131104 | tf_op jit(solution)/shard_map/all_to_all | solution.py:249
  22.8 1.3 collective-permute-start.4
  24.1 1.3 collective-permute-start.3
  25.4 1.3 collective-permute-start.2
  26.7 0.0 collective-permute-done.1.rim
  26.7 9.3 %collective-permute-done.4.refs_2_ = f32[4,8,128]{2,1,0:T(8,128)S(1)} collective-permute-done((f32[4,8,128]{2,1,0:T(8,128)S(1)}, f32[4,8,128]{2,1,0:T(8,128)S(1)}, u32[]{:S(2)}, u32[]{:S(2)}) %collective-permute-start.4) | collective-permute-done | bytes 16416 | tf_op jit(solution)/shard_map/ppermute | solution.py:252
  36.0 0.0 collective-permute-done.3.refs_1_
  36.0 3.5 %collective-permute-done.2.refs_0_ = f32[4,8,128]{2,1,0:T(8,128)S(1)} collective-permute-done((f32[4,8,128]{2,1,0:T(8,128)S(1)}, f32[4,8,128]{2,1,0:T(8,128)S(1)}, u32[]{:S(2)}, u32[]{:S(2)}) %collective-permute-start.2) | collective-permute-done | bytes 16416 | tf_op jit(solution)/shard_map/ppermute | solution.py:252
  39.5 0.7 shard_map.48
  40.1 3.4 %all-to-all-start.1 = ((f32[8,4,8,128]{3,2,1,0:T(8,128)}), f32[8,4,8,128]{3,2,1,0:T(8,128)S(1)}, u32[]{:S(2)}, u32[]{:S(2)}) async-start(f32[8,4,8,128]{3,2,1,0:T(8,128)} %shard_map.48), calls=%async_computation.1 | async-start | bytes 262144 | tf_op jit(solution)/shard_map/all_to_all | solution.py:249
  43.5 0.0 copy-done.3
  43.5 0.1 copy.11.eps_r
  43.6 6.0 %all-to-all-done.1.carry = f32[8,4,8,128]{3,2,1,0:T(8,128)S(1)} async-done(((f32[8,4,8,128]{3,2,1,0:T(8,128)}), f32[8,4,8,128]{3,2,1,0:T(8,128)S(1)}, u32[]{:S(2)}, u32[]{:S(2)}) %all-to-all-start.1) | async-done | bytes 131104 | tf_op jit(solution)/shard_map/all_to_all | solution.py:249
  49.6 0.2 shard_map.49
  49.9 41.7 %all_to_all.25.own = f32[8,6,64,256]{3,2,1,0:T(8,128)S(1)} all-to-all(f32[8,6,64,256]{3,2,1,0:T(8,128)S(1)} %shard_map.49), channel_id=1, replica_groups=mesh['depth'=64,'row'=8] {'row'}, dimensions={0} | all-to-all | bytes 6291456 | tf_op jit(solution)/shard_map/all_to_all | solution.py:263
  91.6 0.2 fusion.25
  91.8 6.8 %collective-permute-start.6 = (f32[8,2,64,256]{3,2,1,0:T(8,128)S(1)}, f32[8,2,64,256]{3,2,1,0:T(8,128)S(1)}, u32[]{:S(2)}, u32[]{:S(2)}) collective-permute-start(f32[8,2,64,256]{3,2,1,0:T(8,128)S(1)} %get-tuple-element.31), channel_id=1, source_target_pairs={{0,8},{8,0},{16,24},{24,16},{32,40},{40,32},{48,56},{56,48},{64,72... | collective-permute-start | bytes 3145736 | tf_op jit(solution)/shard_map/ppermute | solution.py:264
  98.6 1.9 %collective-permute-start.5 = (f32[8,2,64,256]{3,2,1,0:T(8,128)S(1)}, f32[8,2,64,256]{3,2,1,0:T(8,128)S(1)}, u32[]{:S(2)}, u32[]{:S(2)}) collective-permute-start(f32[8,2,64,256]{3,2,1,0:T(8,128)S(1)} %get-tuple-element.32), channel_id=1, source_target_pairs={{0,8},{8,0},{16,24},{24,16},{32,40},{40,32},{48,56},{56,48},{64,72... | collective-permute-start | bytes 3145736 | tf_op jit(solution)/shard_map/ppermute | solution.py:265
  100.6 1.0 shard_map.50
  101.6 0.0 collective-permute-done.6
  101.6 1.0 shard_map.51.middle
  102.6 0.6 collective-permute-done.5.far
  103.2 1.4 %shard_map.52 = f32[2,8,2,64,128]{4,3,2,1,0:T(8,128)S(1)} custom-call(f32[8,6,64,256]{3,2,1,0:T(8,128)S(1)} %all_to_all.25.own, f32[8,2,64,256]{3,2,1,0:T(8,128)S(1)} %collective-permute-done.5.far, bf16[3,2,512,256]{3,2,1,0:T(8,128)(2,1)S(1)} %shard_map.51.middle), custom_call_target="tpu_custom_call" | custom-call | flops 1207959552 | bytes 8388608 | tf_op jit(solution)/shard_map/pallas_call | solution.py:24
  104.6 19.5 %all_to_all.26.parts = f32[16,2,64,128]{3,2,1,0:T(8,128)S(1)} all-to-all(f32[16,2,64,128]{3,2,1,0:T(8,128)S(1)} %bitcast.14), channel_id=1, replica_groups={{0,1,2,3,4,5,6,7,16,17,18,19,20,21,22,23},{8,9,10,11,12,13,14,15,24,25,..., dimensions={0} | all-to-all | bytes 2097152 | tf_op jit(solution)/shard_map/all_to_all | solution.py:295
  124.2 0.1 shard_map.53
  124.3 16.5 %all_to_all.27.parts = f32[16,8,128]{2,1,0:T(8,128)S(1)} all-to-all(f32[16,8,128]{2,1,0:T(8,128)S(1)} %shard_map.53), channel_id=1, replica_groups={{0,32,64,96,128,160,192,224,256,288,320,352,384,416,448,480},{8,40,72,1..., dimensions={0} | all-to-all | bytes 131072 | tf_op jit(solution)/shard_map/all_to_all | solution.py:249
  140.7 0.1 shard_map.54
  140.8 0.7 copy.12
  (7 shorter events, 0.0 us)
Async XLA Ops:
  0.0 1.1 copy-start
  0.0 11.1 %copy-start.2 = (s32[512]{0:T(512)S(1)}, s32[512]{0:T(512)}, u32[]{:S(2)}) copy-start(s32[512]{0:T(512)} %param.7) | copy-start | bytes 6148
  0.0 11.1 %copy-start.1 = (f32[512]{0:T(512)S(1)}, f32[512]{0:T(512)}, u32[]{:S(2)}) copy-start(f32[512]{0:T(512)} %param.5) | copy-start | bytes 6148
  0.0 43.5 %copy-start.3 = (s32[64]{0:T(128)S(1)}, s32[64]{0:T(128)}, u32[]{:S(2)}) copy-start(s32[64]{0:T(128)} %param.6) | copy-start | bytes 772
  2.1 10.1 %collective-permute-start = (f32[2,3,64,256]{3,2,1,0:T(8,128)S(1)}, f32[2,3,64,256]{3,2,1,0:T(8,128)S(1)}, u32[]{:S(2)}, u32[]{:S(2)}) collective-permute-start(f32[2,3,64,256]{3,2,1,0:T(8,128)S(1)} %bitcast.18), channel_id=1, source_target_pairs={{0,8},{8,0},{16,24},{24,16},{32,40},{40,32},{48,56},{56,48},{64,72... | collective-permute-start | bytes 1179656 | tf_op jit(solution)/shard_map/ppermute | solution.py:224
  13.2 9.6 %all-to-all-start = ((f32[8,4,8,128]{3,2,1,0:T(8,128)}), f32[8,4,8,128]{3,2,1,0:T(8,128)S(1)}, u32[]{:S(2)}, u32[]{:S(2)}) async-start(f32[8,4,8,128]{3,2,1,0:T(8,128)} %get-tuple-element.17), calls=%async_computation | async-start | bytes 262144 | tf_op jit(solution)/shard_map/all_to_all | solution.py:249
  16.5 10.1 %collective-permute-start.1 = (f32[2,2,64,256]{3,2,1,0:T(8,128)S(1)}, f32[2,2,64,256]{3,2,1,0:T(8,128)S(1)}, u32[]{:S(2)}, u32[]{:S(2)}) collective-permute-start(f32[2,2,64,256]{3,2,1,0:T(8,128)S(1)} %get-tuple-element.19), channel_id=1, source_target_pairs={{0,16},{8,24},{16,32},{24,40},{32,48},{40,56},{48,64},{56,72},{64,... | collective-permute-start | bytes 786440 | tf_op jit(solution)/shard_map/ppermute | solution.py:254
  22.8 13.2 %collective-permute-start.4 = (f32[4,8,128]{2,1,0:T(8,128)S(1)}, f32[4,8,128]{2,1,0:T(8,128)S(1)}, u32[]{:S(2)}, u32[]{:S(2)}) collective-permute-start(f32[4,8,128]{2,1,0:T(8,128)S(1)} %get-tuple-element.20), channel_id=1, source_target_pairs={{256,0},{264,8},{272,16},{280,24},{288,32},{296,40},{304,48},{312,... | collective-permute-start | bytes 49160 | tf_op jit(solution)/shard_map/ppermute | solution.py:252
  24.1 11.9 %collective-permute-start.3 = (f32[4,8,128]{2,1,0:T(8,128)S(1)}, f32[4,8,128]{2,1,0:T(8,128)S(1)}, u32[]{:S(2)}, u32[]{:S(2)}) collective-permute-start(f32[4,8,128]{2,1,0:T(8,128)S(1)} %get-tuple-element.20), channel_id=1, source_target_pairs={{128,0},{136,8},{144,16},{152,24},{160,32},{168,40},{176,48},{184,... | collective-permute-start | bytes 49160 | tf_op jit(solution)/shard_map/ppermute | solution.py:252
  25.4 14.1 %collective-permute-start.2 = (f32[4,8,128]{2,1,0:T(8,128)S(1)}, f32[4,8,128]{2,1,0:T(8,128)S(1)}, u32[]{:S(2)}, u32[]{:S(2)}) collective-permute-start(f32[4,8,128]{2,1,0:T(8,128)S(1)} %get-tuple-element.20), channel_id=1, source_target_pairs={{384,0},{392,8},{400,16},{408,24},{416,32},{424,40},{432,48},{440,... | collective-permute-start | bytes 49160 | tf_op jit(solution)/shard_map/ppermute | solution.py:252
  40.1 9.5 %all-to-all-start.1 = ((f32[8,4,8,128]{3,2,1,0:T(8,128)}), f32[8,4,8,128]{3,2,1,0:T(8,128)S(1)}, u32[]{:S(2)}, u32[]{:S(2)}) async-start(f32[8,4,8,128]{3,2,1,0:T(8,128)} %shard_map.48), calls=%async_computation.1 | async-start | bytes 262144 | tf_op jit(solution)/shard_map/all_to_all | solution.py:249
  91.8 9.8 %collective-permute-start.6 = (f32[8,2,64,256]{3,2,1,0:T(8,128)S(1)}, f32[8,2,64,256]{3,2,1,0:T(8,128)S(1)}, u32[]{:S(2)}, u32[]{:S(2)}) collective-permute-start(f32[8,2,64,256]{3,2,1,0:T(8,128)S(1)} %get-tuple-element.31), channel_id=1, source_target_pairs={{0,8},{8,0},{16,24},{24,16},{32,40},{40,32},{48,56},{56,48},{64,72... | collective-permute-start | bytes 3145736 | tf_op jit(solution)/shard_map/ppermute | solution.py:264
  98.6 4.6 %collective-permute-start.5 = (f32[8,2,64,256]{3,2,1,0:T(8,128)S(1)}, f32[8,2,64,256]{3,2,1,0:T(8,128)S(1)}, u32[]{:S(2)}, u32[]{:S(2)}) collective-permute-start(f32[8,2,64,256]{3,2,1,0:T(8,128)S(1)} %get-tuple-element.32), channel_id=1, source_target_pairs={{0,8},{8,0},{16,24},{24,16},{32,40},{40,32},{48,56},{56,48},{64,72... | collective-permute-start | bytes 3145736 | tf_op jit(solution)/shard_map/ppermute | solution.py:265

commit v6 on v5

--- a/solution.py
+++ b/solution.py
@@ -38,7 +38,7 @@
     return row_cos * col_cos - row_sin * col_sin, row_sin * col_cos + row_cos * col_sin
 
 
-def phase_kernel(core, kept, taken, row_trig, col_trig, down, up, rim, total):
+def phase_kernel(core, kept, taken, row_trig, col_trig, _row, _col, down, up, rim, total):
     first_core = core[0] == 0
     held = kept.shape[1]
     totals = [None, None]
@@ -95,7 +95,7 @@
             rows = slice(8 * block, 8 * block + 8)
             for lane in range(2):
                 cols = slice(128 * lane, 128 * lane + 128)
-                near_col = eps_c[:, cols] == 1
+                near_col = eps_c[:, cols] == 1.0
                 below = carry[(8 * part + block) // 2, 2 * (block % 2) + lane]
                 for slab in range(SLABS - 1, -1, -1):
                     here = below + down[part, slab, rows, cols]
@@ -193,10 +193,9 @@
     total = parts[0]
     for place in range(1, parts.shape[0]):
         total = total + parts[place]
-    turned = total.T
-    rows = out.shape[1]
-    out[0] = turned[:rows]
-    out[1] = turned[rows:]
+    rows = out.shape[2]
+    out[0] = total[:, :rows]
+    out[1] = total[:, rows:]
 
 
 def body(data, wavenumbers, eps_rows, eps_cols):
@@ -217,7 +216,7 @@
     line, plane = spot % half // (half // 2), spot % (half // 2) // CHUNK
     column = ((plane * 2 + line) * 2 + parity) * CHUNK + spot % CHUNK
     chosen = (jnp.arange(width)[:, None] == column[None, :]).astype(f32)
-    sorted_data = jnp.dot(data.reshape(-1, width), chosen, precision=lax.Precision.HIGHEST)
+    sorted_data = jnp.dot(data.reshape(-1, width), chosen, precision=lax.Precision.HIGH)
     kept = sorted_data[:, :half].reshape(2, slab_count, row_count, half)
     given = sorted_data[:, half:].reshape(2, slab_count, row_count, half)
     swap = [(i, i ^ 1) for i in range(deep)]
@@ -226,12 +225,13 @@
     row_waves = lax.dynamic_slice_in_dim(wavenumbers, lax.axis_index("row") * row_count, row_count)
     mine = lambda v: jnp.sum(chosen[:, :half] * v[:, None], axis=0)
     col_waves = mine(wavenumbers)
-    near_cols = mine(eps_cols.astype(f32)).astype(jnp.int32).reshape(1, half)
+    near_cols = mine(eps_cols.astype(f32)).reshape(1, half)
     levels = (pair * SLABS + jnp.arange(8)).astype(f32) + 0.5
     row_phase = row_waves[:, None] * levels[None, :]
     col_phase = levels[:, None] * col_waves[None, :]
     row_trig = jnp.concatenate([jnp.cos(row_phase), jnp.sin(row_phase)], axis=1)
     col_trig = jnp.concatenate([jnp.cos(col_phase), jnp.sin(col_phase)], axis=0)
+    row_marks = eps_rows.reshape(row_count, 1)
     down, up, rim, total = call(
         phase_kernel,
         [
@@ -240,7 +240,7 @@
             (2, EPS_MOST, row_count, half),
             (NEAR, 32 // NEAR, 8, 128),
         ],
-        me, kept, taken, row_trig, col_trig,
+        me, kept, taken, row_trig, col_trig, row_marks, near_cols,
         smem=(0,),
         room=10,
     )
@@ -258,7 +258,7 @@
     late = call(
         late_kernel,
         (chips, 6, row_count, half),
-        carry, down, up, rim, eps_rows.reshape(row_count, 1), near_cols,
+        carry, down, up, rim, row_marks, near_cols,
     )
     whole = lax.all_to_all(late, "row", 0, 0, tiled=True)
     up_far = lax.ppermute(whole[:, 2:4], "depth", swap)
@@ -299,7 +299,7 @@
         gathered,
     )
     ends = spread(turned, [[4 * z + k for z in range(planes)] for k in range(4)])
-    return call(last_kernel, (2, row_count, CHUNK), ends)
+    return call(last_kernel, (2, CHUNK, row_count), ends).transpose(0, 2, 1)
 
 
 def solution(mesh):

time: 142 us -> 141 us (level)
  blocking collectives: 77.7 us -> 87 us
  waiting for transfers between devices: 22.8 us -> 16.6 us
  starting transfers between devices: 31.4 us -> 28.1 us
    all_to_all x1 -> x2, blocking collectives: 16.5 us -> 25.8 us  [body(): lax.all_to_all(v, 'depth', 0, 0, axis_index_groups=groups, tiled=True)]
    all_to_all x2 -> x1, waiting for transfers between devices: 8.97 us -> 2.93 us  [body(): lax.all_to_all(v, 'depth', 0, 0, axis_index_groups=groups, tiled=True)]
    all_to_all x2 -> x1, starting transfers between devices: 6.74 us -> 3.37 us  [body(): lax.all_to_all(v, 'depth', 0, 0, axis_index_groups=groups, tiled=True)]
  transfers between devices with their start and end apart: 9 -> 8, of which waited for: 6 -> 5; matrix products, arithmetic and copies ran while one was open for 1% -> 1% of each run, Pallas kernels for 1% -> 1%
where the time goes in v6:
time: 141 us; the launch traced here: 140 us
  blocking collectives  87 us (62%)
  starting transfers between devices  28.1 us (20%)
  waiting for transfers between devices  16.6 us (12%)
  Pallas kernels  5.55 us (4%)
  local copies, waits for them, and re-layouts  1.61 us (1%)
    all_to_all x1, blocking collectives, body(): whole = lax.all_to_all(late, 'row', 0, 0, tiled=True)  41.7 us
    all_to_all x2, blocking collectives, body(): lax.all_to_all(v, 'depth', 0, 0, axis_index_groups=groups, tiled=True)  25.8 us
    all_to_all x1, blocking collectives, body(): lax.all_to_all(partial, ('depth', 'row'), 0, 0, axis_index_groups=in_plan...  19.5 us
    ppermute x3, waiting for transfers between devices, body(): lax.ppermute(v, 'depth', [(i, i - by) for i in range(by, deep)])  12.8 us
    ppermute x1, starting transfers between devices, body(): taken = lax.ppermute(given, 'depth', swap)  8.78 us
    ppermute x1, starting transfers between devices, body(): up_far = lax.ppermute(whole[:, 2:4], 'depth', swap)  6.83 us
    pallas_call x9, Pallas kernels, call(): pl.pallas_call(kernel, out_shape=shapes[0] if single else shapes, in_spec...  5.55 us
    ppermute x3, starting transfers between devices, body(): lax.ppermute(v, 'depth', [(i, i - by) for i in range(by, deep)])  3.88 us
  transfers between devices with their start and end apart: 8, of which 5 were waited for; matrix products, arithmetic and copies ran while one was open for 1% of the time, Pallas kernels for 1%

profile of v6, /device:TPU:1, one launch (start us, length us, event | category | flops | bytes accessed | tf_op | source)
XLA Modules:
  0.0 140.3 jit_solution(12360254360381172612)
XLA Ops:
  0.0 0.0 copy-start
  0.0 0.0 copy-start.2
  0.0 0.0 copy-start.1
  0.0 0.0 copy-start.3
  0.1 1.1 copy-done
  1.1 0.6 convolution_bitcast_fusion
  1.8 0.1 fusion.26
  1.8 8.8 %collective-permute-start = (f32[2,3,64,256]{3,2,1,0:T(8,128)S(1)}, f32[2,3,64,256]{3,2,1,0:T(8,128)S(1)}, u32[]{:S(2)}, u32[]{:S(2)}) collective-permute-start(f32[2,3,64,256]{3,2,1,0:T(8,128)S(1)} %bitcast.20), channel_id=1, source_target_pairs={{0,8},{8,0},{16,24},{24,16},{32,40},{40,32},{48,56},{56,48},{64,72... | collective-permute-start | bytes 1179656 | tf_op jit(solution)/shard_map/ppermute | solution.py:223
  10.6 0.2 iota_compare_fusion
  10.8 0.0 copy-done.2
  10.9 0.0 copy-done.1
  10.9 0.1 dynamic_slice.3
  10.9 0.1 multiply_cosine_fusion.1
  11.1 0.2 select_reduce_fusion
  11.3 0.1 copy.10.row_trig
  11.4 0.0 copy-done.3
  11.4 0.1 copy.11._row.eps_r
  11.5 0.1 multiply_cosine_fusion
  11.6 0.4 collective-permute-done.taken
  12.0 1.0 shard_map.46
  12.9 3.4 %all-to-all-start = ((f32[8,4,8,128]{3,2,1,0:T(8,128)}), f32[8,4,8,128]{3,2,1,0:T(8,128)S(1)}, u32[]{:S(2)}, u32[]{:S(2)}) async-start(f32[8,4,8,128]{3,2,1,0:T(8,128)} %get-tuple-element.17), calls=%async_computation | async-start | bytes 262144 | tf_op jit(solution)/shard_map/all_to_all | solution.py:249
  16.3 3.3 %collective-permute-start.1 = (f32[2,2,64,256]{3,2,1,0:T(8,128)S(1)}, f32[2,2,64,256]{3,2,1,0:T(8,128)S(1)}, u32[]{:S(2)}, u32[]{:S(2)}) collective-permute-start(f32[2,2,64,256]{3,2,1,0:T(8,128)S(1)} %get-tuple-element.19), channel_id=1, source_target_pairs={{0,16},{8,24},{16,32},{24,40},{32,48},{40,56},{48,64},{56,72},{64,... | collective-permute-start | bytes 786440 | tf_op jit(solution)/shard_map/ppermute | solution.py:254
  19.6 2.9 %all-to-all-done.parts = f32[8,4,8,128]{3,2,1,0:T(8,128)S(1)} async-done(((f32[8,4,8,128]{3,2,1,0:T(8,128)}), f32[8,4,8,128]{3,2,1,0:T(8,128)S(1)}, u32[]{:S(2)}, u32[]{:S(2)}) %all-to-all-start) | async-done | bytes 131104 | tf_op jit(solution)/shard_map/all_to_all | solution.py:249
  22.5 1.3 collective-permute-start.4
  23.8 1.3 collective-permute-start.3
  25.1 1.3 collective-permute-start.2
  26.4 0.0 collective-permute-done.1.rim
  26.5 9.3 %collective-permute-done.4.refs_2_ = f32[4,8,128]{2,1,0:T(8,128)S(1)} collective-permute-done((f32[4,8,128]{2,1,0:T(8,128)S(1)}, f32[4,8,128]{2,1,0:T(8,128)S(1)}, u32[]{:S(2)}, u32[]{:S(2)}) %collective-permute-start.4) | collective-permute-done | bytes 16416 | tf_op jit(solution)/shard_map/ppermute | solution.py:252
  35.7 0.0 collective-permute-done.3.refs_1_
  35.7 3.5 %collective-permute-done.2.refs_0_ = f32[4,8,128]{2,1,0:T(8,128)S(1)} collective-permute-done((f32[4,8,128]{2,1,0:T(8,128)S(1)}, f32[4,8,128]{2,1,0:T(8,128)S(1)}, u32[]{:S(2)}, u32[]{:S(2)}) %collective-permute-start.2) | collective-permute-done | bytes 16416 | tf_op jit(solution)/shard_map/ppermute | solution.py:252
  39.3 9.3 %all_to_all.25.carry = f32[8,4,8,128]{3,2,1,0:T(8,128)S(1)} all-to-all(f32[8,4,8,128]{3,2,1,0:T(8,128)S(1)} %shard_map.48), channel_id=1, replica_groups={{0,16,32,48,64,80,96,112},{8,24,40,56,72,88,104,120},{128,144,160,176,1..., dimensions={0} | all-to-all | bytes 262144 | tf_op jit(solution)/shard_map/all_to_all | solution.py:249
  48.6 0.2 shard_map.49
  48.8 41.7 %all_to_all.26.own = f32[8,6,64,256]{3,2,1,0:T(8,128)S(1)} all-to-all(f32[8,6,64,256]{3,2,1,0:T(8,128)S(1)} %shard_map.49), channel_id=1, replica_groups=mesh['depth'=64,'row'=8] {'row'}, dimensions={0} | all-to-all | bytes 6291456 | tf_op jit(solution)/shard_map/all_to_all | solution.py:263
  90.5 0.2 fusion.25
  90.7 6.8 %collective-permute-start.6 = (f32[8,2,64,256]{3,2,1,0:T(8,128)S(1)}, f32[8,2,64,256]{3,2,1,0:T(8,128)S(1)}, u32[]{:S(2)}, u32[]{:S(2)}) collective-permute-start(f32[8,2,64,256]{3,2,1,0:T(8,128)S(1)} %get-tuple-element.31), channel_id=1, source_target_pairs={{0,8},{8,0},{16,24},{24,16},{32,40},{40,32},{48,56},{56,48},{64,72... | collective-permute-start | bytes 3145736 | tf_op jit(solution)/shard_map/ppermute | solution.py:264
  97.6 1.9 %collective-permute-start.5 = (f32[8,2,64,256]{3,2,1,0:T(8,128)S(1)}, f32[8,2,64,256]{3,2,1,0:T(8,128)S(1)}, u32[]{:S(2)}, u32[]{:S(2)}) collective-permute-start(f32[8,2,64,256]{3,2,1,0:T(8,128)S(1)} %get-tuple-element.32), channel_id=1, source_target_pairs={{0,8},{8,0},{16,24},{24,16},{32,40},{40,32},{48,56},{56,48},{64,72... | collective-permute-start | bytes 3145736 | tf_op jit(solution)/shard_map/ppermute | solution.py:265
  99.5 1.0 shard_map.50
  100.5 0.0 collective-permute-done.6
  100.6 1.0 shard_map.51.middle
  101.6 0.5 collective-permute-done.5.far
  102.1 1.4 %shard_map.52 = f32[2,8,2,64,128]{4,3,2,1,0:T(8,128)S(1)} custom-call(f32[8,6,64,256]{3,2,1,0:T(8,128)S(1)} %all_to_all.26.own, f32[8,2,64,256]{3,2,1,0:T(8,128)S(1)} %collective-permute-done.5.far, bf16[3,2,512,256]{3,2,1,0:T(8,128)(2,1)S(1)} %shard_map.51.middle), custom_call_target="tpu_custom_call" | custom-call | flops 1207959552 | bytes 8388608 | tf_op jit(solution)/shard_map/pallas_call | solution.py:24
  103.6 19.5 %all_to_all.27.parts = f32[16,2,64,128]{3,2,1,0:T(8,128)S(1)} all-to-all(f32[16,2,64,128]{3,2,1,0:T(8,128)S(1)} %bitcast.15), channel_id=1, replica_groups={{0,1,2,3,4,5,6,7,16,17,18,19,20,21,22,23},{8,9,10,11,12,13,14,15,24,25,..., dimensions={0} | all-to-all | bytes 2097152 | tf_op jit(solution)/shard_map/all_to_all | solution.py:295
  123.1 0.1 shard_map.53
  123.2 16.5 %all_to_all.28.parts = f32[16,8,128]{2,1,0:T(8,128)S(1)} all-to-all(f32[16,8,128]{2,1,0:T(8,128)S(1)} %shard_map.53), channel_id=1, replica_groups={{0,32,64,96,128,160,192,224,256,288,320,352,384,416,448,480},{8,40,72,1..., dimensions={0} | all-to-all | bytes 131072 | tf_op jit(solution)/shard_map/all_to_all | solution.py:249
  139.7 0.7 shard_map.54
  (7 shorter events, 0.1 us)
Async XLA Ops:
  0.0 1.1 copy-start
  0.0 10.8 %copy-start.2 = (s32[512]{0:T(512)S(1)}, s32[512]{0:T(512)}, u32[]{:S(2)}) copy-start(s32[512]{0:T(512)} %param.7) | copy-start | bytes 6148
  0.0 10.9 %copy-start.1 = (f32[512]{0:T(512)S(1)}, f32[512]{0:T(512)}, u32[]{:S(2)}) copy-start(f32[512]{0:T(512)} %param.5) | copy-start | bytes 6148
  0.0 11.4 %copy-start.3 = (s32[64]{0:T(128)S(1)}, s32[64]{0:T(128)}, u32[]{:S(2)}) copy-start(s32[64]{0:T(128)} %param.6) | copy-start | bytes 772
  1.8 10.1 %collective-permute-start = (f32[2,3,64,256]{3,2,1,0:T(8,128)S(1)}, f32[2,3,64,256]{3,2,1,0:T(8,128)S(1)}, u32[]{:S(2)}, u32[]{:S(2)}) collective-permute-start(f32[2,3,64,256]{3,2,1,0:T(8,128)S(1)} %bitcast.20), channel_id=1, source_target_pairs={{0,8},{8,0},{16,24},{24,16},{32,40},{40,32},{48,56},{56,48},{64,72... | collective-permute-start | bytes 1179656 | tf_op jit(solution)/shard_map/ppermute | solution.py:223
  12.9 9.6 %all-to-all-start = ((f32[8,4,8,128]{3,2,1,0:T(8,128)}), f32[8,4,8,128]{3,2,1,0:T(8,128)S(1)}, u32[]{:S(2)}, u32[]{:S(2)}) async-start(f32[8,4,8,128]{3,2,1,0:T(8,128)} %get-tuple-element.17), calls=%async_computation | async-start | bytes 262144 | tf_op jit(solution)/shard_map/all_to_all | solution.py:249
  16.3 10.1 %collective-permute-start.1 = (f32[2,2,64,256]{3,2,1,0:T(8,128)S(1)}, f32[2,2,64,256]{3,2,1,0:T(8,128)S(1)}, u32[]{:S(2)}, u32[]{:S(2)}) collective-permute-start(f32[2,2,64,256]{3,2,1,0:T(8,128)S(1)} %get-tuple-element.19), channel_id=1, source_target_pairs={{0,16},{8,24},{16,32},{24,40},{32,48},{40,56},{48,64},{56,72},{64,... | collective-permute-start | bytes 786440 | tf_op jit(solution)/shard_map/ppermute | solution.py:254
  22.5 13.2 %collective-permute-start.4 = (f32[4,8,128]{2,1,0:T(8,128)S(1)}, f32[4,8,128]{2,1,0:T(8,128)S(1)}, u32[]{:S(2)}, u32[]{:S(2)}) collective-permute-start(f32[4,8,128]{2,1,0:T(8,128)S(1)} %get-tuple-element.20), channel_id=1, source_target_pairs={{256,0},{264,8},{272,16},{280,24},{288,32},{296,40},{304,48},{312,... | collective-permute-start | bytes 49160 | tf_op jit(solution)/shard_map/ppermute | solution.py:252
  23.8 11.9 %collective-permute-start.3 = (f32[4,8,128]{2,1,0:T(8,128)S(1)}, f32[4,8,128]{2,1,0:T(8,128)S(1)}, u32[]{:S(2)}, u32[]{:S(2)}) collective-permute-start(f32[4,8,128]{2,1,0:T(8,128)S(1)} %get-tuple-element.20), channel_id=1, source_target_pairs={{128,0},{136,8},{144,16},{152,24},{160,32},{168,40},{176,48},{184,... | collective-permute-start | bytes 49160 | tf_op jit(solution)/shard_map/ppermute | solution.py:252
  25.1 14.1 %collective-permute-start.2 = (f32[4,8,128]{2,1,0:T(8,128)S(1)}, f32[4,8,128]{2,1,0:T(8,128)S(1)}, u32[]{:S(2)}, u32[]{:S(2)}) collective-permute-start(f32[4,8,128]{2,1,0:T(8,128)S(1)} %get-tuple-element.20), channel_id=1, source_target_pairs={{384,0},{392,8},{400,16},{408,24},{416,32},{424,40},{432,48},{440,... | collective-permute-start | bytes 49160 | tf_op jit(solution)/shard_map/ppermute | solution.py:252
  90.7 9.8 %collective-permute-start.6 = (f32[8,2,64,256]{3,2,1,0:T(8,128)S(1)}, f32[8,2,64,256]{3,2,1,0:T(8,128)S(1)}, u32[]{:S(2)}, u32[]{:S(2)}) collective-permute-start(f32[8,2,64,256]{3,2,1,0:T(8,128)S(1)} %get-tuple-element.31), channel_id=1, source_target_pairs={{0,8},{8,0},{16,24},{24,16},{32,40},{40,32},{48,56},{56,48},{64,72... | collective-permute-start | bytes 3145736 | tf_op jit(solution)/shard_map/ppermute | solution.py:264
  97.6 4.6 %collective-permute-start.5 = (f32[8,2,64,256]{3,2,1,0:T(8,128)S(1)}, f32[8,2,64,256]{3,2,1,0:T(8,128)S(1)}, u32[]{:S(2)}, u32[]{:S(2)}) collective-permute-start(f32[8,2,64,256]{3,2,1,0:T(8,128)S(1)} %get-tuple-element.32), channel_id=1, source_target_pairs={{0,8},{8,0},{16,24},{24,16},{32,40},{40,32},{48,56},{56,48},{64,72... | collective-permute-start | bytes 3145736 | tf_op jit(solution)/shard_map/ppermute | solution.py:265

commit v7 on v6

--- a/solution.py
+++ b/solution.py
@@ -216,11 +216,12 @@
     line, plane = spot % half // (half // 2), spot % (half // 2) // CHUNK
     column = ((plane * 2 + line) * 2 + parity) * CHUNK + spot % CHUNK
     chosen = (jnp.arange(width)[:, None] == column[None, :]).astype(f32)
-    sorted_data = jnp.dot(data.reshape(-1, width), chosen, precision=lax.Precision.HIGH)
-    kept = sorted_data[:, :half].reshape(2, slab_count, row_count, half)
-    given = sorted_data[:, half:].reshape(2, slab_count, row_count, half)
+    rows = data.reshape(-1, width)
+    pick = lambda columns: jnp.dot(rows, columns, precision=lax.Precision.HIGH).reshape(2, slab_count, row_count, half)
+    given = pick(chosen[:, half:])
     swap = [(i, i ^ 1) for i in range(deep)]
     taken = lax.ppermute(given, "depth", swap)
+    kept = pick(chosen[:, :half])
 
     row_waves = lax.dynamic_slice_in_dim(wavenumbers, lax.axis_index("row") * row_count, row_count)
     mine = lambda v: jnp.sum(chosen[:, :half] * v[:, None], axis=0)

time: 141 us -> 142 us (level)
  transfers between devices with their start and end apart: 8 -> 8, of which waited for: 5 -> 4; matrix products, arithmetic and copies ran while one was open for 1% -> 1% of each run, Pallas kernels for 1% -> 1%
where the time goes in v7:
time: 142 us; the launch traced here: 141 us
  blocking collectives  86.9 us (61%)
  starting transfers between devices  27.8 us (20%)
  waiting for transfers between devices  16.5 us (12%)
  Pallas kernels  5.53 us (4%)
  local copies, waits for them, and re-layouts  1.72 us (1%)
    all_to_all x1, blocking collectives, body(): whole = lax.all_to_all(late, 'row', 0, 0, tiled=True)  42.1 us
    all_to_all x2, blocking collectives, body(): lax.all_to_all(v, 'depth', 0, 0, axis_index_groups=groups, tiled=True)  25.3 us
    all_to_all x1, blocking collectives, body(): lax.all_to_all(partial, ('depth', 'row'), 0, 0, axis_index_groups=in_plan...  19.5 us
    ppermute x3, waiting for transfers between devices, body(): lax.ppermute(v, 'depth', [(i, i - by) for i in range(by, deep)])  12.8 us
    ppermute x1, starting transfers between devices, body(): taken = lax.ppermute(given, 'depth', swap)  8.79 us
    ppermute x1, starting transfers between devices, body(): up_far = lax.ppermute(whole[:, 2:4], 'depth', swap)  6.55 us
    pallas_call x9, Pallas kernels, call(): pl.pallas_call(kernel, out_shape=shapes[0] if single else shapes, in_spec...  5.53 us
    ppermute x3, starting transfers between devices, body(): lax.ppermute(v, 'depth', [(i, i - by) for i in range(by, deep)])  3.88 us
  transfers between devices with their start and end apart: 8, of which 4 were waited for; matrix products, arithmetic and copies ran while one was open for 1% of the time, Pallas kernels for 1%

profile of v7, /device:TPU:1, one launch (start us, length us, event | category | flops | bytes accessed | tf_op | source)
XLA Modules:
  0.0 140.5 jit_solution(9308321526651176974)
XLA Ops:
  0.0 0.0 copy-start
  0.0 0.0 copy-start.2
  0.0 0.0 copy-start.1
  0.0 0.0 copy-start.3
  0.1 0.2 iota_compare_fusion
  0.2 0.9 copy-done
  1.1 0.6 convolution_bitcast_fusion
  1.7 0.2 copy.15
  1.9 8.8 %collective-permute-start = (f32[2,3,64,256]{3,2,1,0:T(8,128)S(1)}, f32[2,3,64,256]{3,2,1,0:T(8,128)S(1)}, u32[]{:S(2)}, u32[]{:S(2)}) collective-permute-start(f32[2,3,64,256]{3,2,1,0:T(8,128)S(1)} %bitcast.24), channel_id=1, source_target_pairs={{0,8},{8,0},{16,24},{24,16},{32,40},{40,32},{48,56},{56,48},{64,72... | collective-permute-start | bytes 1179656 | tf_op jit(solution)/shard_map/ppermute | solution.py:223
  10.7 0.6 convolution_bitcast_fusion.1
  11.3 0.0 copy-done.2
  11.3 0.0 copy-done.1
  11.3 0.1 dynamic_slice.3
  11.4 0.2 select_reduce_fusion
  11.6 0.1 multiply_cosine_fusion.1
  11.7 0.1 copy.16.row_trig
  11.8 0.0 copy-done.3
  11.8 0.1 copy.17._row.eps_r
  11.9 0.2 copy.14
  12.1 0.1 multiply_cosine_fusion
  12.2 0.0 collective-permute-done.taken
  12.2 1.0 shard_map.46
  13.2 3.4 %all-to-all-start = ((f32[8,4,8,128]{3,2,1,0:T(8,128)}), f32[8,4,8,128]{3,2,1,0:T(8,128)S(1)}, u32[]{:S(2)}, u32[]{:S(2)}) async-start(f32[8,4,8,128]{3,2,1,0:T(8,128)} %get-tuple-element.17), calls=%async_computation | async-start | bytes 262144 | tf_op jit(solution)/shard_map/all_to_all | solution.py:250
  16.6 3.3 %collective-permute-start.1 = (f32[2,2,64,256]{3,2,1,0:T(8,128)S(1)}, f32[2,2,64,256]{3,2,1,0:T(8,128)S(1)}, u32[]{:S(2)}, u32[]{:S(2)}) collective-permute-start(f32[2,2,64,256]{3,2,1,0:T(8,128)S(1)} %get-tuple-element.19), channel_id=1, source_target_pairs={{0,16},{8,24},{16,32},{24,40},{32,48},{40,56},{48,64},{56,72},{64,... | collective-permute-start | bytes 786440 | tf_op jit(solution)/shard_map/ppermute | solution.py:255
  19.9 3.2 %all-to-all-done.parts = f32[8,4,8,128]{3,2,1,0:T(8,128)S(1)} async-done(((f32[8,4,8,128]{3,2,1,0:T(8,128)}), f32[8,4,8,128]{3,2,1,0:T(8,128)S(1)}, u32[]{:S(2)}, u32[]{:S(2)}) %all-to-all-start) | async-done | bytes 131104 | tf_op jit(solution)/shard_map/all_to_all | solution.py:250
  23.1 1.3 collective-permute-start.4
  24.4 1.3 collective-permute-start.3
  25.7 1.3 collective-permute-start.2
  27.0 0.0 collective-permute-done.1.rim
  27.0 9.4 %collective-permute-done.4.refs_2_ = f32[4,8,128]{2,1,0:T(8,128)S(1)} collective-permute-done((f32[4,8,128]{2,1,0:T(8,128)S(1)}, f32[4,8,128]{2,1,0:T(8,128)S(1)}, u32[]{:S(2)}, u32[]{:S(2)}) %collective-permute-start.4) | collective-permute-done | bytes 16416 | tf_op jit(solution)/shard_map/ppermute | solution.py:253
  36.4 0.0 collective-permute-done.3.refs_1_
  36.4 3.4 %collective-permute-done.2.refs_0_ = f32[4,8,128]{2,1,0:T(8,128)S(1)} collective-permute-done((f32[4,8,128]{2,1,0:T(8,128)S(1)}, f32[4,8,128]{2,1,0:T(8,128)S(1)}, u32[]{:S(2)}, u32[]{:S(2)}) %collective-permute-start.2) | collective-permute-done | bytes 16416 | tf_op jit(solution)/shard_map/ppermute | solution.py:253
  39.8 9.1 %all_to_all.25.carry = f32[8,4,8,128]{3,2,1,0:T(8,128)S(1)} all-to-all(f32[8,4,8,128]{3,2,1,0:T(8,128)S(1)} %shard_map.48), channel_id=1, replica_groups={{0,16,32,48,64,80,96,112},{8,24,40,56,72,88,104,120},{128,144,160,176,1..., dimensions={0} | all-to-all | bytes 262144 | tf_op jit(solution)/shard_map/all_to_all | solution.py:250
  48.8 0.2 shard_map.49
  49.1 42.1 %all_to_all.26.own = f32[8,6,64,256]{3,2,1,0:T(8,128)S(1)} all-to-all(f32[8,6,64,256]{3,2,1,0:T(8,128)S(1)} %shard_map.49), channel_id=1, replica_groups=mesh['depth'=64,'row'=8] {'row'}, dimensions={0} | all-to-all | bytes 6291456 | tf_op jit(solution)/shard_map/all_to_all | solution.py:264
  91.2 0.2 fusion.25
  91.4 6.5 %collective-permute-start.6 = (f32[8,2,64,256]{3,2,1,0:T(8,128)S(1)}, f32[8,2,64,256]{3,2,1,0:T(8,128)S(1)}, u32[]{:S(2)}, u32[]{:S(2)}) collective-permute-start(f32[8,2,64,256]{3,2,1,0:T(8,128)S(1)} %get-tuple-element.31), channel_id=1, source_target_pairs={{0,8},{8,0},{16,24},{24,16},{32,40},{40,32},{48,56},{56,48},{64,72... | collective-permute-start | bytes 3145736 | tf_op jit(solution)/shard_map/ppermute | solution.py:265
  98.0 1.9 %collective-permute-start.5 = (f32[8,2,64,256]{3,2,1,0:T(8,128)S(1)}, f32[8,2,64,256]{3,2,1,0:T(8,128)S(1)}, u32[]{:S(2)}, u32[]{:S(2)}) collective-permute-start(f32[8,2,64,256]{3,2,1,0:T(8,128)S(1)} %get-tuple-element.32), channel_id=1, source_target_pairs={{0,8},{8,0},{16,24},{24,16},{32,40},{40,32},{48,56},{56,48},{64,72... | collective-permute-start | bytes 3145736 | tf_op jit(solution)/shard_map/ppermute | solution.py:266
  99.9 1.0 shard_map.50
  101.0 0.0 collective-permute-done.6
  101.0 1.0 shard_map.51.middle
  102.0 0.6 collective-permute-done.5.far
  102.6 1.4 %shard_map.52 = f32[2,8,2,64,128]{4,3,2,1,0:T(8,128)S(1)} custom-call(f32[8,6,64,256]{3,2,1,0:T(8,128)S(1)} %all_to_all.26.own, f32[8,2,64,256]{3,2,1,0:T(8,128)S(1)} %collective-permute-done.5.far, bf16[3,2,512,256]{3,2,1,0:T(8,128)(2,1)S(1)} %shard_map.51.middle), custom_call_target="tpu_custom_call" | custom-call | flops 1207959552 | bytes 8388608 | tf_op jit(solution)/shard_map/pallas_call | solution.py:24
  104.0 19.5 %all_to_all.27.parts = f32[16,2,64,128]{3,2,1,0:T(8,128)S(1)} all-to-all(f32[16,2,64,128]{3,2,1,0:T(8,128)S(1)} %bitcast.19), channel_id=1, replica_groups={{0,1,2,3,4,5,6,7,16,17,18,19,20,21,22,23},{8,9,10,11,12,13,14,15,24,25,..., dimensions={0} | all-to-all | bytes 2097152 | tf_op jit(solution)/shard_map/all_to_all | solution.py:296
  123.5 0.1 shard_map.53
  123.6 16.2 %all_to_all.28.parts = f32[16,8,128]{2,1,0:T(8,128)S(1)} all-to-all(f32[16,8,128]{2,1,0:T(8,128)S(1)} %shard_map.53), channel_id=1, replica_groups={{0,32,64,96,128,160,192,224,256,288,320,352,384,416,448,480},{8,40,72,1..., dimensions={0} | all-to-all | bytes 131072 | tf_op jit(solution)/shard_map/all_to_all | solution.py:250
  139.8 0.7 shard_map.54
  (7 shorter events, 0.1 us)
Async XLA Ops:
  0.0 1.1 copy-start
  0.0 11.3 %copy-start.2 = (s32[512]{0:T(512)S(1)}, s32[512]{0:T(512)}, u32[]{:S(2)}) copy-start(s32[512]{0:T(512)} %param.7) | copy-start | bytes 6148
  0.0 11.3 %copy-start.1 = (f32[512]{0:T(512)S(1)}, f32[512]{0:T(512)}, u32[]{:S(2)}) copy-start(f32[512]{0:T(512)} %param.5) | copy-start | bytes 6148
  0.0 11.8 %copy-start.3 = (s32[64]{0:T(128)S(1)}, s32[64]{0:T(128)}, u32[]{:S(2)}) copy-start(s32[64]{0:T(128)} %param.6) | copy-start | bytes 772
  1.9 10.3 %collective-permute-start = (f32[2,3,64,256]{3,2,1,0:T(8,128)S(1)}, f32[2,3,64,256]{3,2,1,0:T(8,128)S(1)}, u32[]{:S(2)}, u32[]{:S(2)}) collective-permute-start(f32[2,3,64,256]{3,2,1,0:T(8,128)S(1)} %bitcast.24), channel_id=1, source_target_pairs={{0,8},{8,0},{16,24},{24,16},{32,40},{40,32},{48,56},{56,48},{64,72... | collective-permute-start | bytes 1179656 | tf_op jit(solution)/shard_map/ppermute | solution.py:223
  13.2 9.8 %all-to-all-start = ((f32[8,4,8,128]{3,2,1,0:T(8,128)}), f32[8,4,8,128]{3,2,1,0:T(8,128)S(1)}, u32[]{:S(2)}, u32[]{:S(2)}) async-start(f32[8,4,8,128]{3,2,1,0:T(8,128)} %get-tuple-element.17), calls=%async_computation | async-start | bytes 262144 | tf_op jit(solution)/shard_map/all_to_all | solution.py:250
  16.6 10.4 %collective-permute-start.1 = (f32[2,2,64,256]{3,2,1,0:T(8,128)S(1)}, f32[2,2,64,256]{3,2,1,0:T(8,128)S(1)}, u32[]{:S(2)}, u32[]{:S(2)}) collective-permute-start(f32[2,2,64,256]{3,2,1,0:T(8,128)S(1)} %get-tuple-element.19), channel_id=1, source_target_pairs={{0,16},{8,24},{16,32},{24,40},{32,48},{40,56},{48,64},{56,72},{64,... | collective-permute-start | bytes 786440 | tf_op jit(solution)/shard_map/ppermute | solution.py:255
  23.1 13.3 %collective-permute-start.4 = (f32[4,8,128]{2,1,0:T(8,128)S(1)}, f32[4,8,128]{2,1,0:T(8,128)S(1)}, u32[]{:S(2)}, u32[]{:S(2)}) collective-permute-start(f32[4,8,128]{2,1,0:T(8,128)S(1)} %get-tuple-element.20), channel_id=1, source_target_pairs={{256,0},{264,8},{272,16},{280,24},{288,32},{296,40},{304,48},{312,... | collective-permute-start | bytes 49160 | tf_op jit(solution)/shard_map/ppermute | solution.py:253
  24.4 12.0 %collective-permute-start.3 = (f32[4,8,128]{2,1,0:T(8,128)S(1)}, f32[4,8,128]{2,1,0:T(8,128)S(1)}, u32[]{:S(2)}, u32[]{:S(2)}) collective-permute-start(f32[4,8,128]{2,1,0:T(8,128)S(1)} %get-tuple-element.20), channel_id=1, source_target_pairs={{128,0},{136,8},{144,16},{152,24},{160,32},{168,40},{176,48},{184,... | collective-permute-start | bytes 49160 | tf_op jit(solution)/shard_map/ppermute | solution.py:253
  25.7 14.1 %collective-permute-start.2 = (f32[4,8,128]{2,1,0:T(8,128)S(1)}, f32[4,8,128]{2,1,0:T(8,128)S(1)}, u32[]{:S(2)}, u32[]{:S(2)}) collective-permute-start(f32[4,8,128]{2,1,0:T(8,128)S(1)} %get-tuple-element.20), channel_id=1, source_target_pairs={{384,0},{392,8},{400,16},{408,24},{416,32},{424,40},{432,48},{440,... | collective-permute-start | bytes 49160 | tf_op jit(solution)/shard_map/ppermute | solution.py:253
  91.4 9.5 %collective-permute-start.6 = (f32[8,2,64,256]{3,2,1,0:T(8,128)S(1)}, f32[8,2,64,256]{3,2,1,0:T(8,128)S(1)}, u32[]{:S(2)}, u32[]{:S(2)}) collective-permute-start(f32[8,2,64,256]{3,2,1,0:T(8,128)S(1)} %get-tuple-element.31), channel_id=1, source_target_pairs={{0,8},{8,0},{16,24},{24,16},{32,40},{40,32},{48,56},{56,48},{64,72... | collective-permute-start | bytes 3145736 | tf_op jit(solution)/shard_map/ppermute | solution.py:265
  98.0 4.6 %collective-permute-start.5 = (f32[8,2,64,256]{3,2,1,0:T(8,128)S(1)}, f32[8,2,64,256]{3,2,1,0:T(8,128)S(1)}, u32[]{:S(2)}, u32[]{:S(2)}) collective-permute-start(f32[8,2,64,256]{3,2,1,0:T(8,128)S(1)} %get-tuple-element.32), channel_id=1, source_target_pairs={{0,8},{8,0},{16,24},{24,16},{32,40},{40,32},{48,56},{56,48},{64,72... | collective-permute-start | bytes 3145736 | tf_op jit(solution)/shard_map/ppermute | solution.py:266

commit v8 on v6

--- a/solution.py
+++ b/solution.py
@@ -38,34 +38,36 @@
     return row_cos * col_cos - row_sin * col_sin, row_sin * col_cos + row_cos * col_sin
 
 
-def phase_kernel(core, kept, taken, row_trig, col_trig, _row, _col, down, up, rim, total):
-    first_core = core[0] == 0
+def rotations(core, kept, taken, row_trig, col_trig):
     held = kept.shape[1]
+    for slab in range(2 * held):
+        first, second = (kept, taken) if slab < held else (taken, kept)
+        re, im = (jnp.where(core[0] == 0, first[part, slab % held], second[part, slab % held]) for part in range(2))
+        yield (slab, re, im) + turned(row_trig, col_trig, slab)
+
+
+def total_kernel(core, kept, taken, row_trig, col_trig, _row, _col, total):
     totals = [None, None]
-    for slab in range(2 * held):
-        local = slab % held
-        pick = lambda part: (
-            jnp.where(first_core, kept[part, local], taken[part, local])
-            if slab < held
-            else jnp.where(first_core, taken[part, local], kept[part, local])
-        )
-        re, im = pick(0), pick(1)
-        cosine, sine = turned(row_trig, col_trig, slab)
-        a, b, c, d = re * cosine, im * sine, re * sine, im * cosine
-        sums = (a - b, c + d)
-        rises = (a + b, d - c)
-        for part in range(2):
-            down[part, slab] = sums[part]
-            totals[part] = sums[part] if slab == 0 else totals[part] + sums[part]
-            if slab < 2 * held - EPS_MOST:
-                up[part, slab] = rises[part]
-            else:
-                rim[part, slab - 2 * held + EPS_MOST] = rises[part]
+    for slab, re, im, cosine, sine in rotations(core, kept, taken, row_trig, col_trig):
+        for part, value in enumerate((re * cosine - im * sine, re * sine + im * cosine)):
+            totals[part] = value if slab == 0 else totals[part] + value
     for part in range(2):
         for block in range(8):
             for lane in range(2):
                 tile = totals[part][8 * block : 8 * block + 8, 128 * lane : 128 * lane + 128]
                 total[(8 * part + block) // 2, 2 * (block % 2) + lane] = tile
+
+
+def phase_kernel(core, kept, taken, row_trig, col_trig, down, up, rim):
+    risen = up.shape[1]
+    for slab, re, im, cosine, sine in rotations(core, kept, taken, row_trig, col_trig):
+        a, b, c, d = re * cosine, im * sine, re * sine, im * cosine
+        for part, (fall, rise) in enumerate(((a - b, a + b), (c + d, d - c))):
+            down[part, slab] = fall
+            if slab < risen:
+                up[part, slab] = rise
+            else:
+                rim[part, slab - risen] = rise
 
 
 def group_kernel(parts, out, total):
@@ -232,15 +234,16 @@
     row_trig = jnp.concatenate([jnp.cos(row_phase), jnp.sin(row_phase)], axis=1)
     col_trig = jnp.concatenate([jnp.cos(col_phase), jnp.sin(col_phase)], axis=0)
     row_marks = eps_rows.reshape(row_count, 1)
-    down, up, rim, total = call(
+    held = (me, kept, taken, row_trig, col_trig)
+    total = call(total_kernel, (NEAR, 32 // NEAR, 8, 128), *held, row_marks, near_cols, smem=(0,))
+    down, up, rim = call(
         phase_kernel,
         [
             (2, SLABS, row_count, half),
             (2, SLABS - EPS_MOST, row_count, half),
             (2, EPS_MOST, row_count, half),
-            (NEAR, 32 // NEAR, 8, 128),
         ],
-        me, kept, taken, row_trig, col_trig, row_marks, near_cols,
+        *held,
         smem=(0,),
         room=10,
     )

time: 141 us -> 141 us (level)
    pallas_call x9 -> x10, Pallas kernels: 5.55 us -> 5.77 us  [call(): pl.pallas_call(kernel, out_shape=shapes[0] if single else shapes, in_spec...]
  transfers between devices with their start and end apart: 8 -> 8, of which waited for: 5 -> 5; matrix products, arithmetic and copies ran while one was open for 1% -> 1% of each run, Pallas kernels for 1% -> 2%
where the time goes in v8:
time: 141 us
  blocking collectives  87.1 us (62%)
  starting transfers between devices  28.3 us (20%)
  waiting for transfers between devices  16.3 us (12%)
  Pallas kernels  5.77 us (4%)
  local copies, waits for them, and re-layouts  1.61 us (1%)
    all_to_all x1, blocking collectives, body(): whole = lax.all_to_all(late, 'row', 0, 0, tiled=True)  41.6 us
    all_to_all x2, blocking collectives, body(): lax.all_to_all(v, 'depth', 0, 0, axis_index_groups=groups, tiled=True)  25.9 us
    all_to_all x1, blocking collectives, body(): lax.all_to_all(partial, ('depth', 'row'), 0, 0, axis_index_groups=in_plan...  19.5 us
    ppermute x3, waiting for transfers between devices, body(): lax.ppermute(v, 'depth', [(i, i - by) for i in range(by, deep)])  12.8 us
    ppermute x1, starting transfers between devices, body(): taken = lax.ppermute(given, 'depth', swap)  8.78 us
    ppermute x1, starting transfers between devices, body(): up_far = lax.ppermute(whole[:, 2:4], 'depth', swap)  7.04 us
    pallas_call x10, Pallas kernels, call(): pl.pallas_call(kernel, out_shape=shapes[0] if single else shapes, in_spec...  5.77 us
    ppermute x3, starting transfers between devices, body(): lax.ppermute(v, 'depth', [(i, i - by) for i in range(by, deep)])  3.88 us
  transfers between devices with their start and end apart: 8, of which 5 were waited for; matrix products, arithmetic and copies ran while one was open for 1% of the time, Pallas kernels for 2%

profile of v8, /device:TPU:1, one launch (start us, length us, event | category | flops | bytes accessed | tf_op | source)
XLA Modules:
  0.0 140.6 jit_solution(15705103376889408782)
XLA Ops:
  0.0 0.0 copy-start
  0.0 0.0 copy-start.2
  0.0 0.0 copy-start.1
  0.0 0.0 copy-start.3
  0.1 1.1 copy-done
  1.1 0.6 convolution_bitcast_fusion
  1.8 0.1 fusion.26
  1.8 8.8 %collective-permute-start = (f32[2,3,64,256]{3,2,1,0:T(8,128)S(1)}, f32[2,3,64,256]{3,2,1,0:T(8,128)S(1)}, u32[]{:S(2)}, u32[]{:S(2)}) collective-permute-start(f32[2,3,64,256]{3,2,1,0:T(8,128)S(1)} %bitcast.21), channel_id=1, source_target_pairs={{0,8},{8,0},{16,24},{24,16},{32,40},{40,32},{48,56},{56,48},{64,72... | collective-permute-start | bytes 1179656 | tf_op jit(solution)/shard_map/ppermute | solution.py:225
  10.6 0.2 iota_compare_fusion
  10.8 0.0 copy-done.2
  10.9 0.0 copy-done.1
  10.9 0.1 dynamic_slice.3
  10.9 0.1 multiply_cosine_fusion.1
  11.1 0.2 select_reduce_fusion
  11.3 0.1 copy.11.row_trig
  11.4 0.0 copy-done.3
  11.4 0.1 copy.12._row.eps_r
  11.5 0.1 multiply_cosine_fusion
  11.6 0.4 collective-permute-done.taken
  12.0 0.9 shard_map.46
  12.9 3.4 %all-to-all-start = ((f32[8,4,8,128]{3,2,1,0:T(8,128)}), f32[8,4,8,128]{3,2,1,0:T(8,128)S(1)}, u32[]{:S(2)}, u32[]{:S(2)}) async-start(f32[8,4,8,128]{3,2,1,0:T(8,128)} %shard_map.46), calls=%async_computation | async-start | bytes 262144 | tf_op jit(solution)/shard_map/all_to_all | solution.py:252
  16.3 0.3 shard_map.48
  16.6 3.3 %collective-permute-start.1 = (f32[2,2,64,256]{3,2,1,0:T(8,128)S(1)}, f32[2,2,64,256]{3,2,1,0:T(8,128)S(1)}, u32[]{:S(2)}, u32[]{:S(2)}) collective-permute-start(f32[2,2,64,256]{3,2,1,0:T(8,128)S(1)} %get-tuple-element.17), channel_id=1, source_target_pairs={{0,16},{8,24},{16,32},{24,40},{32,48},{40,56},{48,64},{56,72},{64,... | collective-permute-start | bytes 786440 | tf_op jit(solution)/shard_map/ppermute | solution.py:257
  19.8 2.6 %all-to-all-done.parts = f32[8,4,8,128]{3,2,1,0:T(8,128)S(1)} async-done(((f32[8,4,8,128]{3,2,1,0:T(8,128)}), f32[8,4,8,128]{3,2,1,0:T(8,128)S(1)}, u32[]{:S(2)}, u32[]{:S(2)}) %all-to-all-start) | async-done | bytes 131104 | tf_op jit(solution)/shard_map/all_to_all | solution.py:252
  22.5 1.3 collective-permute-start.4
  23.8 1.3 collective-permute-start.3
  25.1 1.3 collective-permute-start.2
  26.4 0.0 collective-permute-done.1.rim
  26.4 9.3 %collective-permute-done.4.refs_2_ = f32[4,8,128]{2,1,0:T(8,128)S(1)} collective-permute-done((f32[4,8,128]{2,1,0:T(8,128)S(1)}, f32[4,8,128]{2,1,0:T(8,128)S(1)}, u32[]{:S(2)}, u32[]{:S(2)}) %collective-permute-start.4) | collective-permute-done | bytes 16416 | tf_op jit(solution)/shard_map/ppermute | solution.py:255
  35.7 0.0 collective-permute-done.3.refs_1_
  35.7 3.5 %collective-permute-done.2.refs_0_ = f32[4,8,128]{2,1,0:T(8,128)S(1)} collective-permute-done((f32[4,8,128]{2,1,0:T(8,128)S(1)}, f32[4,8,128]{2,1,0:T(8,128)S(1)}, u32[]{:S(2)}, u32[]{:S(2)}) %collective-permute-start.2) | collective-permute-done | bytes 16416 | tf_op jit(solution)/shard_map/ppermute | solution.py:255
  39.2 9.3 %all_to_all.25.carry = f32[8,4,8,128]{3,2,1,0:T(8,128)S(1)} all-to-all(f32[8,4,8,128]{3,2,1,0:T(8,128)S(1)} %shard_map.49), channel_id=1, replica_groups={{0,16,32,48,64,80,96,112},{8,24,40,56,72,88,104,120},{128,144,160,176,1..., dimensions={0} | all-to-all | bytes 262144 | tf_op jit(solution)/shard_map/all_to_all | solution.py:252
  48.5 0.2 shard_map.50
  48.8 41.6 %all_to_all.26.own = f32[8,6,64,256]{3,2,1,0:T(8,128)S(1)} all-to-all(f32[8,6,64,256]{3,2,1,0:T(8,128)S(1)} %shard_map.50), channel_id=1, replica_groups=mesh['depth'=64,'row'=8] {'row'}, dimensions={0} | all-to-all | bytes 6291456 | tf_op jit(solution)/shard_map/all_to_all | solution.py:266
  90.4 0.2 fusion.25
  90.6 7.0 %collective-permute-start.6 = (f32[8,2,64,256]{3,2,1,0:T(8,128)S(1)}, f32[8,2,64,256]{3,2,1,0:T(8,128)S(1)}, u32[]{:S(2)}, u32[]{:S(2)}) collective-permute-start(f32[8,2,64,256]{3,2,1,0:T(8,128)S(1)} %get-tuple-element.29), channel_id=1, source_target_pairs={{0,8},{8,0},{16,24},{24,16},{32,40},{40,32},{48,56},{56,48},{64,72... | collective-permute-start | bytes 3145736 | tf_op jit(solution)/shard_map/ppermute | solution.py:267
  97.6 1.9 %collective-permute-start.5 = (f32[8,2,64,256]{3,2,1,0:T(8,128)S(1)}, f32[8,2,64,256]{3,2,1,0:T(8,128)S(1)}, u32[]{:S(2)}, u32[]{:S(2)}) collective-permute-start(f32[8,2,64,256]{3,2,1,0:T(8,128)S(1)} %get-tuple-element.30), channel_id=1, source_target_pairs={{0,8},{8,0},{16,24},{24,16},{32,40},{40,32},{48,56},{56,48},{64,72... | collective-permute-start | bytes 3145736 | tf_op jit(solution)/shard_map/ppermute | solution.py:268
  99.6 1.0 shard_map.51
  100.6 0.0 collective-permute-done.6
  100.6 1.0 shard_map.52.middle
  101.6 0.6 collective-permute-done.5.far
  102.2 1.5 %shard_map.53 = f32[2,8,2,64,128]{4,3,2,1,0:T(8,128)S(1)} custom-call(f32[8,6,64,256]{3,2,1,0:T(8,128)S(1)} %all_to_all.26.own, f32[8,2,64,256]{3,2,1,0:T(8,128)S(1)} %collective-permute-done.5.far, bf16[3,2,512,256]{3,2,1,0:T(8,128)(2,1)S(1)} %shard_map.52.middle), custom_call_target="tpu_custom_call" | custom-call | flops 1207959552 | bytes 8388608 | tf_op jit(solution)/shard_map/pallas_call | solution.py:24
  103.7 19.5 %all_to_all.27.parts = f32[16,2,64,128]{3,2,1,0:T(8,128)S(1)} all-to-all(f32[16,2,64,128]{3,2,1,0:T(8,128)S(1)} %bitcast.15), channel_id=1, replica_groups={{0,1,2,3,4,5,6,7,16,17,18,19,20,21,22,23},{8,9,10,11,12,13,14,15,24,25,..., dimensions={0} | all-to-all | bytes 2097152 | tf_op jit(solution)/shard_map/all_to_all | solution.py:298
  123.2 0.1 shard_map.54
  123.3 16.6 %all_to_all.28.parts = f32[16,8,128]{2,1,0:T(8,128)S(1)} all-to-all(f32[16,8,128]{2,1,0:T(8,128)S(1)} %shard_map.54), channel_id=1, replica_groups={{0,32,64,96,128,160,192,224,256,288,320,352,384,416,448,480},{8,40,72,1..., dimensions={0} | all-to-all | bytes 131072 | tf_op jit(solution)/shard_map/all_to_all | solution.py:252
  139.9 0.7 shard_map.55
  (7 shorter events, 0.1 us)
Async XLA Ops:
  0.0 1.1 copy-start
  0.0 10.8 %copy-start.2 = (s32[512]{0:T(512)S(1)}, s32[512]{0:T(512)}, u32[]{:S(2)}) copy-start(s32[512]{0:T(512)} %param.7) | copy-start | bytes 6148
  0.0 10.9 %copy-start.1 = (f32[512]{0:T(512)S(1)}, f32[512]{0:T(512)}, u32[]{:S(2)}) copy-start(f32[512]{0:T(512)} %param.5) | copy-start | bytes 6148
  0.0 11.4 %copy-start.3 = (s32[64]{0:T(128)S(1)}, s32[64]{0:T(128)}, u32[]{:S(2)}) copy-start(s32[64]{0:T(128)} %param.6) | copy-start | bytes 772
  1.8 10.1 %collective-permute-start = (f32[2,3,64,256]{3,2,1,0:T(8,128)S(1)}, f32[2,3,64,256]{3,2,1,0:T(8,128)S(1)}, u32[]{:S(2)}, u32[]{:S(2)}) collective-permute-start(f32[2,3,64,256]{3,2,1,0:T(8,128)S(1)} %bitcast.21), channel_id=1, source_target_pairs={{0,8},{8,0},{16,24},{24,16},{32,40},{40,32},{48,56},{56,48},{64,72... | collective-permute-start | bytes 1179656 | tf_op jit(solution)/shard_map/ppermute | solution.py:225
  12.9 9.6 %all-to-all-start = ((f32[8,4,8,128]{3,2,1,0:T(8,128)}), f32[8,4,8,128]{3,2,1,0:T(8,128)S(1)}, u32[]{:S(2)}, u32[]{:S(2)}) async-start(f32[8,4,8,128]{3,2,1,0:T(8,128)} %shard_map.46), calls=%async_computation | async-start | bytes 262144 | tf_op jit(solution)/shard_map/all_to_all | solution.py:252
  16.6 9.8 %collective-permute-start.1 = (f32[2,2,64,256]{3,2,1,0:T(8,128)S(1)}, f32[2,2,64,256]{3,2,1,0:T(8,128)S(1)}, u32[]{:S(2)}, u32[]{:S(2)}) collective-permute-start(f32[2,2,64,256]{3,2,1,0:T(8,128)S(1)} %get-tuple-element.17), channel_id=1, source_target_pairs={{0,16},{8,24},{16,32},{24,40},{32,48},{40,56},{48,64},{56,72},{64,... | collective-permute-start | bytes 786440 | tf_op jit(solution)/shard_map/ppermute | solution.py:257
  22.5 13.2 %collective-permute-start.4 = (f32[4,8,128]{2,1,0:T(8,128)S(1)}, f32[4,8,128]{2,1,0:T(8,128)S(1)}, u32[]{:S(2)}, u32[]{:S(2)}) collective-permute-start(f32[4,8,128]{2,1,0:T(8,128)S(1)} %get-tuple-element.18), channel_id=1, source_target_pairs={{256,0},{264,8},{272,16},{280,24},{288,32},{296,40},{304,48},{312,... | collective-permute-start | bytes 49160 | tf_op jit(solution)/shard_map/ppermute | solution.py:255
  23.8 11.9 %collective-permute-start.3 = (f32[4,8,128]{2,1,0:T(8,128)S(1)}, f32[4,8,128]{2,1,0:T(8,128)S(1)}, u32[]{:S(2)}, u32[]{:S(2)}) collective-permute-start(f32[4,8,128]{2,1,0:T(8,128)S(1)} %get-tuple-element.18), channel_id=1, source_target_pairs={{128,0},{136,8},{144,16},{152,24},{160,32},{168,40},{176,48},{184,... | collective-permute-start | bytes 49160 | tf_op jit(solution)/shard_map/ppermute | solution.py:255
  25.1 14.1 %collective-permute-start.2 = (f32[4,8,128]{2,1,0:T(8,128)S(1)}, f32[4,8,128]{2,1,0:T(8,128)S(1)}, u32[]{:S(2)}, u32[]{:S(2)}) collective-permute-start(f32[4,8,128]{2,1,0:T(8,128)S(1)} %get-tuple-element.18), channel_id=1, source_target_pairs={{384,0},{392,8},{400,16},{408,24},{416,32},{424,40},{432,48},{440,... | collective-permute-start | bytes 49160 | tf_op jit(solution)/shard_map/ppermute | solution.py:255
  90.6 10.0 %collective-permute-start.6 = (f32[8,2,64,256]{3,2,1,0:T(8,128)S(1)}, f32[8,2,64,256]{3,2,1,0:T(8,128)S(1)}, u32[]{:S(2)}, u32[]{:S(2)}) collective-permute-start(f32[8,2,64,256]{3,2,1,0:T(8,128)S(1)} %get-tuple-element.29), channel_id=1, source_target_pairs={{0,8},{8,0},{16,24},{24,16},{32,40},{40,32},{48,56},{56,48},{64,72... | collective-permute-start | bytes 3145736 | tf_op jit(solution)/shard_map/ppermute | solution.py:267
  97.6 4.6 %collective-permute-start.5 = (f32[8,2,64,256]{3,2,1,0:T(8,128)S(1)}, f32[8,2,64,256]{3,2,1,0:T(8,128)S(1)}, u32[]{:S(2)}, u32[]{:S(2)}) collective-permute-start(f32[8,2,64,256]{3,2,1,0:T(8,128)S(1)} %get-tuple-element.30), channel_id=1, source_target_pairs={{0,8},{8,0},{16,24},{24,16},{32,40},{40,32},{48,56},{56,48},{64,72... | collective-permute-start | bytes 3145736 | tf_op jit(solution)/shard_map/ppermute | solution.py:268

commit v9 on v8

--- a/solution.py
+++ b/solution.py
@@ -158,7 +158,7 @@
     for block, parity in enumerate((core[0], 1 - core[0])):
         for line in range(2):
             rows = slice(block * half + line * step, block * half + line * step + step)
-            rises = [far[:, level, :, line, parity].reshape(step, half) for level in range(2)]
+            rises = [far[:, 2 + level, :, line, parity].reshape(step, half) for level in range(2)]
             product = complex_dot(triple(*rises), second)
             both = triple(*(product[level] + part[level, rows] for level in range(2)))
             for kind in range(3):
@@ -264,8 +264,7 @@
         carry, down, up, rim, row_marks, near_cols,
     )
     whole = lax.all_to_all(late, "row", 0, 0, tiled=True)
-    up_far = lax.ppermute(whole[:, 2:4], "depth", swap)
-    left_far = lax.ppermute(whole[:, :2], "depth", swap)
+    other = lax.ppermute(whole[:, :4], "depth", swap)
     shape = lambda v: v.reshape(chips, v.shape[1], row_count // 32, 2, 2, CHUNK, half)
     parts = lambda n: jax.ShapeDtypeStruct((3, 2, n, half), jnp.bfloat16)
     far_right, part = call(
@@ -279,7 +278,7 @@
     middle = call(
         first_kernel,
         parts(width),
-        me, shape(up_far), far_right, part,
+        me, shape(other), far_right, part,
         smem=(0,),
         flops=9 * width * width * half,
         room=12,
@@ -287,7 +286,7 @@
     partial = call(
         second_kernel,
         (2, chips, 2, row_count, half // 2),
-        whole, left_far, middle,
+        whole, other, middle,
         flops=18 * width * width * half,
         room=12,
     )

time: 141 us -> 143 us (1.014)
  blocking collectives: 87.1 us -> 89.5 us
  starting transfers between devices: 28.3 us -> 25.9 us
    ppermute x2 -> x1, starting transfers between devices: 8.96 us -> 6.56 us  [body(): other = lax.ppermute(whole[:, :4], 'depth', swap)]
    ppermute x2 -> x1, waiting for transfers between devices: 0.57 us -> 2.72 us  [body(): other = lax.ppermute(whole[:, :4], 'depth', swap)]
    all_to_all x2, blocking collectives: 25.9 us -> 28.1 us  [body(): lax.all_to_all(v, 'depth', 0, 0, axis_index_groups=groups, tiled=True)]
  transfers between devices with their start and end apart: 8 -> 7, of which waited for: 5 -> 6; matrix products, arithmetic and copies ran while one was open for 1% -> 1% of each run, Pallas kernels for 2% -> 1%
where the time goes in v9:
time: 143 us; the launch traced here: 142 us
  blocking collectives  89.5 us (63%)
  starting transfers between devices  25.9 us (18%)
  waiting for transfers between devices  17.6 us (12%)
  Pallas kernels  5.82 us (4%)
  local copies, waits for them, and re-layouts  1.61 us (1%)
    all_to_all x1, blocking collectives, body(): whole = lax.all_to_all(late, 'row', 0, 0, tiled=True)  42.1 us
    all_to_all x2, blocking collectives, body(): lax.all_to_all(v, 'depth', 0, 0, axis_index_groups=groups, tiled=True)  28.1 us
    all_to_all x1, blocking collectives, body(): lax.all_to_all(partial, ('depth', 'row'), 0, 0, axis_index_groups=in_plan...  19.4 us
    ppermute x3, waiting for transfers between devices, body(): lax.ppermute(v, 'depth', [(i, i - by) for i in range(by, deep)])  11.9 us
    ppermute x1, starting transfers between devices, body(): taken = lax.ppermute(given, 'depth', swap)  8.78 us
    ppermute x1, starting transfers between devices, body(): other = lax.ppermute(whole[:, :4], 'depth', swap)  6.56 us
    pallas_call x10, Pallas kernels, call(): pl.pallas_call(kernel, out_shape=shapes[0] if single else shapes, in_spec...  5.82 us
    ppermute x3, starting transfers between devices, body(): lax.ppermute(v, 'depth', [(i, i - by) for i in range(by, deep)])  3.88 us
  transfers between devices with their start and end apart: 7, of which 6 were waited for; matrix products, arithmetic and copies ran while one was open for 1% of the time, Pallas kernels for 1%

profile of v9, /device:TPU:1, one launch (start us, length us, event | category | flops | bytes accessed | tf_op | source)
XLA Modules:
  0.0 141.9 jit_solution(1459943087760651276)
XLA Ops:
  0.0 0.0 copy-start
  0.0 0.0 copy-start.2
  0.0 0.0 copy-start.1
  0.0 0.0 copy-start.3
  0.1 1.1 copy-done
  1.1 0.6 convolution_bitcast_fusion
  1.8 0.1 fusion.25
  1.8 8.8 %collective-permute-start = (f32[2,3,64,256]{3,2,1,0:T(8,128)S(1)}, f32[2,3,64,256]{3,2,1,0:T(8,128)S(1)}, u32[]{:S(2)}, u32[]{:S(2)}) collective-permute-start(f32[2,3,64,256]{3,2,1,0:T(8,128)S(1)} %bitcast.21), channel_id=1, source_target_pairs={{0,8},{8,0},{16,24},{24,16},{32,40},{40,32},{48,56},{56,48},{64,72... | collective-permute-start | bytes 1179656 | tf_op jit(solution)/shard_map/ppermute | solution.py:225
  10.6 0.2 iota_compare_fusion
  10.8 0.0 copy-done.2
  10.9 0.0 copy-done.1
  10.9 0.1 dynamic_slice.3
  10.9 0.2 select_reduce_fusion
  11.2 0.1 multiply_cosine_fusion.1
  11.3 0.1 copy.11.row_trig
  11.4 0.0 copy-done.3
  11.4 0.1 copy.12._row.eps_r
  11.5 0.1 multiply_cosine_fusion
  11.6 0.4 collective-permute-done.taken
  12.0 0.9 shard_map.46
  12.9 3.4 %all-to-all-start = ((f32[8,4,8,128]{3,2,1,0:T(8,128)}), f32[8,4,8,128]{3,2,1,0:T(8,128)S(1)}, u32[]{:S(2)}, u32[]{:S(2)}) async-start(f32[8,4,8,128]{3,2,1,0:T(8,128)} %shard_map.46), calls=%async_computation | async-start | bytes 262144 | tf_op jit(solution)/shard_map/all_to_all | solution.py:252
  16.3 0.3 shard_map.48
  16.6 3.3 %collective-permute-start.1 = (f32[2,2,64,256]{3,2,1,0:T(8,128)S(1)}, f32[2,2,64,256]{3,2,1,0:T(8,128)S(1)}, u32[]{:S(2)}, u32[]{:S(2)}) collective-permute-start(f32[2,2,64,256]{3,2,1,0:T(8,128)S(1)} %get-tuple-element.17), channel_id=1, source_target_pairs={{0,16},{8,24},{16,32},{24,40},{32,48},{40,56},{48,64},{56,72},{64,... | collective-permute-start | bytes 786440 | tf_op jit(solution)/shard_map/ppermute | solution.py:257
  19.8 2.6 %all-to-all-done.parts = f32[8,4,8,128]{3,2,1,0:T(8,128)S(1)} async-done(((f32[8,4,8,128]{3,2,1,0:T(8,128)}), f32[8,4,8,128]{3,2,1,0:T(8,128)S(1)}, u32[]{:S(2)}, u32[]{:S(2)}) %all-to-all-start) | async-done | bytes 131104 | tf_op jit(solution)/shard_map/all_to_all | solution.py:252
  22.5 1.3 collective-permute-start.2
  23.8 1.3 collective-permute-start.3
  25.1 1.3 collective-permute-start.4
  26.4 0.0 collective-permute-done.1.rim
  26.4 4.5 %collective-permute-done.2.refs_0_ = f32[4,8,128]{2,1,0:T(8,128)S(1)} collective-permute-done((f32[4,8,128]{2,1,0:T(8,128)S(1)}, f32[4,8,128]{2,1,0:T(8,128)S(1)}, u32[]{:S(2)}, u32[]{:S(2)}) %collective-permute-start.2) | collective-permute-done | bytes 16416 | tf_op jit(solution)/shard_map/ppermute | solution.py:255
  30.9 1.3 collective-permute-done.3.refs_1_
  32.2 6.1 %collective-permute-done.4.refs_2_ = f32[4,8,128]{2,1,0:T(8,128)S(1)} collective-permute-done((f32[4,8,128]{2,1,0:T(8,128)S(1)}, f32[4,8,128]{2,1,0:T(8,128)S(1)}, u32[]{:S(2)}, u32[]{:S(2)}) %collective-permute-start.4) | collective-permute-done | bytes 16416 | tf_op jit(solution)/shard_map/ppermute | solution.py:255
  38.3 9.3 %all_to_all.25.carry = f32[8,4,8,128]{3,2,1,0:T(8,128)S(1)} all-to-all(f32[8,4,8,128]{3,2,1,0:T(8,128)S(1)} %shard_map.49), channel_id=1, replica_groups={{0,16,32,48,64,80,96,112},{8,24,40,56,72,88,104,120},{128,144,160,176,1..., dimensions={0} | all-to-all | bytes 262144 | tf_op jit(solution)/shard_map/all_to_all | solution.py:252
  47.6 0.2 shard_map.50
  47.9 42.1 %all_to_all.26.own = f32[8,6,64,256]{3,2,1,0:T(8,128)S(1)} all-to-all(f32[8,6,64,256]{3,2,1,0:T(8,128)S(1)} %shard_map.50), channel_id=1, replica_groups=mesh['depth'=64,'row'=8] {'row'}, dimensions={0} | all-to-all | bytes 6291456 | tf_op jit(solution)/shard_map/all_to_all | solution.py:266
  89.9 0.2 slice.21
  90.2 6.6 %collective-permute-start.5 = (f32[8,4,64,256]{3,2,1,0:T(8,128)S(1)}, f32[8,4,64,256]{3,2,1,0:T(8,128)S(1)}, u32[]{:S(2)}, u32[]{:S(2)}) collective-permute-start(f32[8,4,64,256]{3,2,1,0:T(8,128)S(1)} %slice.21), channel_id=1, source_target_pairs={{0,8},{8,0},{16,24},{24,16},{32,40},{40,32},{48,56},{56,48},{64,72... | collective-permute-start | bytes 6291464 | tf_op jit(solution)/shard_map/ppermute | solution.py:267
  96.7 1.0 shard_map.51
  97.8 2.7 %collective-permute-done.5.far = f32[8,4,64,256]{3,2,1,0:T(8,128)S(1)} collective-permute-done((f32[8,4,64,256]{3,2,1,0:T(8,128)S(1)}, f32[8,4,64,256]{3,2,1,0:T(8,128)S(1)}, u32[]{:S(2)}, u32[]{:S(2)}) %collective-permute-start.5) | collective-permute-done | bytes 2097184 | tf_op jit(solution)/shard_map/ppermute | solution.py:267
  100.5 1.0 shard_map.52.middle
  101.5 1.5 %shard_map.53 = f32[2,8,2,64,128]{4,3,2,1,0:T(8,128)S(1)} custom-call(f32[8,6,64,256]{3,2,1,0:T(8,128)S(1)} %all_to_all.26.own, f32[8,4,64,256]{3,2,1,0:T(8,128)S(1)} %collective-permute-done.5.far, bf16[3,2,512,256]{3,2,1,0:T(8,128)(2,1)S(1)} %shard_map.52.middle), custom_call_target="tpu_custom_call" | custom-call | flops 1207959552 | bytes 9437184 | tf_op jit(solution)/shard_map/pallas_call | solution.py:24
  103.0 19.4 %all_to_all.27.parts = f32[16,2,64,128]{3,2,1,0:T(8,128)S(1)} all-to-all(f32[16,2,64,128]{3,2,1,0:T(8,128)S(1)} %bitcast.16), channel_id=1, replica_groups={{0,1,2,3,4,5,6,7,16,17,18,19,20,21,22,23},{8,9,10,11,12,13,14,15,24,25,..., dimensions={0} | all-to-all | bytes 2097152 | tf_op jit(solution)/shard_map/all_to_all | solution.py:297
  122.4 0.1 shard_map.54
  122.5 18.7 %all_to_all.28.parts = f32[16,8,128]{2,1,0:T(8,128)S(1)} all-to-all(f32[16,8,128]{2,1,0:T(8,128)S(1)} %shard_map.54), channel_id=1, replica_groups={{0,32,64,96,128,160,192,224,256,288,320,352,384,416,448,480},{8,40,72,1..., dimensions={0} | all-to-all | bytes 131072 | tf_op jit(solution)/shard_map/all_to_all | solution.py:252
  141.2 0.7 shard_map.55
  (7 shorter events, 0.1 us)
Async XLA Ops:
  0.0 1.1 copy-start
  0.0 10.8 %copy-start.2 = (s32[512]{0:T(512)S(1)}, s32[512]{0:T(512)}, u32[]{:S(2)}) copy-start(s32[512]{0:T(512)} %param.7) | copy-start | bytes 6148
  0.0 10.8 %copy-start.1 = (f32[512]{0:T(512)S(1)}, f32[512]{0:T(512)}, u32[]{:S(2)}) copy-start(f32[512]{0:T(512)} %param.5) | copy-start | bytes 6148
  0.0 11.4 %copy-start.3 = (s32[64]{0:T(128)S(1)}, s32[64]{0:T(128)}, u32[]{:S(2)}) copy-start(s32[64]{0:T(128)} %param.6) | copy-start | bytes 772
  1.8 10.1 %collective-permute-start = (f32[2,3,64,256]{3,2,1,0:T(8,128)S(1)}, f32[2,3,64,256]{3,2,1,0:T(8,128)S(1)}, u32[]{:S(2)}, u32[]{:S(2)}) collective-permute-start(f32[2,3,64,256]{3,2,1,0:T(8,128)S(1)} %bitcast.21), channel_id=1, source_target_pairs={{0,8},{8,0},{16,24},{24,16},{32,40},{40,32},{48,56},{56,48},{64,72... | collective-permute-start | bytes 1179656 | tf_op jit(solution)/shard_map/ppermute | solution.py:225
  12.9 9.6 %all-to-all-start = ((f32[8,4,8,128]{3,2,1,0:T(8,128)}), f32[8,4,8,128]{3,2,1,0:T(8,128)S(1)}, u32[]{:S(2)}, u32[]{:S(2)}) async-start(f32[8,4,8,128]{3,2,1,0:T(8,128)} %shard_map.46), calls=%async_computation | async-start | bytes 262144 | tf_op jit(solution)/shard_map/all_to_all | solution.py:252
  16.6 9.8 %collective-permute-start.1 = (f32[2,2,64,256]{3,2,1,0:T(8,128)S(1)}, f32[2,2,64,256]{3,2,1,0:T(8,128)S(1)}, u32[]{:S(2)}, u32[]{:S(2)}) collective-permute-start(f32[2,2,64,256]{3,2,1,0:T(8,128)S(1)} %get-tuple-element.17), channel_id=1, source_target_pairs={{0,16},{8,24},{16,32},{24,40},{32,48},{40,56},{48,64},{56,72},{64,... | collective-permute-start | bytes 786440 | tf_op jit(solution)/shard_map/ppermute | solution.py:257
  22.5 8.4 %collective-permute-start.2 = (f32[4,8,128]{2,1,0:T(8,128)S(1)}, f32[4,8,128]{2,1,0:T(8,128)S(1)}, u32[]{:S(2)}, u32[]{:S(2)}) collective-permute-start(f32[4,8,128]{2,1,0:T(8,128)S(1)} %get-tuple-element.18), channel_id=1, source_target_pairs={{384,0},{392,8},{400,16},{408,24},{416,32},{424,40},{432,48},{440,... | collective-permute-start | bytes 49160 | tf_op jit(solution)/shard_map/ppermute | solution.py:255
  23.8 8.4 %collective-permute-start.3 = (f32[4,8,128]{2,1,0:T(8,128)S(1)}, f32[4,8,128]{2,1,0:T(8,128)S(1)}, u32[]{:S(2)}, u32[]{:S(2)}) collective-permute-start(f32[4,8,128]{2,1,0:T(8,128)S(1)} %get-tuple-element.18), channel_id=1, source_target_pairs={{128,0},{136,8},{144,16},{152,24},{160,32},{168,40},{176,48},{184,... | collective-permute-start | bytes 49160 | tf_op jit(solution)/shard_map/ppermute | solution.py:255
  25.1 13.2 %collective-permute-start.4 = (f32[4,8,128]{2,1,0:T(8,128)S(1)}, f32[4,8,128]{2,1,0:T(8,128)S(1)}, u32[]{:S(2)}, u32[]{:S(2)}) collective-permute-start(f32[4,8,128]{2,1,0:T(8,128)S(1)} %get-tuple-element.18), channel_id=1, source_target_pairs={{256,0},{264,8},{272,16},{280,24},{288,32},{296,40},{304,48},{312,... | collective-permute-start | bytes 49160 | tf_op jit(solution)/shard_map/ppermute | solution.py:255
  90.2 10.3 %collective-permute-start.5 = (f32[8,4,64,256]{3,2,1,0:T(8,128)S(1)}, f32[8,4,64,256]{3,2,1,0:T(8,128)S(1)}, u32[]{:S(2)}, u32[]{:S(2)}) collective-permute-start(f32[8,4,64,256]{3,2,1,0:T(8,128)S(1)} %slice.21), channel_id=1, source_target_pairs={{0,8},{8,0},{16,24},{24,16},{32,40},{40,32},{48,56},{56,48},{64,72... | collective-permute-start | bytes 6291464 | tf_op jit(solution)/shard_map/ppermute | solution.py:267
